TPU v7x, 32 devices: a whole 2x2x4 slice. The times are simulated.
32 devices in a mesh: row: 4 (over y, core), col: 8 (over z, x).
Axes of the slice: x: 2, y: 2, z: 4, core: 2. Of those that a mesh axis runs over, the one named last changes fastest.
Arguments:
- vectors: bfloat16 [32, 8192], P(None, ('col', 'row')), may hold values from -6 to 6
- tile_data: bfloat16 [2048, 128, 128], P(('col', 'row')), may hold values from -0.09375 to 0.09375
- tile_row: int32 [2048], P(('col', 'row')), may hold values from 0 to 7
- tile_offset: int32 [2048], P(('col', 'row')), may hold values from 0 to 7
- tile_live: int32 [32], P(('col', 'row')), may hold values from 1 to 64, as said below
- damp_center: float32 [1], replicated, may hold values from -0.5 to 0.5
- damp_radius: float32 [1], replicated, may hold values from 1 to 2
Outputs:
- first_degree: bfloat16 [32, 8192], P(None, ('col', 'row'))
- second_degree: float32 [32, 8192], P(None, ('col', 'row'))
Inputs may be any that keep to these rules, and one draw needn't show every extreme that they name: `tile_live`: every device has at least one live slot, and some device has all 64.
All inputs are finite; a program needn't handle non-finite values.
Results may differ from a plain program's by a relative error of at most 0.0024.
Values may be sent and summed in bfloat16 or wider, within the bound.
No kernel may reach another device: no remote copies, remote signals or barrier semaphores. Data moves between devices by JAX's collectives and lax.ppermute only.
A program may use at most 64 MiB of HBM per device.

v0:
```python
import jax
import jax.numpy as jnp
from jax import lax
from jax.sharding import PartitionSpec as P


def passed_along(block, axis, distance):
    devices = range(lax.axis_size(axis))
    route = [(i - distance, i) for i in devices if i - distance in devices]
    return lax.ppermute(block, axis, route)


def apply_operator(vectors_bf, tile_data, tile_row, tile_offset, tile_live):
    vec_count = vectors_bf.shape[0]
    tile_size = tile_data.shape[-1]
    slot_count = tile_data.shape[0]
    own_range = lax.all_gather(vectors_bf, "row", axis=1, tiled=True)
    next_blocks = passed_along(own_range, "col", -1)
    range_blocks = own_range.shape[1] // tile_size
    window = jnp.concatenate([own_range, next_blocks], axis=1)
    blocks = window.reshape(vec_count, 2 * range_blocks, tile_size)
    tile_cols = tile_row + tile_offset
    live_mask = (jnp.arange(slot_count, dtype=jnp.int32) < tile_live[0]).astype(jnp.float32)
    picked_col = jnp.take(blocks, tile_cols, axis=1)
    picked_row = jnp.take(blocks, tile_row, axis=1)
    direct = jnp.einsum("vkb,kab->vka", picked_col, tile_data, preferred_element_type=jnp.float32)
    mirrored = jnp.einsum("vka,kab->vkb", picked_row, tile_data, preferred_element_type=jnp.float32)
    slot_ids = jnp.arange(2 * range_blocks, dtype=jnp.int32)
    to_row = (tile_row[:, None] == slot_ids[None, :]).astype(jnp.float32) * live_mask[:, None]
    to_col = (tile_cols[:, None] == slot_ids[None, :]).astype(jnp.float32) * live_mask[:, None]
    partial_value = jnp.einsum("kr,vkb->vrb", to_row, direct, precision=lax.Precision.HIGHEST)
    partial_value = partial_value + jnp.einsum(
        "kr,vkb->vrb", to_col, mirrored, precision=lax.Precision.HIGHEST
    )
    partial_value = partial_value.reshape(vec_count, 2 * range_blocks * tile_size)
    lower_half = partial_value[:, : range_blocks * tile_size]
    upper_half = partial_value[:, range_blocks * tile_size :]
    arrived = passed_along(upper_half, "col", 1)
    return lax.psum_scatter(lower_half + arrived, "row", scatter_dimension=1, tiled=True)


def local(vectors, tile_data, tile_row, tile_offset, tile_live, damp_center, damp_radius):
    center = damp_center[0]
    radius = damp_radius[0]
    vectors_f = vectors.astype(jnp.float32)
    image = apply_operator(vectors, tile_data, tile_row, tile_offset, tile_live)
    first_degree = ((image - center * vectors_f) / radius).astype(jnp.bfloat16)
    second_image = apply_operator(first_degree, tile_data, tile_row, tile_offset, tile_live)
    second_degree = (
        2.0 * (second_image - center * first_degree.astype(jnp.float32)) / radius - vectors_f
    )
    return (first_degree, second_degree)


def solution(mesh):
    placed = (
        P(None, ("col", "row")),
        P(("col", "row"), None, None),
        P(("col", "row")),
        P(("col", "row")),
        P(("col", "row")),
        P(),
        P(),
    )
    return jax.shard_map(
        local,
        mesh=mesh,
        in_specs=placed,
        out_specs=(P(None, ("col", "row")), P(None, ("col", "row"))),
        check_vma=False,
    )
```

profile of v0, /device:TPU:0, one launch (start us, length us, event | category | flops | bytes accessed | tf_op | source)
XLA Modules:
  0.0 108.6 jit_solution(11327627978004644071)
XLA Ops:
  7.2 6.6 %all_gather.6 = bf16[32,1024]{1,0:T(8,128)(2,1)S(1)} all-gather(bf16[32,256]{1,0:T(8,128)(2,1)} %param.9), channel_id=1, replica_groups=mesh['row'=4,'col'=8] {'row'}, dimensions={1}, use_global_device_ids=true | all-gather | bytes 81920 | tf_op jit(solution)/shard_map/all_gather | solution.py:17
  13.8 1.3 %collective-permute-start = (bf16[32,1024]{1,0:T(8,128)(2,1)S(1)}, bf16[32,1024]{1,0:T(8,128)(2,1)S(1)}, u32[]{:S(2)}, u32[]{:S(2)}) collective-permute-start(bf16[32,1024]{1,0:T(8,128)(2,1)S(1)} %all_gather.6), channel_id=1, source_target_pairs={{1,0},{2,1},{3,2},{4,3},{5,4},{6,5},{7,6},{9,8},{10,9},{11,10},{12... | collective-permute-start | bytes 196616 | tf_op jit(solution)/shard_map/ppermute | solution.py:10
  15.8 0.7 compare_and_fusion.1
  17.1 3.1 %collective-permute-done = bf16[32,1024]{1,0:T(8,128)(2,1)S(1)} collective-permute-done((bf16[32,1024]{1,0:T(8,128)(2,1)S(1)}, bf16[32,1024]{1,0:T(8,128)(2,1)S(1)}, u32[]{:S(2)}, u32[]{:S(2)}) %collective-permute-start) | collective-permute-done | bytes 65568 | tf_op jit(solution)/shard_map/ppermute | solution.py:10
  21.6 1.2 %convolution_bitcast_fusion.3 = f32[32,64,128]{2,0,1:T(8,128)S(1)} fusion(bf16[64,128,128]{2,1,0:T(8,128)(2,1)S(1)} %copy-done, bf16[64,32,128]{2,1,0:T(8,128)(2,1)S(1)} %gather_fusion, pred[64]{0:T(512)(128)(4,1)S(1)} %get-tuple-element.3), kind=kOutput, calls=%fused_computation.7 | convolution fusion | flops 67371008 | bytes 3670080 | tf_op jit(solution)/shard_map/vkb,kab->vka/dot_general | solution.py:26
  22.8 1.3 %fusion.4 = f32[32,128,16]{1,2,0:T(8,128)S(1)} fusion(f32[32,64,128]{2,0,1:T(8,128)S(1)} %convolution_bitcast_fusion.3, f32[64]{0:T(128)S(1)} %compare_convert_fusion, s32[64]{0:T(128)S(1)} %copy-done.3), kind=kOutput, calls=%fused_computation.14 | convolution fusion | flops 50333696 | bytes 1311232 | tf_op jit(solution)/shard_map/kr,vkb->vrb/dot_general | solution.py:31
  24.1 0.7 convolution_bitcast_fusion.2
  24.8 1.2 %convolution_add_fusion.1 = f32[32,128,16]{1,2,0:T(8,128)S(1)} fusion(f32[32,128,16]{1,2,0:T(8,128)S(1)} %fusion.4, f32[32,64,128]{2,0,1:T(8,128)S(1)} %convolution_bitcast_fusion.2, s32[64]{0:T(128)S(1)} %get-tuple-element.4, f32[64]{0:T(128)S(1)} %compare_convert_fusion), kind=kOutput, calls=%fused_computation.9 | convolution fusion | flops 50399232 | bytes 1573376 | tf_op jit(solution)/shard_map/kr,vkb->vrb/dot_general | solution.py:32
  26.2 4.5 %collective-permute-start.1 = (f32[32,1024]{1,0:T(8,128)S(1)}, f32[32,1024]{1,0:T(8,128)S(1)}, u32[]{:S(2)}, u32[]{:S(2)}) collective-permute-start(f32[32,1024]{1,0:T(8,128)S(1)} %slice.25), channel_id=1, source_target_pairs={{0,1},{1,2},{2,3},{3,4},{4,5},{5,6},{6,7},{8,9},{9,10},{10,11},{11... | collective-permute-start | bytes 393224 | tf_op jit(solution)/shard_map/ppermute | solution.py:10
  30.7 2.5 %collective-permute-done.1 = f32[32,1024]{1,0:T(8,128)S(1)} collective-permute-done((f32[32,1024]{1,0:T(8,128)S(1)}, f32[32,1024]{1,0:T(8,128)S(1)}, u32[]{:S(2)}, u32[]{:S(2)}) %collective-permute-start.1) | collective-permute-done | bytes 131104 | tf_op jit(solution)/shard_map/ppermute | solution.py:10
  33.2 0.7 slice_add_fusion.1
  35.3 19.7 %reduce-scatter.3.cloned.1.call-done = f32[32,256]{1,0:T(8,128)} async-done(((f32[32,1024]{1,0:T(8,128)}), f32[32,256]{1,0:T(8,128)}) %reduce-scatter.3.cloned.1.call-update) | async-done | bytes 32784 | tf_op jit(solution)/shard_map/reduce_scatter | solution.py:39
  54.9 0.8 fusion.24
  55.7 5.2 %all_gather.7 = bf16[32,1024]{1,0:T(8,128)(2,1)S(1)} all-gather(bf16[32,256]{1,0:T(8,128)(2,1)S(1)} %fusion.24), channel_id=1, replica_groups=mesh['row'=4,'col'=8] {'row'}, dimensions={1}, use_global_device_ids=true | all-gather | bytes 81920 | tf_op jit(solution)/shard_map/all_gather | solution.py:17
  61.0 1.3 %collective-permute-start.2 = (bf16[32,1024]{1,0:T(8,128)(2,1)S(1)}, bf16[32,1024]{1,0:T(8,128)(2,1)S(1)}, u32[]{:S(2)}, u32[]{:S(2)}) collective-permute-start(bf16[32,1024]{1,0:T(8,128)(2,1)S(1)} %all_gather.7), channel_id=1, source_target_pairs={{1,0},{2,1},{3,2},{4,3},{5,4},{6,5},{7,6},{9,8},{10,9},{11,10},{12... | collective-permute-start | bytes 196616 | tf_op jit(solution)/shard_map/ppermute | solution.py:10
  62.2 4.9 %collective-permute-done.2 = bf16[32,1024]{1,0:T(8,128)(2,1)S(1)} collective-permute-done((bf16[32,1024]{1,0:T(8,128)(2,1)S(1)}, bf16[32,1024]{1,0:T(8,128)(2,1)S(1)}, u32[]{:S(2)}, u32[]{:S(2)}) %collective-permute-start.2) | collective-permute-done | bytes 65568 | tf_op jit(solution)/shard_map/ppermute | solution.py:10
  68.5 1.2 %convolution_bitcast_fusion.1 = f32[32,64,128]{2,0,1:T(8,128)S(1)} fusion(bf16[64,128,128]{2,1,0:T(8,128)(2,1)S(1)} %copy-done, bf16[64,32,128]{2,1,0:T(8,128)(2,1)S(1)} %gather_fusion.2, pred[64]{0:T(512)(128)(4,1)S(1)} %get-tuple-element.3), kind=kOutput, calls=%fused_computation.5 | convolution fusion | flops 67371008 | bytes 3670080 | tf_op jit(solution)/shard_map/vkb,kab->vka/dot_general | solution.py:26
  69.8 1.3 %fusion.1 = f32[32,128,16]{1,2,0:T(8,128)S(1)} fusion(f32[32,64,128]{2,0,1:T(8,128)S(1)} %convolution_bitcast_fusion.1, f32[64]{0:T(128)S(1)} %compare_convert_fusion, s32[64]{0:T(128)S(1)} %copy-done.3), kind=kOutput, calls=%fused_computation.11 | convolution fusion | flops 50333696 | bytes 1311232 | tf_op jit(solution)/shard_map/kr,vkb->vrb/dot_general | solution.py:31
  71.0 0.7 convolution_bitcast_fusion
  71.7 1.3 %convolution_add_fusion = f32[32,128,16]{1,2,0:T(8,128)S(1)} fusion(f32[32,128,16]{1,2,0:T(8,128)S(1)} %fusion.1, f32[32,64,128]{2,0,1:T(8,128)S(1)} %convolution_bitcast_fusion, s32[64]{0:T(128)S(1)} %get-tuple-element.4, f32[64]{0:T(128)S(1)} %compare_convert_fusion), kind=kOutput, calls=%fused_computation.8 | convolution fusion | flops 50399232 | bytes 1573376 | tf_op jit(solution)/shard_map/kr,vkb->vrb/dot_general | solution.py:32
  73.1 4.3 %collective-permute-start.3 = (f32[32,1024]{1,0:T(8,128)S(1)}, f32[32,1024]{1,0:T(8,128)S(1)}, u32[]{:S(2)}, u32[]{:S(2)}) collective-permute-start(f32[32,1024]{1,0:T(8,128)S(1)} %slice.27), channel_id=1, source_target_pairs={{0,1},{1,2},{2,3},{3,4},{4,5},{5,6},{6,7},{8,9},{9,10},{10,11},{11... | collective-permute-start | bytes 393224 | tf_op jit(solution)/shard_map/ppermute | solution.py:10
  77.4 2.5 %collective-permute-done.3 = f32[32,1024]{1,0:T(8,128)S(1)} collective-permute-done((f32[32,1024]{1,0:T(8,128)S(1)}, f32[32,1024]{1,0:T(8,128)S(1)}, u32[]{:S(2)}, u32[]{:S(2)}) %collective-permute-start.3) | collective-permute-done | bytes 131104 | tf_op jit(solution)/shard_map/ppermute | solution.py:10
  80.6 19.8 %reduce-scatter.5.cloned.1.call-done = f32[32,256]{1,0:T(8,128)} async-done(((f32[32,1024]{1,0:T(8,128)}), f32[32,256]{1,0:T(8,128)}) %reduce-scatter.5.cloned.1.call-update) | async-done | bytes 32784 | tf_op jit(solution)/shard_map/reduce_scatter | solution.py:39
  100.4 1.4 %convert_subtract_fusion = f32[32,256]{1,0:T(8,128)} fusion(bf16[32,256]{1,0:T(8,128)(2,1)S(1)} %copy-done.1, f32[32,256]{1,0:T(8,128)} %reduce-scatter.5.cloned.1.call-done, bf16[32,256]{1,0:T(8,128)(2,1)S(1)} %fusion.24, f32[]{:T(128)} %bitcast.61, f32[]{:T(128)} %bitcast.59), kind=kLoop, calls=%fused_computation.40 | loop fusion | flops 57344 | bytes 98312 | tf_op jit(solution)/shard_map/sub | solution.py:50
  (28 shorter events, 4.3 us)
Async XLA Ops:
  7.2 14.4 %copy-start = (bf16[64,128,128]{2,1,0:T(8,128)(2,1)S(1)}, bf16[64,128,128]{2,1,0:T(8,128)(2,1)}, u32[]{:S(2)}) copy-start(bf16[64,128,128]{2,1,0:T(8,128)(2,1)} %param.10) | copy-start | bytes 6291460
  7.2 47.8 %reduce-scatter.3.cloned.1.call-start = ((), (), s32[]{:S(2)}) async-start(), calls=%async_computation.2 | async-start | bytes 163840 | tf_op jit(solution)/shard_map/reduce_scatter | solution.py:39
  13.8 6.4 %collective-permute-start = (bf16[32,1024]{1,0:T(8,128)(2,1)S(1)}, bf16[32,1024]{1,0:T(8,128)(2,1)S(1)}, u32[]{:S(2)}, u32[]{:S(2)}) collective-permute-start(bf16[32,1024]{1,0:T(8,128)(2,1)S(1)} %all_gather.6), channel_id=1, source_target_pairs={{1,0},{2,1},{3,2},{4,3},{5,4},{6,5},{7,6},{9,8},{10,9},{11,10},{12... | collective-permute-start | bytes 196616 | tf_op jit(solution)/shard_map/ppermute | solution.py:10
  21.6 1.3 %copy-start.3 = (s32[64]{0:T(128)S(1)}, s32[64]{0:T(128)}, u32[]{:S(2)}) copy-start(s32[64]{0:T(128)} %param.11) | copy-start | bytes 772
  24.8 30.1 %copy-start.1 = (bf16[32,256]{1,0:T(8,128)(2,1)S(1)}, bf16[32,256]{1,0:T(8,128)(2,1)}, u32[]{:S(2)}) copy-start(bf16[32,256]{1,0:T(8,128)(2,1)} %param.9) | copy-start | bytes 49156
  26.2 7.0 %collective-permute-start.1 = (f32[32,1024]{1,0:T(8,128)S(1)}, f32[32,1024]{1,0:T(8,128)S(1)}, u32[]{:S(2)}, u32[]{:S(2)}) collective-permute-start(f32[32,1024]{1,0:T(8,128)S(1)} %slice.25), channel_id=1, source_target_pairs={{0,1},{1,2},{2,3},{3,4},{4,5},{5,6},{6,7},{8,9},{9,10},{10,11},{11... | collective-permute-start | bytes 393224 | tf_op jit(solution)/shard_map/ppermute | solution.py:10
  33.9 66.4 %reduce-scatter.5.cloned.1.call-start = ((), (), s32[]{:S(2)}) async-start(), calls=%async_computation.3 | async-start | bytes 163840 | tf_op jit(solution)/shard_map/reduce_scatter | solution.py:39
  55.7 44.7 %copy-start.2 = (bf16[32,256]{1,0:T(8,128)(2,1)}, bf16[32,256]{1,0:T(8,128)(2,1)S(1)}, u32[]{:S(2)}) copy-start(bf16[32,256]{1,0:T(8,128)(2,1)S(1)} %fusion.24) | copy-start | bytes 49156
  61.0 6.2 %collective-permute-start.2 = (bf16[32,1024]{1,0:T(8,128)(2,1)S(1)}, bf16[32,1024]{1,0:T(8,128)(2,1)S(1)}, u32[]{:S(2)}, u32[]{:S(2)}) collective-permute-start(bf16[32,1024]{1,0:T(8,128)(2,1)S(1)} %all_gather.7), channel_id=1, source_target_pairs={{1,0},{2,1},{3,2},{4,3},{5,4},{6,5},{7,6},{9,8},{10,9},{11,10},{12... | collective-permute-start | bytes 196616 | tf_op jit(solution)/shard_map/ppermute | solution.py:10
  73.1 6.8 %collective-permute-start.3 = (f32[32,1024]{1,0:T(8,128)S(1)}, f32[32,1024]{1,0:T(8,128)S(1)}, u32[]{:S(2)}, u32[]{:S(2)}) collective-permute-start(f32[32,1024]{1,0:T(8,128)S(1)} %slice.27), channel_id=1, source_target_pairs={{0,1},{1,2},{2,3},{3,4},{4,5},{5,6},{6,7},{8,9},{9,10},{10,11},{11... | collective-permute-start | bytes 393224 | tf_op jit(solution)/shard_map/ppermute | solution.py:10
Sparse Core Ops, SparseCore 0:
  34.0 20.8 reduce-scatter.2
  80.7 19.6 reduce-scatter.4
where the time goes:
time: 109 us
  waiting for transfers between devices  52.5 us (48%)
  between operations  16.2 us (15%)
  blocking collectives  11.8 us (11%)
  starting transfers between devices  11.5 us (11%)
  matrix products  8.9 us (8%)
  other arithmetic  4.89 us (4%)
  local copies, waits for them, and re-layouts  2.84 us (3%)
    reduce_scatter x2, waiting for transfers between devices, apply_operator(): lax.psum_scatter(lower_half + arrived, 'row', scatter_dimension=1, tiled=...  39.5 us
    ppermute x4, waiting for transfers between devices, passed_along(): return lax.ppermute(block, axis, route)  13 us
    all_gather x2, blocking collectives, apply_operator(): own_range = lax.all_gather(vectors_bf, 'row', axis=1, tiled=True)  11.8 us
    ppermute x4, starting transfers between devices, passed_along(): return lax.ppermute(block, axis, route)  11.4 us
    dot_general x2, matrix products, apply_operator(): jnp.einsum('kr,vkb->vrb', to_row, direct, precision=lax.Precision.HIGHEST)  2.52 us
    dot_general x2, matrix products, apply_operator(): jnp.einsum('kr,vkb->vrb', to_col, mirrored, precision=lax.Precision.HIGHEST)  2.5 us
    dot_general x2, matrix products, apply_operator(): jnp.einsum('vkb,kab->vka', picked_col, tile_data, preferred_element_type=...  2.46 us
  transfers between devices with their start and end apart: 6, of which 6 were waited for; matrix products, arithmetic and copies ran while one was open for 1% of the time, Pallas kernels for 0%

commit v1 on v0

v1 whole, which is shorter than its diff:
```python
import functools

import jax
import jax.numpy as jnp
from jax import lax
from jax.experimental import pallas as pl
from jax.experimental.pallas import tpu as pltpu
from jax.sharding import PartitionSpec as P

VMEM = pl.BlockSpec(memory_space=pltpu.VMEM)
SMEM = pl.BlockSpec(memory_space=pltpu.SMEM)
AXES = ("row", "col")


def row_swap(block, distance):
    rows, cols = lax.axis_size("row"), lax.axis_size("col")
    route = [(r * cols + c, (r ^ distance) * cols + c) for r in range(rows) for c in range(cols)]
    return lax.ppermute(block, AXES, route)


def pair_swap(block, odd):
    rows, cols = lax.axis_size("row"), lax.axis_size("col")
    route = []
    for r in range(rows):
        for c in range(odd, cols - 1, 2):
            route.append((r * cols + c, (r ^ 1) * cols + c + 1))
            route.append((r * cols + c + 1, (r ^ 1) * cols + c))
    return lax.ppermute(block, AXES, route)


def select_kernel(own_ref, even_ref, odd_ref, out_ref):
    parity = lax.rem(lax.axis_index("col"), 2)
    out_ref[0] = own_ref[...]

    @pl.when(parity == 0)
    def _():
        out_ref[1] = even_ref[...]

    @pl.when(parity == 1)
    def _():
        out_ref[1] = odd_ref[...]


def tiles_kernel(rows, blk, tile_row_ref, tile_offset_ref, live_ref, tile_ref, *refs):
    parts = refs[:rows]
    outs = refs[rows : 2 * rows]
    window, total = refs[2 * rows :]
    span = rows * blk
    size = tile_ref.shape[-1]
    me = lax.axis_index("row")
    for s in range(rows):
        for half in range(2):
            for b in range(blk):
                window[half * span + s * blk + b] = parts[s][half, :, b * size : (b + 1) * size]
    total[...] = jnp.zeros_like(total)
    own_mask = me * blk
    next_mask = (me ^ 1) * blk
    live = live_ref[0]

    def tile(k):
        i = tile_row_ref[k]
        j = i + tile_offset_ref[k]
        at_i = i ^ own_mask
        at_j = jnp.where(j < span, j ^ own_mask, span + ((j - span) ^ next_mask))
        to_i = jnp.where(k < live, at_i, 2 * span)
        to_j = jnp.where(k < live, at_j, 2 * span)
        u = tile_ref[k]
        direct = lax.dot_general(
            window[at_j], u, (((1,), (1,)), ((), ())), preferred_element_type=jnp.float32
        )
        mirrored = jnp.dot(window[at_i], u, preferred_element_type=jnp.float32)
        return to_i, to_j, direct, mirrored

    group = 8

    def body(g, carry):
        done = [tile(g * group + k) for k in range(group)]
        for to_i, to_j, direct, mirrored in done:
            total[to_i] += direct
            total[to_j] += mirrored
        return carry

    lax.fori_loop(0, tile_ref.shape[0] // group, body, 0)
    for s in range(rows):
        for half in range(2):
            for b in range(blk):
                outs[s][half, :, b * size : (b + 1) * size] = total[half * span + s * blk + b]


def add_kernel(rows, *refs):
    parts, (even_ref, odd_ref, sum_ref) = refs[:rows], refs[rows:]
    total = parts[0][...]
    for s in range(1, rows):
        total = total + parts[s][...]
    sum_ref[...] = total
    parity = lax.rem(lax.axis_index("col"), 2)

    @pl.when(parity == 0)
    def _():
        even_ref[...] = total[1]
        odd_ref[...] = total[0]

    @pl.when(parity == 1)
    def _():
        even_ref[...] = total[0]
        odd_ref[...] = total[1]


def first_kernel(center_ref, radius_ref, vectors_ref, sum_ref, even_ref, odd_ref, out_ref, first_ref):
    col = lax.axis_index("col")
    parity = lax.rem(col, 2)
    center, radius = center_ref[0], radius_ref[0]

    def degree(image, vectors):
        return ((image - center * vectors.astype(jnp.float32)) / radius).astype(jnp.bfloat16)

    def both(from_previous, from_next):
        own = degree(sum_ref[0] + from_previous[...], vectors_ref[0])
        out_ref[0] = own
        first_ref[...] = own
        inside = col < lax.axis_size("col") - 1
        beyond = degree(sum_ref[1] + from_next[...], vectors_ref[1])
        out_ref[1] = jnp.where(inside, beyond, jnp.zeros_like(beyond))

    @pl.when(parity == 0)
    def _():
        both(odd_ref, even_ref)

    @pl.when(parity == 1)
    def _():
        both(even_ref, odd_ref)


def second_kernel(center_ref, radius_ref, vectors_ref, first_ref, sum_ref, even_ref, odd_ref, out_ref):
    parity = lax.rem(lax.axis_index("col"), 2)
    center, radius = center_ref[0], radius_ref[0]

    def finish(from_previous):
        image = sum_ref[...] + from_previous[...]
        first = first_ref[...].astype(jnp.float32)
        out_ref[...] = 2.0 * (image - center * first) / radius - vectors_ref[...].astype(jnp.float32)

    @pl.when(parity == 0)
    def _():
        finish(odd_ref)

    @pl.when(parity == 1)
    def _():
        finish(even_ref)


def add_last_kernel(rows, *refs):
    parts, (low_ref, up_ref) = refs[:rows], refs[rows:]
    total = parts[0][...]
    for s in range(1, rows):
        total = total + parts[s][...]
    low_ref[...] = total[0]
    up_ref[...] = total[1]


def local(vectors, tile_data, tile_row, tile_offset, tile_live, damp_center, damp_radius):
    rows = lax.axis_size("row")
    count, width = vectors.shape
    size = tile_data.shape[-1]
    blk = width // size
    f32, bf16 = jnp.float32, jnp.bfloat16
    piece = jax.ShapeDtypeStruct((2, count, width), f32)
    single = jax.ShapeDtypeStruct((count, width), f32)
    pair_bf = jax.ShapeDtypeStruct((2, count, width), bf16)

    def apply(pair):
        gathered = [pair] + [row_swap(pair, s) for s in range(1, rows)]
        parts = pl.pallas_call(
            functools.partial(tiles_kernel, rows, blk),
            out_shape=[piece] * rows,
            in_specs=[SMEM] * 3 + [VMEM] * (1 + rows),
            out_specs=[VMEM] * rows,
            scratch_shapes=[
                pltpu.VMEM((2 * rows * blk, count, size), bf16),
                pltpu.VMEM((2 * rows * blk + 1, count, size), f32),
            ],
            name="tiles",
        )(tile_row, tile_offset, tile_live, tile_data, *gathered)
        return [parts[0]] + [row_swap(parts[s], s) for s in range(1, rows)]

    pair = pl.pallas_call(
        select_kernel, out_shape=pair_bf, in_specs=[VMEM] * 3, out_specs=VMEM, name="select"
    )(vectors, pair_swap(vectors, 0), pair_swap(vectors, 1))
    parts = apply(pair)
    even, odd, total = pl.pallas_call(
        functools.partial(add_kernel, rows),
        out_shape=[single, single, piece],
        in_specs=[VMEM] * rows,
        out_specs=[VMEM] * 3,
        name="add",
    )(*parts)
    first_pair, first = pl.pallas_call(
        first_kernel,
        out_shape=[pair_bf, jax.ShapeDtypeStruct((count, width), bf16)],
        in_specs=[SMEM] * 2 + [VMEM] * 4,
        out_specs=[VMEM] * 2,
        name="first",
    )(damp_center, damp_radius, pair, total, pair_swap(even, 0), pair_swap(odd, 1))
    parts = apply(first_pair)
    low, up = pl.pallas_call(
        functools.partial(add_last_kernel, rows),
        out_shape=[single, single],
        in_specs=[VMEM] * rows,
        out_specs=[VMEM] * 2,
        name="add_last",
    )(*parts)
    second = pl.pallas_call(
        second_kernel,
        out_shape=single,
        in_specs=[SMEM] * 2 + [VMEM] * 5,
        out_specs=VMEM,
        name="second",
    )(damp_center, damp_radius, vectors, first, low, pair_swap(up, 0), pair_swap(up, 1))
    return first, second


def solution(mesh):
    placed = (
        P(None, ("col", "row")),
        P(("col", "row"), None, None),
        P(("col", "row")),
        P(("col", "row")),
        P(("col", "row")),
        P(),
        P(),
    )
    return jax.shard_map(
        local,
        mesh=mesh,
        in_specs=placed,
        out_specs=(P(None, ("col", "row")), P(None, ("col", "row"))),
        check_vma=False,
    )
```

time: 109 us -> 67.8 us (0.62)
  the two profiles are of different devices: /device:TPU:0 before, /device:TPU:9 now
where the time goes in v1:
time: 67.8 us; the launch traced here: 67.3 us
  waiting for transfers between devices  24.5 us (36%)
  starting transfers between devices  18.1 us (27%)
  Pallas kernels  17.7 us (26%)
  local copies, waits for them, and re-layouts  4.32 us (6%)
  between operations  2.67 us (4%)
    ppermute x12, waiting for transfers between devices, row_swap(): return lax.ppermute(block, AXES, route)  12.8 us
    ppermute x6, waiting for transfers between devices, pair_swap(): return lax.ppermute(block, AXES, route)  11.8 us
    pallas_call x2, Pallas kernels, apply(): pl.pallas_call(functools.partial(tiles_kernel, rows, blk), out_shape=[pie...  10.2 us
    ppermute x6, starting transfers between devices, pair_swap(): return lax.ppermute(block, AXES, route)  9.44 us
    ppermute x12, starting transfers between devices, row_swap(): return lax.ppermute(block, AXES, route)  8.62 us
    unnamed x36, local copies, waits for them, and re-layouts  4.32 us
    pallas_call x1, Pallas kernels, local(): pl.pallas_call(functools.partial(add_kernel, rows), out_shape=[single, si...  1.6 us
    pallas_call x1, Pallas kernels, local(): pl.pallas_call(functools.partial(add_last_kernel, rows), out_shape=[singl...  1.57 us
  transfers between devices with their start and end apart: 18, of which 13 were waited for; matrix products, arithmetic and copies ran while one was open for 0% of the time, Pallas kernels for 0%

profile of v1, /device:TPU:9, one launch (start us, length us, event | category | flops | bytes accessed | tf_op | source)
XLA Modules:
  0.0 67.3 jit_solution(18197577360629557408)
XLA Ops:
  0.6 1.8 %collective-permute-start = (bf16[32,256]{1,0:T(8,128)(2,1)}, bf16[32,256]{1,0:T(8,128)(2,1)S(1)}, u32[]{:S(2)}, u32[]{:S(2)}) collective-permute-start(bf16[32,256]{1,0:T(8,128)(2,1)} %vectors_ref.1), channel_id=1, source_target_pairs={{0,9},{1,8},{2,11},{3,10},{4,13},{5,12},{6,15},{7,14},{8,1},{9,0},... | collective-permute-start | bytes 49160 | tf_op jit(solution)/shard_map/ppermute | solution.py:28
  2.5 1.9 %collective-permute-start.1 = (bf16[32,256]{1,0:T(8,128)(2,1)}, bf16[32,256]{1,0:T(8,128)(2,1)S(1)}, u32[]{:S(2)}, u32[]{:S(2)}) collective-permute-start(bf16[32,256]{1,0:T(8,128)(2,1)} %vectors_ref.1), channel_id=1, source_target_pairs={{1,10},{2,9},{3,12},{4,11},{5,14},{6,13},{9,2},{10,1},{11,4},{12,3... | collective-permute-start | bytes 49160 | tf_op jit(solution)/shard_map/ppermute | solution.py:28
  4.5 4.1 %collective-permute-done.1.odd_ref = bf16[32,256]{1,0:T(8,128)(2,1)S(1)} collective-permute-done((bf16[32,256]{1,0:T(8,128)(2,1)}, bf16[32,256]{1,0:T(8,128)(2,1)S(1)}, u32[]{:S(2)}, u32[]{:S(2)}) %collective-permute-start.1) | collective-permute-done | bytes 16416 | tf_op jit(solution)/shard_map/ppermute | solution.py:28
  9.2 1.4 %select.1.refs_0_.vectors_ref = bf16[2,32,256]{2,1,0:T(8,128)(2,1)} custom-call(bf16[32,256]{1,0:T(8,128)(2,1)} %vectors_ref.1, bf16[32,256]{1,0:T(8,128)(2,1)} %copy-done.16, bf16[32,256]{1,0:T(8,128)(2,1)} %copy-done.17), custom_call_target="tpu_custom_call" | custom-call | tf_op jit(solution)/shard_map/select/pallas_call | solution.py:186
  10.6 1.2 %collective-permute-start.3 = (bf16[2,32,256]{2,1,0:T(8,128)(2,1)}, bf16[2,32,256]{2,1,0:T(8,128)(2,1)S(1)}, u32[]{:S(2)}, u32[]{:S(2)}) collective-permute-start(bf16[2,32,256]{2,1,0:T(8,128)(2,1)} %select.1.refs_0_.vectors_ref), channel_id=1, source_target_pairs={{0,16},{1,17},{2,18},{3,19},{4,20},{5,21},{6,22},{7,23},{8,24},{9,... | collective-permute-start | bytes 98312 | tf_op jit(solution)/shard_map/ppermute | solution.py:18
  13.6 2.4 %collective-permute-done.4.refs_3_ = bf16[2,32,256]{2,1,0:T(8,128)(2,1)S(1)} collective-permute-done((bf16[2,32,256]{2,1,0:T(8,128)(2,1)}, bf16[2,32,256]{2,1,0:T(8,128)(2,1)S(1)}, u32[]{:S(2)}, u32[]{:S(2)}) %collective-permute-start.4) | collective-permute-done | bytes 32800 | tf_op jit(solution)/shard_map/ppermute | solution.py:18
  16.6 5.1 %tiles.2 = (f32[2,32,256]{2,1,0:T(8,128)}, f32[2,32,256]{2,1,0:T(8,128)}, f32[2,32,256]{2,1,0:T(8,128)}, f32[2,32,256]{2,1,0:T(8,128)}) custom-call(s32[64]{0:T(128)} %tile_row_ref.3, s32[64]{0:T(128)} %tile_offset_ref.3, s32[1]{0:T(128)S(6)} %copy.9.live_ref, bf16[64,128,128]{2,1,0:T(8,128)(2,1)} %tile_ref.3, ...), custom_call_target="tpu_custom_call" | custom-call | tf_op jit(solution)/shard_map/tiles/pallas_call | solution.py:173
  23.9 2.2 %collective-permute-done.6.refs_2_ = f32[2,32,256]{2,1,0:T(8,128)S(1)} collective-permute-done((f32[2,32,256]{2,1,0:T(8,128)}, f32[2,32,256]{2,1,0:T(8,128)S(1)}, u32[]{:S(2)}, u32[]{:S(2)}) %collective-permute-start.6) | collective-permute-done | bytes 65568 | tf_op jit(solution)/shard_map/ppermute | solution.py:18
  26.1 1.6 %collective-permute-done.7.refs_3_ = f32[2,32,256]{2,1,0:T(8,128)S(1)} collective-permute-done((f32[2,32,256]{2,1,0:T(8,128)}, f32[2,32,256]{2,1,0:T(8,128)S(1)}, u32[]{:S(2)}, u32[]{:S(2)}) %collective-permute-start.7) | collective-permute-done | bytes 65568 | tf_op jit(solution)/shard_map/ppermute | solution.py:18
  28.3 1.6 %add.1 = (f32[32,256]{1,0:T(8,128)}, f32[32,256]{1,0:T(8,128)}, f32[2,32,256]{2,1,0:T(8,128)}) custom-call(f32[2,32,256]{2,1,0:T(8,128)} %get-tuple-element.17.refs_0_, f32[2,32,256]{2,1,0:T(8,128)} %copy-done, f32[2,32,256]{2,1,0:T(8,128)} %copy-done.2, f32[2,32,256]{2,1,0:T(8,128)} %copy-done.4), custom_call_target="tpu_custom_call" | custom-call | tf_op jit(solution)/shard_map/add/pallas_call | solution.py:190
  30.4 1.9 %collective-permute-start.9 = (f32[32,256]{1,0:T(8,128)}, f32[32,256]{1,0:T(8,128)S(1)}, u32[]{:S(2)}, u32[]{:S(2)}) collective-permute-start(f32[32,256]{1,0:T(8,128)} %get-tuple-element.23), channel_id=1, source_target_pairs={{1,10},{2,9},{3,12},{4,11},{5,14},{6,13},{9,2},{10,1},{11,4},{12,3... | collective-permute-start | bytes 98312 | tf_op jit(solution)/shard_map/ppermute | solution.py:28
  33.6 3.1 %collective-permute-done.9.odd_ref = f32[32,256]{1,0:T(8,128)S(1)} collective-permute-done((f32[32,256]{1,0:T(8,128)}, f32[32,256]{1,0:T(8,128)S(1)}, u32[]{:S(2)}, u32[]{:S(2)}) %collective-permute-start.9) | collective-permute-done | bytes 32800 | tf_op jit(solution)/shard_map/ppermute | solution.py:28
  37.3 1.5 %first.1 = (bf16[2,32,256]{2,1,0:T(8,128)(2,1)}, bf16[32,256]{1,0:T(8,128)(2,1)}) custom-call(f32[1]{0:T(128)S(6)} %copy.10.center_ref, f32[1]{0:T(128)S(6)} %copy.11.radius_ref, bf16[2,32,256]{2,1,0:T(8,128)(2,1)} %select.1.refs_0_.vectors_ref, f32[2,32,256]{2,1,0:T(8,128)} %get-tuple-element.21.sum_ref, f32[32,256]{1,0:T(8,128)} %copy-done.12, ...), custom_call_target="tpu_custom_call" | custom-call | tf_op jit(solution)/shard_map/first/pallas_call | solution.py:197
  39.8 1.1 %collective-permute-start.12 = (bf16[2,32,256]{2,1,0:T(8,128)(2,1)}, bf16[2,32,256]{2,1,0:T(8,128)(2,1)S(1)}, u32[]{:S(2)}, u32[]{:S(2)}) collective-permute-start(bf16[2,32,256]{2,1,0:T(8,128)(2,1)} %get-tuple-element.25.refs_0_), channel_id=1, source_target_pairs={{0,24},{1,25},{2,26},{3,27},{4,28},{5,29},{6,30},{7,31},{8,16},{9,... | collective-permute-start | bytes 98312 | tf_op jit(solution)/shard_map/ppermute | solution.py:18
  40.9 1.0 %collective-permute-done.11.refs_2_ = bf16[2,32,256]{2,1,0:T(8,128)(2,1)S(1)} collective-permute-done((bf16[2,32,256]{2,1,0:T(8,128)(2,1)}, bf16[2,32,256]{2,1,0:T(8,128)(2,1)S(1)}, u32[]{:S(2)}, u32[]{:S(2)}) %collective-permute-start.11) | collective-permute-done | bytes 32800 | tf_op jit(solution)/shard_map/ppermute | solution.py:18
  41.9 1.8 %collective-permute-done.12.refs_3_ = bf16[2,32,256]{2,1,0:T(8,128)(2,1)S(1)} collective-permute-done((bf16[2,32,256]{2,1,0:T(8,128)(2,1)}, bf16[2,32,256]{2,1,0:T(8,128)(2,1)S(1)}, u32[]{:S(2)}, u32[]{:S(2)}) %collective-permute-start.12) | collective-permute-done | bytes 32800 | tf_op jit(solution)/shard_map/ppermute | solution.py:18
  44.3 5.1 %tiles.3 = (f32[2,32,256]{2,1,0:T(8,128)}, f32[2,32,256]{2,1,0:T(8,128)}, f32[2,32,256]{2,1,0:T(8,128)}, f32[2,32,256]{2,1,0:T(8,128)}) custom-call(s32[64]{0:T(128)} %tile_row_ref.3, s32[64]{0:T(128)} %tile_offset_ref.3, s32[1]{0:T(128)S(6)} %copy.9.live_ref, bf16[64,128,128]{2,1,0:T(8,128)(2,1)} %tile_ref.3, ...), custom_call_target="tpu_custom_call" | custom-call | tf_op jit(solution)/shard_map/tiles/pallas_call | solution.py:173
  51.6 2.1 %collective-permute-done.14.refs_2_ = f32[2,32,256]{2,1,0:T(8,128)S(1)} collective-permute-done((f32[2,32,256]{2,1,0:T(8,128)}, f32[2,32,256]{2,1,0:T(8,128)S(1)}, u32[]{:S(2)}, u32[]{:S(2)}) %collective-permute-start.14) | collective-permute-done | bytes 65568 | tf_op jit(solution)/shard_map/ppermute | solution.py:18
  53.7 1.6 %collective-permute-done.15.refs_3_ = f32[2,32,256]{2,1,0:T(8,128)S(1)} collective-permute-done((f32[2,32,256]{2,1,0:T(8,128)}, f32[2,32,256]{2,1,0:T(8,128)S(1)}, u32[]{:S(2)}, u32[]{:S(2)}) %collective-permute-start.15) | collective-permute-done | bytes 65568 | tf_op jit(solution)/shard_map/ppermute | solution.py:18
  55.9 1.6 %add_last.1 = (f32[32,256]{1,0:T(8,128)}, f32[32,256]{1,0:T(8,128)}) custom-call(f32[2,32,256]{2,1,0:T(8,128)} %get-tuple-element.26.refs_0_, f32[2,32,256]{2,1,0:T(8,128)} %copy-done.1, f32[2,32,256]{2,1,0:T(8,128)} %copy-done.3, f32[2,32,256]{2,1,0:T(8,128)} %copy-done.5), custom_call_target="tpu_custom_call" | custom-call | tf_op jit(solution)/shard_map/add_last/pallas_call | solution.py:205
  57.5 1.4 %collective-permute-start.16 = (f32[32,256]{1,0:T(8,128)}, f32[32,256]{1,0:T(8,128)S(1)}, u32[]{:S(2)}, u32[]{:S(2)}) collective-permute-start(f32[32,256]{1,0:T(8,128)} %get-tuple-element.31), channel_id=1, source_target_pairs={{0,9},{1,8},{2,11},{3,10},{4,13},{5,12},{6,15},{7,14},{8,1},{9,0},... | collective-permute-start | bytes 98312 | tf_op jit(solution)/shard_map/ppermute | solution.py:28
  58.9 1.9 %collective-permute-start.17 = (f32[32,256]{1,0:T(8,128)}, f32[32,256]{1,0:T(8,128)S(1)}, u32[]{:S(2)}, u32[]{:S(2)}) collective-permute-start(f32[32,256]{1,0:T(8,128)} %get-tuple-element.31), channel_id=1, source_target_pairs={{1,10},{2,9},{3,12},{4,11},{5,14},{6,13},{9,2},{10,1},{11,4},{12,3... | collective-permute-start | bytes 98312 | tf_op jit(solution)/shard_map/ppermute | solution.py:28
  61.1 4.2 %collective-permute-done.17.odd_ref = f32[32,256]{1,0:T(8,128)S(1)} collective-permute-done((f32[32,256]{1,0:T(8,128)}, f32[32,256]{1,0:T(8,128)S(1)}, u32[]{:S(2)}, u32[]{:S(2)}) %collective-permute-start.17) | collective-permute-done | bytes 32800 | tf_op jit(solution)/shard_map/ppermute | solution.py:28
  65.8 1.5 %second.1 = f32[32,256]{1,0:T(8,128)} custom-call(f32[1]{0:T(128)S(6)} %copy.10.center_ref, f32[1]{0:T(128)S(6)} %copy.11.radius_ref, bf16[32,256]{1,0:T(8,128)(2,1)} %vectors_ref.1, bf16[32,256]{1,0:T(8,128)(2,1)} %get-tuple-element.15.first_ref, f32[32,256]{1,0:T(8,128)} %get-tuple-element.30.sum_ref, f32[32,256]{1,0:T(8,128)} %copy-done.14, ...), custom_call_target="tpu_custom_call" | custom-call | tf_op jit(solution)/shard_map/second/pallas_call | solution.py:212
  (55 shorter events, 11.6 us)
Async XLA Ops:
  0.6 3.8 %collective-permute-start = (bf16[32,256]{1,0:T(8,128)(2,1)}, bf16[32,256]{1,0:T(8,128)(2,1)S(1)}, u32[]{:S(2)}, u32[]{:S(2)}) collective-permute-start(bf16[32,256]{1,0:T(8,128)(2,1)} %vectors_ref.1), channel_id=1, source_target_pairs={{0,9},{1,8},{2,11},{3,10},{4,13},{5,12},{6,15},{7,14},{8,1},{9,0},... | collective-permute-start | bytes 49160 | tf_op jit(solution)/shard_map/ppermute | solution.py:28
  2.5 6.2 %collective-permute-start.1 = (bf16[32,256]{1,0:T(8,128)(2,1)}, bf16[32,256]{1,0:T(8,128)(2,1)S(1)}, u32[]{:S(2)}, u32[]{:S(2)}) collective-permute-start(bf16[32,256]{1,0:T(8,128)(2,1)} %vectors_ref.1), channel_id=1, source_target_pairs={{1,10},{2,9},{3,12},{4,11},{5,14},{6,13},{9,2},{10,1},{11,4},{12,3... | collective-permute-start | bytes 49160 | tf_op jit(solution)/shard_map/ppermute | solution.py:28
  4.5 4.2 %copy-start.16 = (bf16[32,256]{1,0:T(8,128)(2,1)}, bf16[32,256]{1,0:T(8,128)(2,1)S(1)}, u32[]{:S(2)}) copy-start(bf16[32,256]{1,0:T(8,128)(2,1)S(1)} %collective-permute-done.even_ref) | copy-start | bytes 49156
  10.6 2.8 %collective-permute-start.2 = (bf16[2,32,256]{2,1,0:T(8,128)(2,1)}, bf16[2,32,256]{2,1,0:T(8,128)(2,1)S(1)}, u32[]{:S(2)}, u32[]{:S(2)}) collective-permute-start(bf16[2,32,256]{2,1,0:T(8,128)(2,1)} %select.1.refs_0_.vectors_ref), channel_id=1, source_target_pairs={{0,8},{1,9},{2,10},{3,11},{4,12},{5,13},{6,14},{7,15},{8,0},{9,1},... | collective-permute-start | bytes 98312 | tf_op jit(solution)/shard_map/ppermute | solution.py:18
  10.6 3.0 %collective-permute-start.3 = (bf16[2,32,256]{2,1,0:T(8,128)(2,1)}, bf16[2,32,256]{2,1,0:T(8,128)(2,1)S(1)}, u32[]{:S(2)}, u32[]{:S(2)}) collective-permute-start(bf16[2,32,256]{2,1,0:T(8,128)(2,1)} %select.1.refs_0_.vectors_ref), channel_id=1, source_target_pairs={{0,16},{1,17},{2,18},{3,19},{4,20},{5,21},{6,22},{7,23},{8,24},{9,... | collective-permute-start | bytes 98312 | tf_op jit(solution)/shard_map/ppermute | solution.py:18
  11.8 4.1 %collective-permute-start.4 = (bf16[2,32,256]{2,1,0:T(8,128)(2,1)}, bf16[2,32,256]{2,1,0:T(8,128)(2,1)S(1)}, u32[]{:S(2)}, u32[]{:S(2)}) collective-permute-start(bf16[2,32,256]{2,1,0:T(8,128)(2,1)} %select.1.refs_0_.vectors_ref), channel_id=1, source_target_pairs={{0,24},{1,25},{2,26},{3,27},{4,28},{5,29},{6,30},{7,31},{8,16},{9,... | collective-permute-start | bytes 98312 | tf_op jit(solution)/shard_map/ppermute | solution.py:18
  21.7 2.2 %collective-permute-start.5 = (f32[2,32,256]{2,1,0:T(8,128)}, f32[2,32,256]{2,1,0:T(8,128)S(1)}, u32[]{:S(2)}, u32[]{:S(2)}) collective-permute-start(f32[2,32,256]{2,1,0:T(8,128)} %get-tuple-element.18), channel_id=1, source_target_pairs={{0,8},{1,9},{2,10},{3,11},{4,12},{5,13},{6,14},{7,15},{8,0},{9,1},... | collective-permute-start | bytes 196616 | tf_op jit(solution)/shard_map/ppermute | solution.py:18
  22.2 3.9 %collective-permute-start.6 = (f32[2,32,256]{2,1,0:T(8,128)}, f32[2,32,256]{2,1,0:T(8,128)S(1)}, u32[]{:S(2)}, u32[]{:S(2)}) collective-permute-start(f32[2,32,256]{2,1,0:T(8,128)} %get-tuple-element.19), channel_id=1, source_target_pairs={{0,16},{1,17},{2,18},{3,19},{4,20},{5,21},{6,22},{7,23},{8,24},{9,... | collective-permute-start | bytes 196616 | tf_op jit(solution)/shard_map/ppermute | solution.py:18
  23.1 4.5 %collective-permute-start.7 = (f32[2,32,256]{2,1,0:T(8,128)}, f32[2,32,256]{2,1,0:T(8,128)S(1)}, u32[]{:S(2)}, u32[]{:S(2)}) collective-permute-start(f32[2,32,256]{2,1,0:T(8,128)} %get-tuple-element.20), channel_id=1, source_target_pairs={{0,24},{1,25},{2,26},{3,27},{4,28},{5,29},{6,30},{7,31},{8,16},{9,... | collective-permute-start | bytes 196616 | tf_op jit(solution)/shard_map/ppermute | solution.py:18
  23.9 3.7 %copy-start = (f32[2,32,256]{2,1,0:T(8,128)}, f32[2,32,256]{2,1,0:T(8,128)S(1)}, u32[]{:S(2)}) copy-start(f32[2,32,256]{2,1,0:T(8,128)S(1)} %collective-permute-done.5.refs_1_) | copy-start | bytes 196612
  29.9 3.7 %collective-permute-start.8 = (f32[32,256]{1,0:T(8,128)}, f32[32,256]{1,0:T(8,128)S(1)}, u32[]{:S(2)}, u32[]{:S(2)}) collective-permute-start(f32[32,256]{1,0:T(8,128)} %get-tuple-element.22), channel_id=1, source_target_pairs={{0,9},{1,8},{2,11},{3,10},{4,13},{5,12},{6,15},{7,14},{8,1},{9,0},... | collective-permute-start | bytes 98312 | tf_op jit(solution)/shard_map/ppermute | solution.py:28
  30.4 6.3 %collective-permute-start.9 = (f32[32,256]{1,0:T(8,128)}, f32[32,256]{1,0:T(8,128)S(1)}, u32[]{:S(2)}, u32[]{:S(2)}) collective-permute-start(f32[32,256]{1,0:T(8,128)} %get-tuple-element.23), channel_id=1, source_target_pairs={{1,10},{2,9},{3,12},{4,11},{5,14},{6,13},{9,2},{10,1},{11,4},{12,3... | collective-permute-start | bytes 98312 | tf_op jit(solution)/shard_map/ppermute | solution.py:28
  33.6 3.1 %copy-start.12 = (f32[32,256]{1,0:T(8,128)}, f32[32,256]{1,0:T(8,128)S(1)}, u32[]{:S(2)}) copy-start(f32[32,256]{1,0:T(8,128)S(1)} %collective-permute-done.8.even_ref) | copy-start | bytes 98308
  38.8 2.1 %collective-permute-start.10 = (bf16[2,32,256]{2,1,0:T(8,128)(2,1)}, bf16[2,32,256]{2,1,0:T(8,128)(2,1)S(1)}, u32[]{:S(2)}, u32[]{:S(2)}) collective-permute-start(bf16[2,32,256]{2,1,0:T(8,128)(2,1)} %get-tuple-element.25.refs_0_), channel_id=1, source_target_pairs={{0,8},{1,9},{2,10},{3,11},{4,12},{5,13},{6,14},{7,15},{8,0},{9,1},... | collective-permute-start | bytes 98312 | tf_op jit(solution)/shard_map/ppermute | solution.py:18
  38.9 3.0 %collective-permute-start.11 = (bf16[2,32,256]{2,1,0:T(8,128)(2,1)}, bf16[2,32,256]{2,1,0:T(8,128)(2,1)S(1)}, u32[]{:S(2)}, u32[]{:S(2)}) collective-permute-start(bf16[2,32,256]{2,1,0:T(8,128)(2,1)} %get-tuple-element.25.refs_0_), channel_id=1, source_target_pairs={{0,16},{1,17},{2,18},{3,19},{4,20},{5,21},{6,22},{7,23},{8,24},{9,... | collective-permute-start | bytes 98312 | tf_op jit(solution)/shard_map/ppermute | solution.py:18
  39.8 3.9 %collective-permute-start.12 = (bf16[2,32,256]{2,1,0:T(8,128)(2,1)}, bf16[2,32,256]{2,1,0:T(8,128)(2,1)S(1)}, u32[]{:S(2)}, u32[]{:S(2)}) collective-permute-start(bf16[2,32,256]{2,1,0:T(8,128)(2,1)} %get-tuple-element.25.refs_0_), channel_id=1, source_target_pairs={{0,24},{1,25},{2,26},{3,27},{4,28},{5,29},{6,30},{7,31},{8,16},{9,... | collective-permute-start | bytes 98312 | tf_op jit(solution)/shard_map/ppermute | solution.py:18
  40.9 2.8 %copy-start.6 = (bf16[2,32,256]{2,1,0:T(8,128)(2,1)}, bf16[2,32,256]{2,1,0:T(8,128)(2,1)S(1)}, u32[]{:S(2)}) copy-start(bf16[2,32,256]{2,1,0:T(8,128)(2,1)S(1)} %collective-permute-done.10.refs_1_) | copy-start | bytes 98308
  49.5 2.1 %collective-permute-start.13 = (f32[2,32,256]{2,1,0:T(8,128)}, f32[2,32,256]{2,1,0:T(8,128)S(1)}, u32[]{:S(2)}, u32[]{:S(2)}) collective-permute-start(f32[2,32,256]{2,1,0:T(8,128)} %get-tuple-element.27), channel_id=1, source_target_pairs={{0,8},{1,9},{2,10},{3,11},{4,12},{5,13},{6,14},{7,15},{8,0},{9,1},... | collective-permute-start | bytes 196616 | tf_op jit(solution)/shard_map/ppermute | solution.py:18
  49.9 3.9 %collective-permute-start.14 = (f32[2,32,256]{2,1,0:T(8,128)}, f32[2,32,256]{2,1,0:T(8,128)S(1)}, u32[]{:S(2)}, u32[]{:S(2)}) collective-permute-start(f32[2,32,256]{2,1,0:T(8,128)} %get-tuple-element.28), channel_id=1, source_target_pairs={{0,16},{1,17},{2,18},{3,19},{4,20},{5,21},{6,22},{7,23},{8,24},{9,... | collective-permute-start | bytes 196616 | tf_op jit(solution)/shard_map/ppermute | solution.py:18
  50.7 4.7 %collective-permute-start.15 = (f32[2,32,256]{2,1,0:T(8,128)}, f32[2,32,256]{2,1,0:T(8,128)S(1)}, u32[]{:S(2)}, u32[]{:S(2)}) collective-permute-start(f32[2,32,256]{2,1,0:T(8,128)} %get-tuple-element.29), channel_id=1, source_target_pairs={{0,24},{1,25},{2,26},{3,27},{4,28},{5,29},{6,30},{7,31},{8,16},{9,... | collective-permute-start | bytes 196616 | tf_op jit(solution)/shard_map/ppermute | solution.py:18
  51.6 3.7 %copy-start.1 = (f32[2,32,256]{2,1,0:T(8,128)}, f32[2,32,256]{2,1,0:T(8,128)S(1)}, u32[]{:S(2)}) copy-start(f32[2,32,256]{2,1,0:T(8,128)S(1)} %collective-permute-done.13.refs_1_) | copy-start | bytes 196612
  57.5 3.6 %collective-permute-start.16 = (f32[32,256]{1,0:T(8,128)}, f32[32,256]{1,0:T(8,128)S(1)}, u32[]{:S(2)}, u32[]{:S(2)}) collective-permute-start(f32[32,256]{1,0:T(8,128)} %get-tuple-element.31), channel_id=1, source_target_pairs={{0,9},{1,8},{2,11},{3,10},{4,13},{5,12},{6,15},{7,14},{8,1},{9,0},... | collective-permute-start | bytes 98312 | tf_op jit(solution)/shard_map/ppermute | solution.py:28
  58.9 6.3 %collective-permute-start.17 = (f32[32,256]{1,0:T(8,128)}, f32[32,256]{1,0:T(8,128)S(1)}, u32[]{:S(2)}, u32[]{:S(2)}) collective-permute-start(f32[32,256]{1,0:T(8,128)} %get-tuple-element.31), channel_id=1, source_target_pairs={{1,10},{2,9},{3,12},{4,11},{5,14},{6,13},{9,2},{10,1},{11,4},{12,3... | collective-permute-start | bytes 98312 | tf_op jit(solution)/shard_map/ppermute | solution.py:28
  61.1 4.2 %copy-start.14 = (f32[32,256]{1,0:T(8,128)}, f32[32,256]{1,0:T(8,128)S(1)}, u32[]{:S(2)}) copy-start(f32[32,256]{1,0:T(8,128)S(1)} %collective-permute-done.16.even_ref) | copy-start | bytes 98308
  (12 other events, 14.2 us)

commit v2 on v1

--- a/solution.py
+++ b/solution.py
@@ -9,7 +9,12 @@
 
 VMEM = pl.BlockSpec(memory_space=pltpu.VMEM)
 SMEM = pl.BlockSpec(memory_space=pltpu.SMEM)
+PARAMS = pltpu.CompilerParams(vmem_limit_bytes=12 * 1024 * 1024)
 AXES = ("row", "col")
+
+
+def near(array):
+    return pltpu.with_memory_space_constraint(array, pltpu.VMEM)
 
 
 def row_swap(block, distance):
@@ -22,26 +27,44 @@
     rows, cols = lax.axis_size("row"), lax.axis_size("col")
     route = []
     for r in range(rows):
-        for c in range(odd, cols - 1, 2):
-            route.append((r * cols + c, (r ^ 1) * cols + c + 1))
-            route.append((r * cols + c + 1, (r ^ 1) * cols + c))
+        for c in range(cols):
+            other = c + 1 if c % 2 == odd else c - 1
+            other = other if 0 <= other < cols else c
+            route.append((r * cols + c, (r ^ 1) * cols + other))
     return lax.ppermute(block, AXES, route)
 
 
+def load_kernel(chunk, vectors_ref, tile_ref, kept_ref, out_ref, flipped_ref, sems):
+    count = tile_ref.shape[0] // chunk
+
+    def copy(g):
+        part = pl.ds(g * chunk, chunk)
+        return pltpu.make_async_copy(tile_ref.at[part], out_ref.at[part], sems.at[g])
+
+    for g in range(count):
+        copy(g).start()
+    kept_ref[...] = vectors_ref[...]
+    for g in range(count):
+        copy(g).wait()
+        for k in range(g * chunk, (g + 1) * chunk):
+            flipped_ref[k] = out_ref[k].T
+
+
 def select_kernel(own_ref, even_ref, odd_ref, out_ref):
-    parity = lax.rem(lax.axis_index("col"), 2)
+    col = lax.axis_index("col")
     out_ref[0] = own_ref[...]
 
-    @pl.when(parity == 0)
+    @pl.when(lax.rem(col, 2) == 0)
     def _():
         out_ref[1] = even_ref[...]
 
-    @pl.when(parity == 1)
-    def _():
-        out_ref[1] = odd_ref[...]
-
-
-def tiles_kernel(rows, blk, tile_row_ref, tile_offset_ref, live_ref, tile_ref, *refs):
+    @pl.when(lax.rem(col, 2) == 1)
+    def _():
+        inside = col < lax.axis_size("col") - 1
+        out_ref[1] = jnp.where(inside, odd_ref[...], jnp.zeros_like(odd_ref))
+
+
+def tiles_kernel(rows, blk, tile_row_ref, tile_offset_ref, live_ref, tile_ref, flipped_ref, *refs):
     parts = refs[:rows]
     outs = refs[rows : 2 * rows]
     window, total = refs[2 * rows :]
@@ -64,11 +87,8 @@
         at_j = jnp.where(j < span, j ^ own_mask, span + ((j - span) ^ next_mask))
         to_i = jnp.where(k < live, at_i, 2 * span)
         to_j = jnp.where(k < live, at_j, 2 * span)
-        u = tile_ref[k]
-        direct = lax.dot_general(
-            window[at_j], u, (((1,), (1,)), ((), ())), preferred_element_type=jnp.float32
-        )
-        mirrored = jnp.dot(window[at_i], u, preferred_element_type=jnp.float32)
+        direct = jnp.dot(window[at_j], flipped_ref[k], preferred_element_type=jnp.float32)
+        mirrored = jnp.dot(window[at_i], tile_ref[k], preferred_element_type=jnp.float32)
         return to_i, to_j, direct, mirrored
 
     group = 8
@@ -115,7 +135,8 @@
         return ((image - center * vectors.astype(jnp.float32)) / radius).astype(jnp.bfloat16)
 
     def both(from_previous, from_next):
-        own = degree(sum_ref[0] + from_previous[...], vectors_ref[0])
+        arrived = jnp.where(col > 0, from_previous[...], 0.0)
+        own = degree(sum_ref[0] + arrived, vectors_ref[0])
         out_ref[0] = own
         first_ref[...] = own
         inside = col < lax.axis_size("col") - 1
@@ -131,12 +152,14 @@
         both(even_ref, odd_ref)
 
 
-def second_kernel(center_ref, radius_ref, vectors_ref, first_ref, sum_ref, even_ref, odd_ref, out_ref):
-    parity = lax.rem(lax.axis_index("col"), 2)
+def second_kernel(center_ref, radius_ref, vectors_ref, first_ref, sum_ref, even_ref, odd_ref, out_ref, first_out_ref):
+    col = lax.axis_index("col")
+    parity = lax.rem(col, 2)
     center, radius = center_ref[0], radius_ref[0]
+    first_out_ref[...] = first_ref[...]
 
     def finish(from_previous):
-        image = sum_ref[...] + from_previous[...]
+        image = sum_ref[...] + jnp.where(col > 0, from_previous[...], 0.0)
         first = first_ref[...].astype(jnp.float32)
         out_ref[...] = 2.0 * (image - center * first) / radius - vectors_ref[...].astype(jnp.float32)
 
@@ -164,58 +187,83 @@
     size = tile_data.shape[-1]
     blk = width // size
     f32, bf16 = jnp.float32, jnp.bfloat16
-    piece = jax.ShapeDtypeStruct((2, count, width), f32)
-    single = jax.ShapeDtypeStruct((count, width), f32)
-    pair_bf = jax.ShapeDtypeStruct((2, count, width), bf16)
+    piece = pltpu.VMEM((2, count, width), f32)
+    single = pltpu.VMEM((count, width), f32)
+    pair_bf = pltpu.VMEM((2, count, width), bf16)
+    sent = pair_swap(vectors, 0), pair_swap(vectors, 1)
+    kept = pltpu.VMEM(tile_data.shape, bf16)
+    chunk = 8
+    vectors, tile_data, flipped = pl.pallas_call(
+        functools.partial(load_kernel, chunk),
+        out_shape=[pltpu.VMEM(vectors.shape, bf16), kept, kept],
+        in_specs=[VMEM, pl.BlockSpec(memory_space=pltpu.HBM)],
+        out_specs=[VMEM] * 3,
+        scratch_shapes=[pltpu.SemaphoreType.DMA((tile_data.shape[0] // chunk,))],
+        compiler_params=PARAMS,
+        cost_estimate=pl.CostEstimate(
+            flops=0, bytes_accessed=3 * tile_data.size * 2, transcendentals=0
+        ),
+        name="load",
+    )(vectors, pltpu.with_memory_space_constraint(tile_data, pltpu.HBM))
+    tile_data, flipped = near(tile_data), near(flipped)
 
     def apply(pair):
-        gathered = [pair] + [row_swap(pair, s) for s in range(1, rows)]
+        gathered = [near(pair)] + [near(row_swap(pair, s)) for s in range(1, rows)]
         parts = pl.pallas_call(
             functools.partial(tiles_kernel, rows, blk),
             out_shape=[piece] * rows,
-            in_specs=[SMEM] * 3 + [VMEM] * (1 + rows),
+            in_specs=[SMEM] * 3 + [VMEM] * (2 + rows),
             out_specs=[VMEM] * rows,
             scratch_shapes=[
                 pltpu.VMEM((2 * rows * blk, count, size), bf16),
                 pltpu.VMEM((2 * rows * blk + 1, count, size), f32),
             ],
-            name="tiles",
-        )(tile_row, tile_offset, tile_live, tile_data, *gathered)
-        return [parts[0]] + [row_swap(parts[s], s) for s in range(1, rows)]
+            compiler_params=PARAMS,
+        name="tiles",
+        )(tile_row, tile_offset, tile_live, tile_data, flipped, *gathered)
+        return [near(parts[0])] + [near(row_swap(parts[s], s)) for s in range(1, rows)]
 
     pair = pl.pallas_call(
-        select_kernel, out_shape=pair_bf, in_specs=[VMEM] * 3, out_specs=VMEM, name="select"
-    )(vectors, pair_swap(vectors, 0), pair_swap(vectors, 1))
+        select_kernel, out_shape=pair_bf, in_specs=[VMEM] * 3, out_specs=VMEM,
+        compiler_params=PARAMS, name="select"
+    )(near(vectors), near(sent[0]), near(sent[1]))
     parts = apply(pair)
     even, odd, total = pl.pallas_call(
         functools.partial(add_kernel, rows),
         out_shape=[single, single, piece],
         in_specs=[VMEM] * rows,
         out_specs=[VMEM] * 3,
+        compiler_params=PARAMS,
         name="add",
     )(*parts)
     first_pair, first = pl.pallas_call(
         first_kernel,
-        out_shape=[pair_bf, jax.ShapeDtypeStruct((count, width), bf16)],
+        out_shape=[pair_bf, pltpu.VMEM((count, width), bf16)],
         in_specs=[SMEM] * 2 + [VMEM] * 4,
         out_specs=[VMEM] * 2,
+        compiler_params=PARAMS,
         name="first",
-    )(damp_center, damp_radius, pair, total, pair_swap(even, 0), pair_swap(odd, 1))
+    )(damp_center, damp_radius, near(pair), near(total), near(pair_swap(even, 0)), near(pair_swap(odd, 1)))
     parts = apply(first_pair)
     low, up = pl.pallas_call(
         functools.partial(add_last_kernel, rows),
         out_shape=[single, single],
         in_specs=[VMEM] * rows,
         out_specs=[VMEM] * 2,
+        compiler_params=PARAMS,
         name="add_last",
     )(*parts)
-    second = pl.pallas_call(
+    second, first = pl.pallas_call(
         second_kernel,
-        out_shape=single,
+        out_shape=[
+            jax.ShapeDtypeStruct((count, width), f32),
+            jax.ShapeDtypeStruct((count, width), bf16),
+        ],
         in_specs=[SMEM] * 2 + [VMEM] * 5,
-        out_specs=VMEM,
+        out_specs=[VMEM] * 2,
+        compiler_params=PARAMS,
         name="second",
-    )(damp_center, damp_radius, vectors, first, low, pair_swap(up, 0), pair_swap(up, 1))
+    )(damp_center, damp_radius, near(vectors), near(first), near(low), near(pair_swap(up, 0)), near(pair_swap(up, 1)))
     return first, second
 
 

time: 67.8 us -> 44.9 us (0.66)
  Pallas kernels: 17.7 us -> 8.05 us
  starting transfers between devices: 18.1 us -> 12.1 us
  waiting for transfers between devices: 24.5 us -> 20.9 us
  local copies, waits for them, and re-layouts: 4.32 us -> 0.79 us
    ppermute x6, starting transfers between devices: 9.44 us -> 3.33 us  [pair_swap(): return lax.ppermute(block, AXES, route)]
    pallas_call x2, Pallas kernels: 10.2 us -> 5.32 us  [apply(): pl.pallas_call(functools.partial(tiles_kernel, rows, blk), out_shape=[pie...]
    unnamed x36 -> x6, local copies, waits for them, and re-layouts: 4.32 us -> 0.79 us
    ppermute x6, waiting for transfers between devices: 11.8 us -> 8.61 us  [pair_swap(): return lax.ppermute(block, AXES, route)]
    pallas_call x1, Pallas kernels: 1.6 us -> 0.02 us  [local(): pl.pallas_call(functools.partial(add_kernel, rows), out_shape=[single, si...]
    pallas_call x1, Pallas kernels: 1.57 us -> 0.02 us  [local(): pl.pallas_call(functools.partial(add_last_kernel, rows), out_shape=[singl...]
    pallas_call x1, Pallas kernels: 1.37 us -> 0.01 us  [local(): pl.pallas_call(select_kernel, out_shape=pair_bf, in_specs=[VMEM] * 3, out...]
    pallas_call x2 -> x3, Pallas kernels: 2.93 us -> 2.68 us  [the longest x1 2.03 us: local(): pl.pallas_call(functools.partial(load_kernel, chunk), out_shape=[pltpu.VM...]
  transfers between devices with their start and end apart: 18 -> 18, of which waited for: 13 -> 12; matrix products, arithmetic and copies ran while one was open for 0% -> 0% of each run, Pallas kernels for 0% -> 5%
where the time goes in v2:
time: 44.9 us; the launch traced here: 44.5 us
  waiting for transfers between devices  20.9 us (47%)
  starting transfers between devices  12.1 us (27%)
  Pallas kernels  8.05 us (18%)
  between operations  2.66 us (6%)
  local copies, waits for them, and re-layouts  0.79 us (2%)
    ppermute x12, waiting for transfers between devices, row_swap(): return lax.ppermute(block, AXES, route)  12.3 us
    ppermute x12, starting transfers between devices, row_swap(): return lax.ppermute(block, AXES, route)  8.8 us
    ppermute x6, waiting for transfers between devices, pair_swap(): return lax.ppermute(block, AXES, route)  8.61 us
    pallas_call x2, Pallas kernels, apply(): pl.pallas_call(functools.partial(tiles_kernel, rows, blk), out_shape=[pie...  5.32 us
    ppermute x6, starting transfers between devices, pair_swap(): return lax.ppermute(block, AXES, route)  3.33 us
    pallas_call x1, Pallas kernels, local(): pl.pallas_call(functools.partial(load_kernel, chunk), out_shape=[pltpu.VM...  2.03 us
  transfers between devices with their start and end apart: 18, of which 12 were waited for; matrix products, arithmetic and copies ran while one was open for 0% of the time, Pallas kernels for 5%

profile of v2, /device:TPU:9, one launch (start us, length us, event | category | flops | bytes accessed | tf_op | source)
XLA Modules:
  0.0 44.5 jit_solution(13586921595799044714)
XLA Ops:
  0.6 1.8 %collective-permute-start = (bf16[32,256]{1,0:T(8,128)(2,1)}, bf16[32,256]{1,0:T(8,128)(2,1)S(1)}, u32[]{:S(2)}, u32[]{:S(2)}) collective-permute-start(bf16[32,256]{1,0:T(8,128)(2,1)} %vectors_ref.1), channel_id=1, source_target_pairs={{0,9},{1,8},{2,11},{3,10},{4,13},{5,12},{6,15},{7,14},{8,1},{9,0},... | collective-permute-start | bytes 49160 | tf_op jit(solution)/shard_map/ppermute | solution.py:34
  2.5 0.8 %copy-done = bf16[32,256]{1,0:T(8,128)(2,1)S(1)} copy-done((bf16[32,256]{1,0:T(8,128)(2,1)S(1)}, bf16[32,256]{1,0:T(8,128)(2,1)}, u32[]{:S(2)}) %copy-start) | copy-done | bytes 16408
  3.3 2.0 %load.1 = (bf16[32,256]{1,0:T(8,128)(2,1)S(1)}, bf16[64,128,128]{2,1,0:T(8,128)(2,1)S(1)}, bf16[64,128,128]{2,1,0:T(8,128)(2,1)S(1)}) custom-call(bf16[32,256]{1,0:T(8,128)(2,1)S(1)} %copy-done, bf16[64,128,128]{2,1,0:T(8,128)(2,1)} %tile_ref.1), custom_call_target="tpu_custom_call" | custom-call | bytes 6291456 | tf_op jit(solution)/shard_map/load/pallas_call | solution.py:196
  5.3 1.4 %collective-permute-done.1.odd_ref = bf16[32,256]{1,0:T(8,128)(2,1)S(1)} collective-permute-done((bf16[32,256]{1,0:T(8,128)(2,1)}, bf16[32,256]{1,0:T(8,128)(2,1)S(1)}, u32[]{:S(2)}, u32[]{:S(2)}) %collective-permute-start.1) | collective-permute-done | bytes 16416 | tf_op jit(solution)/shard_map/ppermute | solution.py:34
  6.7 1.3 %collective-permute-start.3 = (bf16[2,32,256]{2,1,0:T(8,128)(2,1)S(1)}, bf16[2,32,256]{2,1,0:T(8,128)(2,1)S(1)}, u32[]{:S(2)}, u32[]{:S(2)}) collective-permute-start(bf16[2,32,256]{2,1,0:T(8,128)(2,1)S(1)} %select.1.refs_0_.vectors_ref), channel_id=1, source_target_pairs={{0,16},{1,17},{2,18},{3,19},{4,20},{5,21},{6,22},{7,23},{8,24},{9,... | collective-permute-start | bytes 98312 | tf_op jit(solution)/shard_map/ppermute | solution.py:23
  8.0 0.8 %collective-permute-start.4 = (bf16[2,32,256]{2,1,0:T(8,128)(2,1)S(1)}, bf16[2,32,256]{2,1,0:T(8,128)(2,1)S(1)}, u32[]{:S(2)}, u32[]{:S(2)}) collective-permute-start(bf16[2,32,256]{2,1,0:T(8,128)(2,1)S(1)} %select.1.refs_0_.vectors_ref), channel_id=1, source_target_pairs={{0,24},{1,25},{2,26},{3,27},{4,28},{5,29},{6,30},{7,31},{8,16},{9,... | collective-permute-start | bytes 98312 | tf_op jit(solution)/shard_map/ppermute | solution.py:23
  9.6 2.4 %collective-permute-done.4.refs_3_ = bf16[2,32,256]{2,1,0:T(8,128)(2,1)S(1)} collective-permute-done((bf16[2,32,256]{2,1,0:T(8,128)(2,1)S(1)}, bf16[2,32,256]{2,1,0:T(8,128)(2,1)S(1)}, u32[]{:S(2)}, u32[]{:S(2)}) %collective-permute-start.4) | collective-permute-done | bytes 32800 | tf_op jit(solution)/shard_map/ppermute | solution.py:23
  12.0 2.7 %tiles.2 = (f32[2,32,256]{2,1,0:T(8,128)S(1)}, f32[2,32,256]{2,1,0:T(8,128)S(1)}, f32[2,32,256]{2,1,0:T(8,128)S(1)}, f32[2,32,256]{2,1,0:T(8,128)S(1)}) custom-call(s32[64]{0:T(128)S(1)} %copy-done.1, s32[64]{0:T(128)S(1)} %copy-done.2, s32[1]{0:T(128)S(6)} %copy.9.live_ref, bf16[64,128,128]{2,1,0:T(8,128)(2,1)S(1)} %get-tuple-element.23.tile_ref, ...), custom_call_target="tpu_custom_call" | custom-call | tf_op jit(solution)/shard_map/tiles/pallas_call | solution.py:212
  15.5 1.4 %collective-permute-start.7 = (f32[2,32,256]{2,1,0:T(8,128)S(1)}, f32[2,32,256]{2,1,0:T(8,128)S(1)}, u32[]{:S(2)}, u32[]{:S(2)}) collective-permute-start(f32[2,32,256]{2,1,0:T(8,128)S(1)} %get-tuple-element.28), channel_id=1, source_target_pairs={{0,24},{1,25},{2,26},{3,27},{4,28},{5,29},{6,30},{7,31},{8,16},{9,... | collective-permute-start | bytes 196616 | tf_op jit(solution)/shard_map/ppermute | solution.py:23
  16.9 2.0 %collective-permute-done.6.refs_2_ = f32[2,32,256]{2,1,0:T(8,128)S(1)} collective-permute-done((f32[2,32,256]{2,1,0:T(8,128)S(1)}, f32[2,32,256]{2,1,0:T(8,128)S(1)}, u32[]{:S(2)}, u32[]{:S(2)}) %collective-permute-start.6) | collective-permute-done | bytes 65568 | tf_op jit(solution)/shard_map/ppermute | solution.py:23
  18.9 1.6 %collective-permute-done.7.refs_3_ = f32[2,32,256]{2,1,0:T(8,128)S(1)} collective-permute-done((f32[2,32,256]{2,1,0:T(8,128)S(1)}, f32[2,32,256]{2,1,0:T(8,128)S(1)}, u32[]{:S(2)}, u32[]{:S(2)}) %collective-permute-start.7) | collective-permute-done | bytes 65568 | tf_op jit(solution)/shard_map/ppermute | solution.py:23
  20.5 0.9 %collective-permute-start.8 = (f32[32,256]{1,0:T(8,128)S(1)}, f32[32,256]{1,0:T(8,128)S(1)}, u32[]{:S(2)}, u32[]{:S(2)}) collective-permute-start(f32[32,256]{1,0:T(8,128)S(1)} %get-tuple-element.30), channel_id=1, source_target_pairs={{0,9},{1,8},{2,11},{3,10},{4,13},{5,12},{6,15},{7,14},{8,1},{9,0},... | collective-permute-start | bytes 98312 | tf_op jit(solution)/shard_map/ppermute | solution.py:34
  22.6 1.2 %collective-permute-done.8.even_ref = f32[32,256]{1,0:T(8,128)S(1)} collective-permute-done((f32[32,256]{1,0:T(8,128)S(1)}, f32[32,256]{1,0:T(8,128)S(1)}, u32[]{:S(2)}, u32[]{:S(2)}) %collective-permute-start.8) | collective-permute-done | bytes 32800 | tf_op jit(solution)/shard_map/ppermute | solution.py:34
  23.9 1.7 %collective-permute-done.9.odd_ref = f32[32,256]{1,0:T(8,128)S(1)} collective-permute-done((f32[32,256]{1,0:T(8,128)S(1)}, f32[32,256]{1,0:T(8,128)S(1)}, u32[]{:S(2)}, u32[]{:S(2)}) %collective-permute-start.9) | collective-permute-done | bytes 32800 | tf_op jit(solution)/shard_map/ppermute | solution.py:34
  26.0 0.6 %collective-permute-start.11 = (bf16[2,32,256]{2,1,0:T(8,128)(2,1)S(1)}, bf16[2,32,256]{2,1,0:T(8,128)(2,1)S(1)}, u32[]{:S(2)}, u32[]{:S(2)}) collective-permute-start(bf16[2,32,256]{2,1,0:T(8,128)(2,1)S(1)} %get-tuple-element.33.refs_0_), channel_id=1, source_target_pairs={{0,16},{1,17},{2,18},{3,19},{4,20},{5,21},{6,22},{7,23},{8,24},{9,... | collective-permute-start | bytes 98312 | tf_op jit(solution)/shard_map/ppermute | solution.py:23
  26.6 1.2 %collective-permute-start.12 = (bf16[2,32,256]{2,1,0:T(8,128)(2,1)S(1)}, bf16[2,32,256]{2,1,0:T(8,128)(2,1)S(1)}, u32[]{:S(2)}, u32[]{:S(2)}) collective-permute-start(bf16[2,32,256]{2,1,0:T(8,128)(2,1)S(1)} %get-tuple-element.33.refs_0_), channel_id=1, source_target_pairs={{0,24},{1,25},{2,26},{3,27},{4,28},{5,29},{6,30},{7,31},{8,16},{9,... | collective-permute-start | bytes 98312 | tf_op jit(solution)/shard_map/ppermute | solution.py:23
  27.8 0.9 %collective-permute-done.11.refs_2_ = bf16[2,32,256]{2,1,0:T(8,128)(2,1)S(1)} collective-permute-done((bf16[2,32,256]{2,1,0:T(8,128)(2,1)S(1)}, bf16[2,32,256]{2,1,0:T(8,128)(2,1)S(1)}, u32[]{:S(2)}, u32[]{:S(2)}) %collective-permute-start.11) | collective-permute-done | bytes 32800 | tf_op jit(solution)/shard_map/ppermute | solution.py:23
  28.8 1.8 %collective-permute-done.12.refs_3_ = bf16[2,32,256]{2,1,0:T(8,128)(2,1)S(1)} collective-permute-done((bf16[2,32,256]{2,1,0:T(8,128)(2,1)S(1)}, bf16[2,32,256]{2,1,0:T(8,128)(2,1)S(1)}, u32[]{:S(2)}, u32[]{:S(2)}) %collective-permute-start.12) | collective-permute-done | bytes 32800 | tf_op jit(solution)/shard_map/ppermute | solution.py:23
  30.6 2.7 %tiles.3 = (f32[2,32,256]{2,1,0:T(8,128)S(1)}, f32[2,32,256]{2,1,0:T(8,128)S(1)}, f32[2,32,256]{2,1,0:T(8,128)S(1)}, f32[2,32,256]{2,1,0:T(8,128)S(1)}) custom-call(s32[64]{0:T(128)S(1)} %copy-done.1, s32[64]{0:T(128)S(1)} %copy-done.2, s32[1]{0:T(128)S(6)} %copy.9.live_ref, bf16[64,128,128]{2,1,0:T(8,128)(2,1)S(1)} %get-tuple-element.23.tile_ref, ...), custom_call_target="tpu_custom_call" | custom-call | tf_op jit(solution)/shard_map/tiles/pallas_call | solution.py:212
  34.3 1.2 %collective-permute-start.15 = (f32[2,32,256]{2,1,0:T(8,128)S(1)}, f32[2,32,256]{2,1,0:T(8,128)S(1)}, u32[]{:S(2)}, u32[]{:S(2)}) collective-permute-start(f32[2,32,256]{2,1,0:T(8,128)S(1)} %get-tuple-element.37), channel_id=1, source_target_pairs={{0,24},{1,25},{2,26},{3,27},{4,28},{5,29},{6,30},{7,31},{8,16},{9,... | collective-permute-start | bytes 196616 | tf_op jit(solution)/shard_map/ppermute | solution.py:23
  35.5 2.0 %collective-permute-done.14.refs_2_ = f32[2,32,256]{2,1,0:T(8,128)S(1)} collective-permute-done((f32[2,32,256]{2,1,0:T(8,128)S(1)}, f32[2,32,256]{2,1,0:T(8,128)S(1)}, u32[]{:S(2)}, u32[]{:S(2)}) %collective-permute-start.14) | collective-permute-done | bytes 65568 | tf_op jit(solution)/shard_map/ppermute | solution.py:23
  37.5 1.6 %collective-permute-done.15.refs_3_ = f32[2,32,256]{2,1,0:T(8,128)S(1)} collective-permute-done((f32[2,32,256]{2,1,0:T(8,128)S(1)}, f32[2,32,256]{2,1,0:T(8,128)S(1)}, u32[]{:S(2)}, u32[]{:S(2)}) %collective-permute-start.15) | collective-permute-done | bytes 65568 | tf_op jit(solution)/shard_map/ppermute | solution.py:23
  39.6 2.8 %collective-permute-done.16.even_ref = f32[32,256]{1,0:T(8,128)S(1)} collective-permute-done((f32[32,256]{1,0:T(8,128)S(1)}, f32[32,256]{1,0:T(8,128)S(1)}, u32[]{:S(2)}, u32[]{:S(2)}) %collective-permute-start.16) | collective-permute-done | bytes 32800 | tf_op jit(solution)/shard_map/ppermute | solution.py:34
  42.4 1.4 %collective-permute-done.17.odd_ref = f32[32,256]{1,0:T(8,128)S(1)} collective-permute-done((f32[32,256]{1,0:T(8,128)S(1)}, f32[32,256]{1,0:T(8,128)S(1)}, u32[]{:S(2)}, u32[]{:S(2)}) %collective-permute-start.17) | collective-permute-done | bytes 32800 | tf_op jit(solution)/shard_map/ppermute | solution.py:34
  (26 shorter events, 3.5 us)
Async XLA Ops:
  0.6 4.7 %collective-permute-start = (bf16[32,256]{1,0:T(8,128)(2,1)}, bf16[32,256]{1,0:T(8,128)(2,1)S(1)}, u32[]{:S(2)}, u32[]{:S(2)}) collective-permute-start(bf16[32,256]{1,0:T(8,128)(2,1)} %vectors_ref.1), channel_id=1, source_target_pairs={{0,9},{1,8},{2,11},{3,10},{4,13},{5,12},{6,15},{7,14},{8,1},{9,0},... | collective-permute-start | bytes 49160 | tf_op jit(solution)/shard_map/ppermute | solution.py:34
  2.5 4.3 %collective-permute-start.1 = (bf16[32,256]{1,0:T(8,128)(2,1)}, bf16[32,256]{1,0:T(8,128)(2,1)S(1)}, u32[]{:S(2)}, u32[]{:S(2)}) collective-permute-start(bf16[32,256]{1,0:T(8,128)(2,1)} %vectors_ref.1), channel_id=1, source_target_pairs={{0,8},{1,10},{2,9},{3,12},{4,11},{5,14},{6,13},{7,15},{8,0},{9,2},... | collective-permute-start | bytes 49160 | tf_op jit(solution)/shard_map/ppermute | solution.py:34
  2.5 0.8 %copy-start = (bf16[32,256]{1,0:T(8,128)(2,1)S(1)}, bf16[32,256]{1,0:T(8,128)(2,1)}, u32[]{:S(2)}) copy-start(bf16[32,256]{1,0:T(8,128)(2,1)} %vectors_ref.1) | copy-start | bytes 49156
  3.3 8.7 %copy-start.1 = (s32[64]{0:T(128)S(1)}, s32[64]{0:T(128)}, u32[]{:S(2)}) copy-start(s32[64]{0:T(128)} %tile_row_ref.3) | copy-start | bytes 772
  3.3 8.7 %copy-start.2 = (s32[64]{0:T(128)S(1)}, s32[64]{0:T(128)}, u32[]{:S(2)}) copy-start(s32[64]{0:T(128)} %tile_offset_ref.3) | copy-start | bytes 772
  6.7 2.8 %collective-permute-start.2 = (bf16[2,32,256]{2,1,0:T(8,128)(2,1)S(1)}, bf16[2,32,256]{2,1,0:T(8,128)(2,1)S(1)}, u32[]{:S(2)}, u32[]{:S(2)}) collective-permute-start(bf16[2,32,256]{2,1,0:T(8,128)(2,1)S(1)} %select.1.refs_0_.vectors_ref), channel_id=1, source_target_pairs={{0,8},{1,9},{2,10},{3,11},{4,12},{5,13},{6,14},{7,15},{8,0},{9,1},... | collective-permute-start | bytes 98312 | tf_op jit(solution)/shard_map/ppermute | solution.py:23
  6.7 2.8 %collective-permute-start.3 = (bf16[2,32,256]{2,1,0:T(8,128)(2,1)S(1)}, bf16[2,32,256]{2,1,0:T(8,128)(2,1)S(1)}, u32[]{:S(2)}, u32[]{:S(2)}) collective-permute-start(bf16[2,32,256]{2,1,0:T(8,128)(2,1)S(1)} %select.1.refs_0_.vectors_ref), channel_id=1, source_target_pairs={{0,16},{1,17},{2,18},{3,19},{4,20},{5,21},{6,22},{7,23},{8,24},{9,... | collective-permute-start | bytes 98312 | tf_op jit(solution)/shard_map/ppermute | solution.py:23
  8.0 3.9 %collective-permute-start.4 = (bf16[2,32,256]{2,1,0:T(8,128)(2,1)S(1)}, bf16[2,32,256]{2,1,0:T(8,128)(2,1)S(1)}, u32[]{:S(2)}, u32[]{:S(2)}) collective-permute-start(bf16[2,32,256]{2,1,0:T(8,128)(2,1)S(1)} %select.1.refs_0_.vectors_ref), channel_id=1, source_target_pairs={{0,24},{1,25},{2,26},{3,27},{4,28},{5,29},{6,30},{7,31},{8,16},{9,... | collective-permute-start | bytes 98312 | tf_op jit(solution)/shard_map/ppermute | solution.py:23
  14.7 2.2 %collective-permute-start.5 = (f32[2,32,256]{2,1,0:T(8,128)S(1)}, f32[2,32,256]{2,1,0:T(8,128)S(1)}, u32[]{:S(2)}, u32[]{:S(2)}) collective-permute-start(f32[2,32,256]{2,1,0:T(8,128)S(1)} %get-tuple-element.26), channel_id=1, source_target_pairs={{0,8},{1,9},{2,10},{3,11},{4,12},{5,13},{6,14},{7,15},{8,0},{9,1},... | collective-permute-start | bytes 196616 | tf_op jit(solution)/shard_map/ppermute | solution.py:23
  15.2 3.7 %collective-permute-start.6 = (f32[2,32,256]{2,1,0:T(8,128)S(1)}, f32[2,32,256]{2,1,0:T(8,128)S(1)}, u32[]{:S(2)}, u32[]{:S(2)}) collective-permute-start(f32[2,32,256]{2,1,0:T(8,128)S(1)} %get-tuple-element.27), channel_id=1, source_target_pairs={{0,16},{1,17},{2,18},{3,19},{4,20},{5,21},{6,22},{7,23},{8,24},{9,... | collective-permute-start | bytes 196616 | tf_op jit(solution)/shard_map/ppermute | solution.py:23
  15.5 5.0 %collective-permute-start.7 = (f32[2,32,256]{2,1,0:T(8,128)S(1)}, f32[2,32,256]{2,1,0:T(8,128)S(1)}, u32[]{:S(2)}, u32[]{:S(2)}) collective-permute-start(f32[2,32,256]{2,1,0:T(8,128)S(1)} %get-tuple-element.28), channel_id=1, source_target_pairs={{0,24},{1,25},{2,26},{3,27},{4,28},{5,29},{6,30},{7,31},{8,16},{9,... | collective-permute-start | bytes 196616 | tf_op jit(solution)/shard_map/ppermute | solution.py:23
  20.5 3.4 %collective-permute-start.8 = (f32[32,256]{1,0:T(8,128)S(1)}, f32[32,256]{1,0:T(8,128)S(1)}, u32[]{:S(2)}, u32[]{:S(2)}) collective-permute-start(f32[32,256]{1,0:T(8,128)S(1)} %get-tuple-element.30), channel_id=1, source_target_pairs={{0,9},{1,8},{2,11},{3,10},{4,13},{5,12},{6,15},{7,14},{8,1},{9,0},... | collective-permute-start | bytes 98312 | tf_op jit(solution)/shard_map/ppermute | solution.py:34
  21.3 4.2 %collective-permute-start.9 = (f32[32,256]{1,0:T(8,128)S(1)}, f32[32,256]{1,0:T(8,128)S(1)}, u32[]{:S(2)}, u32[]{:S(2)}) collective-permute-start(f32[32,256]{1,0:T(8,128)S(1)} %get-tuple-element.31), channel_id=1, source_target_pairs={{0,8},{1,10},{2,9},{3,12},{4,11},{5,14},{6,13},{7,15},{8,0},{9,2},... | collective-permute-start | bytes 98312 | tf_op jit(solution)/shard_map/ppermute | solution.py:34
  25.6 2.2 %collective-permute-start.10 = (bf16[2,32,256]{2,1,0:T(8,128)(2,1)S(1)}, bf16[2,32,256]{2,1,0:T(8,128)(2,1)S(1)}, u32[]{:S(2)}, u32[]{:S(2)}) collective-permute-start(bf16[2,32,256]{2,1,0:T(8,128)(2,1)S(1)} %get-tuple-element.33.refs_0_), channel_id=1, source_target_pairs={{0,8},{1,9},{2,10},{3,11},{4,12},{5,13},{6,14},{7,15},{8,0},{9,1},... | collective-permute-start | bytes 98312 | tf_op jit(solution)/shard_map/ppermute | solution.py:23
  26.0 2.8 %collective-permute-start.11 = (bf16[2,32,256]{2,1,0:T(8,128)(2,1)S(1)}, bf16[2,32,256]{2,1,0:T(8,128)(2,1)S(1)}, u32[]{:S(2)}, u32[]{:S(2)}) collective-permute-start(bf16[2,32,256]{2,1,0:T(8,128)(2,1)S(1)} %get-tuple-element.33.refs_0_), channel_id=1, source_target_pairs={{0,16},{1,17},{2,18},{3,19},{4,20},{5,21},{6,22},{7,23},{8,24},{9,... | collective-permute-start | bytes 98312 | tf_op jit(solution)/shard_map/ppermute | solution.py:23
  26.6 4.0 %collective-permute-start.12 = (bf16[2,32,256]{2,1,0:T(8,128)(2,1)S(1)}, bf16[2,32,256]{2,1,0:T(8,128)(2,1)S(1)}, u32[]{:S(2)}, u32[]{:S(2)}) collective-permute-start(bf16[2,32,256]{2,1,0:T(8,128)(2,1)S(1)} %get-tuple-element.33.refs_0_), channel_id=1, source_target_pairs={{0,24},{1,25},{2,26},{3,27},{4,28},{5,29},{6,30},{7,31},{8,16},{9,... | collective-permute-start | bytes 98312 | tf_op jit(solution)/shard_map/ppermute | solution.py:23
  33.3 2.2 %collective-permute-start.13 = (f32[2,32,256]{2,1,0:T(8,128)S(1)}, f32[2,32,256]{2,1,0:T(8,128)S(1)}, u32[]{:S(2)}, u32[]{:S(2)}) collective-permute-start(f32[2,32,256]{2,1,0:T(8,128)S(1)} %get-tuple-element.35), channel_id=1, source_target_pairs={{0,8},{1,9},{2,10},{3,11},{4,12},{5,13},{6,14},{7,15},{8,0},{9,1},... | collective-permute-start | bytes 196616 | tf_op jit(solution)/shard_map/ppermute | solution.py:23
  33.8 3.7 %collective-permute-start.14 = (f32[2,32,256]{2,1,0:T(8,128)S(1)}, f32[2,32,256]{2,1,0:T(8,128)S(1)}, u32[]{:S(2)}, u32[]{:S(2)}) collective-permute-start(f32[2,32,256]{2,1,0:T(8,128)S(1)} %get-tuple-element.36), channel_id=1, source_target_pairs={{0,16},{1,17},{2,18},{3,19},{4,20},{5,21},{6,22},{7,23},{8,24},{9,... | collective-permute-start | bytes 196616 | tf_op jit(solution)/shard_map/ppermute | solution.py:23
  34.3 4.7 %collective-permute-start.15 = (f32[2,32,256]{2,1,0:T(8,128)S(1)}, f32[2,32,256]{2,1,0:T(8,128)S(1)}, u32[]{:S(2)}, u32[]{:S(2)}) collective-permute-start(f32[2,32,256]{2,1,0:T(8,128)S(1)} %get-tuple-element.37), channel_id=1, source_target_pairs={{0,24},{1,25},{2,26},{3,27},{4,28},{5,29},{6,30},{7,31},{8,16},{9,... | collective-permute-start | bytes 196616 | tf_op jit(solution)/shard_map/ppermute | solution.py:23
  39.0 3.4 %collective-permute-start.16 = (f32[32,256]{1,0:T(8,128)S(1)}, f32[32,256]{1,0:T(8,128)S(1)}, u32[]{:S(2)}, u32[]{:S(2)}) collective-permute-start(f32[32,256]{1,0:T(8,128)S(1)} %get-tuple-element.39), channel_id=1, source_target_pairs={{0,9},{1,8},{2,11},{3,10},{4,13},{5,12},{6,15},{7,14},{8,1},{9,0},... | collective-permute-start | bytes 98312 | tf_op jit(solution)/shard_map/ppermute | solution.py:34
  39.6 4.2 %collective-permute-start.17 = (f32[32,256]{1,0:T(8,128)S(1)}, f32[32,256]{1,0:T(8,128)S(1)}, u32[]{:S(2)}, u32[]{:S(2)}) collective-permute-start(f32[32,256]{1,0:T(8,128)S(1)} %get-tuple-element.39), channel_id=1, source_target_pairs={{0,8},{1,10},{2,9},{3,12},{4,11},{5,14},{6,13},{7,15},{8,0},{9,2},... | collective-permute-start | bytes 98312 | tf_op jit(solution)/shard_map/ppermute | solution.py:34

commit v3 on v0

v3 whole, which is shorter than its diff:
```python
import functools

import jax
import jax.numpy as jnp
from jax import lax
from jax.experimental import pallas as pl
from jax.experimental.pallas import tpu as pltpu
from jax.sharding import PartitionSpec as P

VMEM = pl.BlockSpec(memory_space=pltpu.VMEM)
SMEM = pl.BlockSpec(memory_space=pltpu.SMEM)
HBM = pl.BlockSpec(memory_space=pltpu.HBM)
AXES = ("row", "col")
F32, BF16 = jnp.float32, jnp.bfloat16


def call(kernel, name, outs, places, args, scratch=(), cost=None):
    spaces = {id(VMEM): pltpu.VMEM, id(HBM): pltpu.HBM}
    args = [
        pltpu.with_memory_space_constraint(a, spaces[id(p)]) if id(p) in spaces else a
        for a, p in zip(args, places)
    ]
    results = pl.pallas_call(
        kernel,
        out_shape=list(outs),
        in_specs=list(places),
        out_specs=[VMEM] * len(outs),
        scratch_shapes=list(scratch),
        compiler_params=pltpu.CompilerParams(vmem_limit_bytes=12 * 1024 * 1024),
        cost_estimate=cost,
        name=name,
    )(*args)
    return list(results)


def row_swap(block, distance):
    rows, cols = lax.axis_size("row"), lax.axis_size("col")
    route = [(r * cols + c, (r ^ distance) * cols + c) for r in range(rows) for c in range(cols)]
    return lax.ppermute(block, AXES, route)


def pair_swap(block, odd):
    rows, cols = lax.axis_size("row"), lax.axis_size("col")
    route = []
    for r in range(rows):
        for c in range(cols):
            other = c + 1 if c % 2 == odd else c - 1
            other = other if 0 <= other < cols else c
            route.append((r * cols + c, (r ^ 1) * cols + other))
    return lax.ppermute(block, AXES, route)


def by_parity(even_case, odd_case):
    parity = lax.rem(lax.axis_index("col"), 2)
    pl.when(parity == 0)(even_case)
    pl.when(parity == 1)(odd_case)


def load_kernel(chunk, span, blk, row_hbm, offset_hbm, vectors_hbm, tile_hbm, *refs):
    kept_ref, out_ref, flipped_ref, index_ref, row_ref, offset_ref, sems = refs
    count = tile_hbm.shape[0] // chunk
    small = [
        pltpu.make_async_copy(source, target, sems.at[count + n])
        for n, (source, target) in enumerate(
            [
                (row_hbm, row_ref),
                (offset_hbm, offset_ref),
                (vectors_hbm, kept_ref),
            ]
        )
    ]

    def copy(g):
        part = pl.ds(g * chunk, chunk)
        return pltpu.make_async_copy(tile_hbm.at[part], out_ref.at[part], sems.at[g])

    for one in small:
        one.start()
    for g in range(count):
        copy(g).start()
    for one in small:
        one.wait()
    me = lax.axis_index("row")
    i = row_ref[...]
    j = i + offset_ref[...]
    at_i = i ^ (me * blk)
    at_j = jnp.where(j < span, j ^ (me * blk), span + ((j - span) ^ ((me ^ 1) * blk)))
    index_ref[0:1] = at_i
    index_ref[1:2] = at_j
    for g in range(count):
        copy(g).wait()
        for k in range(g * chunk, (g + 1) * chunk):
            flipped_ref[k] = out_ref[k].T


def select_kernel(own_ref, even_ref, odd_ref, out_ref):
    col = lax.axis_index("col")
    size = out_ref.shape[-1]

    def split(half, value):
        for b in range(out_ref.shape[1]):
            out_ref[half, b] = value[:, b * size : (b + 1) * size]

    split(0, own_ref[...])

    def even_case():
        split(1, even_ref[...])

    def odd_case():
        inside = col < lax.axis_size("col") - 1
        split(1, jnp.where(inside, odd_ref[...], jnp.zeros_like(odd_ref)))

    by_parity(even_case, odd_case)


def tiles_kernel(slots, evens, live_ref, index_ref, tile_ref, flipped_ref, *refs):
    parts = refs[: len(slots)]
    keep_ref, send_ref, window, total = refs[len(slots) :]
    blk = keep_ref.shape[2]
    span = (window.shape[0]) // 2
    for part, wanted in zip(parts, slots):
        for half in range(2):
            for n, s in enumerate(wanted):
                for b in range(blk):
                    value = part[half, n, b] if len(part.shape) == 5 else part[half, b]
                    window[half * span + s * blk + b] = value
    total[...] = jnp.zeros_like(total)
    for k in range(tile_ref.shape[0]):
        direct = jnp.dot(window[index_ref[1, k]], flipped_ref[k], preferred_element_type=F32)
        mirrored = jnp.dot(window[index_ref[0, k]], tile_ref[k], preferred_element_type=F32)
        live = k < live_ref[0]
        total[jnp.where(live, index_ref[0, k], 2 * span)] += direct
        total[jnp.where(live, index_ref[1, k], 2 * span)] += mirrored
    for half in range(2):
        for n, s in enumerate(evens):
            for b in range(blk):
                keep_ref[half, n, b] = total[half * span + s * blk + b]
                send_ref[half, n, b] = total[half * span + (s ^ 1) * blk + b]


def add_kernel(keep_ref, got_ref, out_ref):
    out_ref[...] = keep_ref[...] + got_ref[...]


def gather_kernel(evens, own_ref, *refs):
    others, (even_ref, odd_ref, sum_ref) = refs[: len(evens) - 1], refs[len(evens) - 1 :]
    place = {s: n for n, s in enumerate(evens)}
    for n, s in enumerate(evens):
        value = own_ref[:, n]
        for other, g in zip(others, evens[1:]):
            value = value + other[:, place[s ^ g]]
        sum_ref[:, n] = value

    def even_case():
        even_ref[...] = sum_ref[1]
        odd_ref[...] = sum_ref[0]

    def odd_case():
        even_ref[...] = sum_ref[0]
        odd_ref[...] = sum_ref[1]

    by_parity(even_case, odd_case)


def first_kernel(evens, center_ref, radius_ref, sum_ref, even_ref, odd_ref, *refs):
    parts, out_ref = refs[:-1], refs[-1]
    col = lax.axis_index("col")
    center, radius = center_ref[0], radius_ref[0]

    def degree(image, vectors):
        return ((image - center * vectors.astype(F32)) / radius).astype(BF16)

    def both(from_previous, from_next):
        inside = col < lax.axis_size("col") - 1
        for n in range(len(evens)):
            arrived = jnp.where(col > 0, from_previous[n], 0.0)
            out_ref[0, n] = degree(sum_ref[0, n] + arrived, parts[n][0])
            beyond = degree(sum_ref[1, n] + from_next[n], parts[n][1])
            out_ref[1, n] = jnp.where(inside, beyond, jnp.zeros_like(beyond))

    by_parity(lambda: both(odd_ref, even_ref), lambda: both(even_ref, odd_ref))


def spread_kernel(keep_ref, got_ref, *outs):
    for n, out_ref in enumerate(outs):
        out_ref[...] = keep_ref[:, n] + got_ref[:, n]


def owner_kernel(count, *refs):
    parts, (low_ref, up_ref) = refs[:count], refs[count:]
    low, up = parts[0][0], parts[0][1]
    for part in parts[1:]:
        low, up = low + part[0], up + part[1]
    low_ref[...] = low
    up_ref[...] = up


def second_kernel(center_ref, radius_ref, pair_ref, first_ref, low_ref, even_ref, odd_ref, out_ref, first_out_ref):
    col = lax.axis_index("col")
    center, radius = center_ref[0], radius_ref[0]
    size = low_ref.shape[-1]

    def finish(from_previous):
        for b in range(low_ref.shape[0]):
            image = low_ref[b] + jnp.where(col > 0, from_previous[b], 0.0)
            first = first_ref[0, 0, b].astype(F32)
            second = 2.0 * (image - center * first) / radius - pair_ref[0, b].astype(F32)
            out_ref[:, b * size : (b + 1) * size] = second

    for b in range(low_ref.shape[0]):
        first_out_ref[:, b * size : (b + 1) * size] = first_ref[0, 0, b]
    by_parity(lambda: finish(odd_ref), lambda: finish(even_ref))


def local(vectors, tile_data, tile_row, tile_offset, tile_live, damp_center, damp_radius):
    rows = lax.axis_size("row")
    count, width = vectors.shape
    tiles, size, _ = tile_data.shape
    blk = width // size
    span = rows * blk
    evens = [s for s in range(rows) if bin(s).count("1") % 2 == 0]
    members = len(evens)

    def shape(dtype, *lead):
        return pltpu.VMEM((*lead, count, size), dtype)

    sent = pair_swap(vectors, 0), pair_swap(vectors, 1)
    kept = pltpu.VMEM(tile_data.shape, BF16)
    chunk = 8
    vectors, tile_data, flipped, index = call(
        functools.partial(load_kernel, chunk, span, blk),
        "load",
        [pltpu.VMEM(vectors.shape, BF16), kept, kept, pltpu.VMEM((2, tiles), jnp.int32)],
        [HBM] * 4,
        [tile_row.reshape(1, tiles), tile_offset.reshape(1, tiles), vectors, tile_data],
        scratch=[
            pltpu.VMEM((1, tiles), jnp.int32),
            pltpu.VMEM((1, tiles), jnp.int32),
            pltpu.SemaphoreType.DMA((tiles // chunk + 3,)),
        ],
        cost=pl.CostEstimate(flops=0, bytes_accessed=6 * tile_data.size, transcendentals=0),
    )

    def apply(parts, slots):
        index_near = pltpu.with_memory_space_constraint(index, pltpu.VMEM)
        keep, send = call(
            functools.partial(tiles_kernel, slots, evens),
            "tiles",
            [shape(F32, 2, members, blk)] * 2,
            [SMEM] * 2 + [VMEM] * (2 + len(parts)),
            [tile_live, index_near, tile_data, flipped, *parts],
            scratch=[
                pltpu.VMEM((2 * span, count, size), BF16),
                pltpu.VMEM((2 * span + 1, count, size), F32),
            ],
        )
        return keep, row_swap(send, 1)

    (pair,) = call(select_kernel, "select", [shape(BF16, 2, blk)], [VMEM] * 3, [vectors, *sent])
    gathered = [pair] + [row_swap(pair, s) for s in range(1, rows)]
    keep, got = apply(gathered, [[s] for s in range(rows)])
    (paired,) = call(add_kernel, "add", [shape(F32, 2, members, blk)], [VMEM] * 2, [keep, got])
    even, odd, total = call(
        functools.partial(gather_kernel, evens),
        "gather",
        [shape(F32, members, blk)] * 2 + [shape(F32, 2, members, blk)],
        [VMEM] * members,
        [paired] + [row_swap(paired, g) for g in evens[1:]],
    )
    (first,) = call(
        functools.partial(first_kernel, evens),
        "first",
        [shape(BF16, 2, members, blk)],
        [SMEM] * 2 + [VMEM] * (3 + members),
        [damp_center, damp_radius, total, pair_swap(even, 0), pair_swap(odd, 1)]
        + [gathered[s] for s in evens],
    )
    keep, got = apply([first, row_swap(first, 1)], [evens, [s ^ 1 for s in evens]])
    pieces = call(spread_kernel, "spread", [shape(F32, 2, blk)] * members, [VMEM] * 2, [keep, got])
    pieces = pieces[:1] + [row_swap(p, g) for p, g in zip(pieces[1:], evens[1:])]
    low, up = call(
        functools.partial(owner_kernel, members), "owner", [shape(F32, blk)] * 2, [VMEM] * members, pieces
    )
    second, first = call(
        second_kernel,
        "second",
        [jax.ShapeDtypeStruct((count, width), F32), jax.ShapeDtypeStruct((count, width), BF16)],
        [SMEM] * 2 + [VMEM] * 5,
        [damp_center, damp_radius, pair, first, low, pair_swap(up, 0), pair_swap(up, 1)],
    )
    return first, second


def solution(mesh):
    placed = (
        P(None, ("col", "row")),
        P(("col", "row"), None, None),
        P(("col", "row")),
        P(("col", "row")),
        P(("col", "row")),
        P(),
        P(),
    )
    return jax.shard_map(
        local,
        mesh=mesh,
        in_specs=placed,
        out_specs=(P(None, ("col", "row")), P(None, ("col", "row"))),
        check_vma=False,
    )
```

time: 109 us -> 41.4 us (0.38)
  the two profiles are of different devices: /device:TPU:0 before, /device:TPU:9 now
where the time goes in v3:
time: 41.4 us; the launch traced here: 41.3 us
  waiting for transfers between devices  23.2 us (56%)
  starting transfers between devices  8.85 us (21%)
  Pallas kernels  6.6 us (16%)
  between operations  2.64 us (6%)
    ppermute x8, waiting for transfers between devices, row_swap(): return lax.ppermute(block, AXES, route)  13.3 us
    ppermute x6, waiting for transfers between devices, pair_swap(): return lax.ppermute(block, AXES, route)  9.87 us
    pallas_call x10, Pallas kernels, call(): pl.pallas_call(kernel, out_shape=list(outs), in_specs=list(places), out_s...  6.6 us
    ppermute x8, starting transfers between devices, row_swap(): return lax.ppermute(block, AXES, route)  5.05 us
    ppermute x6, starting transfers between devices, pair_swap(): return lax.ppermute(block, AXES, route)  3.8 us
  transfers between devices with their start and end apart: 14, of which 12 were waited for; matrix products, arithmetic and copies ran while one was open for 0% of the time, Pallas kernels for 5%

profile of v3, /device:TPU:9, one launch (start us, length us, event | category | flops | bytes accessed | tf_op | source)
XLA Modules:
  0.0 41.3 jit_solution(11482969946064213061)
XLA Ops:
  0.6 1.8 %collective-permute-start = (bf16[32,256]{1,0:T(8,128)(2,1)}, bf16[32,256]{1,0:T(8,128)(2,1)S(1)}, u32[]{:S(2)}, u32[]{:S(2)}) collective-permute-start(bf16[32,256]{1,0:T(8,128)(2,1)} %vectors_hbm.1), channel_id=1, source_target_pairs={{0,9},{1,8},{2,11},{3,10},{4,13},{5,12},{6,15},{7,14},{8,1},{9,0},... | collective-permute-start | bytes 49160 | tf_op jit(solution)/shard_map/ppermute | solution.py:50
  2.5 2.1 %load.1 = (bf16[32,256]{1,0:T(8,128)(2,1)S(1)}, bf16[64,128,128]{2,1,0:T(8,128)(2,1)S(1)}, bf16[64,128,128]{2,1,0:T(8,128)(2,1)S(1)}, s32[2,64]{1,0:T(2,128)S(1)}) custom-call(s32[1,64]{1,0:T(1,128)} %bitcast.2, s32[1,64]{1,0:T(1,128)} %bitcast.3, bf16[32,256]{1,0:T(8,128)(2,1)} %vectors_hbm.1, bf16[64,128,128]{2,1,0:T(8,128)(2,1)} %tile_hbm.1), custom_call_target="tpu_custom_call" | custom-call | bytes 6291456 | tf_op jit(solution)/shard_map/load/pallas_call | solution.py:23
  4.6 2.2 %collective-permute-done.1.odd_ref = bf16[32,256]{1,0:T(8,128)(2,1)S(1)} collective-permute-done((bf16[32,256]{1,0:T(8,128)(2,1)}, bf16[32,256]{1,0:T(8,128)(2,1)S(1)}, u32[]{:S(2)}, u32[]{:S(2)}) %collective-permute-start.1) | collective-permute-done | bytes 16416 | tf_op jit(solution)/shard_map/ppermute | solution.py:50
  6.7 1.0 %collective-permute-start.4 = (bf16[2,2,32,128]{3,2,1,0:T(8,128)(2,1)S(1)}, bf16[2,2,32,128]{3,2,1,0:T(8,128)(2,1)S(1)}, u32[]{:S(2)}, u32[]{:S(2)}) collective-permute-start(bf16[2,2,32,128]{3,2,1,0:T(8,128)(2,1)S(1)} %select.1.refs_0_.pair_ref), channel_id=1, source_target_pairs={{0,24},{1,25},{2,26},{3,27},{4,28},{5,29},{6,30},{7,31},{8,16},{9,... | collective-permute-start | bytes 98312 | tf_op jit(solution)/shard_map/ppermute | solution.py:39
  7.7 0.7 %collective-permute-start.2 = (bf16[2,2,32,128]{3,2,1,0:T(8,128)(2,1)S(1)}, bf16[2,2,32,128]{3,2,1,0:T(8,128)(2,1)S(1)}, u32[]{:S(2)}, u32[]{:S(2)}) collective-permute-start(bf16[2,2,32,128]{3,2,1,0:T(8,128)(2,1)S(1)} %select.1.refs_0_.pair_ref), channel_id=1, source_target_pairs={{0,8},{1,9},{2,10},{3,11},{4,12},{5,13},{6,14},{7,15},{8,0},{9,1},... | collective-permute-start | bytes 98312 | tf_op jit(solution)/shard_map/ppermute | solution.py:39
  9.3 0.8 %collective-permute-done.4.refs_3_.refs_1_ = bf16[2,2,32,128]{3,2,1,0:T(8,128)(2,1)S(1)} collective-permute-done((bf16[2,2,32,128]{3,2,1,0:T(8,128)(2,1)S(1)}, bf16[2,2,32,128]{3,2,1,0:T(8,128)(2,1)S(1)}, u32[]{:S(2)}, u32[]{:S(2)}) %collective-permute-start.4) | collective-permute-done | bytes 32800 | tf_op jit(solution)/shard_map/ppermute | solution.py:39
  10.1 1.1 %collective-permute-done.3.refs_2_ = bf16[2,2,32,128]{3,2,1,0:T(8,128)(2,1)S(1)} collective-permute-done((bf16[2,2,32,128]{3,2,1,0:T(8,128)(2,1)S(1)}, bf16[2,2,32,128]{3,2,1,0:T(8,128)(2,1)S(1)}, u32[]{:S(2)}, u32[]{:S(2)}) %collective-permute-start.3) | collective-permute-done | bytes 32800 | tf_op jit(solution)/shard_map/ppermute | solution.py:39
  11.1 1.9 %tiles.2 = (f32[2,2,2,32,128]{4,3,2,1,0:T(8,128)S(1)}, f32[2,2,2,32,128]{4,3,2,1,0:T(8,128)S(1)}) custom-call(s32[1]{0:T(128)S(6)} %copy.9.live_ref, s32[2,64]{1,0:T(2,128)S(1)} %get-tuple-element.20.index_ref, bf16[64,128,128]{2,1,0:T(8,128)(2,1)S(1)} %get-tuple-element.21.tile_ref, bf16[64,128,128]{2,1,0:T(8,128)(2,1)S(1)} %get-tuple-element.22.flipped_ref, ...), custom_call_target="tpu_custom_call" | custom-call | tf_op jit(solution)/shard_map/tiles/pallas_call | solution.py:23
  13.0 1.3 %collective-permute-start.5 = (f32[2,2,2,32,128]{4,3,2,1,0:T(8,128)S(1)}, f32[2,2,2,32,128]{4,3,2,1,0:T(8,128)S(1)}, u32[]{:S(2)}, u32[]{:S(2)}) collective-permute-start(f32[2,2,2,32,128]{4,3,2,1,0:T(8,128)S(1)} %get-tuple-element.24), channel_id=1, source_target_pairs={{0,8},{1,9},{2,10},{3,11},{4,12},{5,13},{6,14},{7,15},{8,0},{9,1},... | collective-permute-start | bytes 393224 | tf_op jit(solution)/shard_map/ppermute | solution.py:39
  14.3 1.0 %collective-permute-done.5.got_ref = f32[2,2,2,32,128]{4,3,2,1,0:T(8,128)S(1)} collective-permute-done((f32[2,2,2,32,128]{4,3,2,1,0:T(8,128)S(1)}, f32[2,2,2,32,128]{4,3,2,1,0:T(8,128)S(1)}, u32[]{:S(2)}, u32[]{:S(2)}) %collective-permute-start.5) | collective-permute-done | bytes 131104 | tf_op jit(solution)/shard_map/ppermute | solution.py:39
  15.3 0.7 %collective-permute-start.6 = (f32[2,2,2,32,128]{4,3,2,1,0:T(8,128)S(1)}, f32[2,2,2,32,128]{4,3,2,1,0:T(8,128)S(1)}, u32[]{:S(2)}, u32[]{:S(2)}) collective-permute-start(f32[2,2,2,32,128]{4,3,2,1,0:T(8,128)S(1)} %add.1.own_ref), channel_id=1, source_target_pairs={{0,24},{1,25},{2,26},{3,27},{4,28},{5,29},{6,30},{7,31},{8,16},{9,... | collective-permute-start | bytes 393224 | tf_op jit(solution)/shard_map/ppermute | solution.py:39
  16.1 4.8 %collective-permute-done.6.refs_0_ = f32[2,2,2,32,128]{4,3,2,1,0:T(8,128)S(1)} collective-permute-done((f32[2,2,2,32,128]{4,3,2,1,0:T(8,128)S(1)}, f32[2,2,2,32,128]{4,3,2,1,0:T(8,128)S(1)}, u32[]{:S(2)}, u32[]{:S(2)}) %collective-permute-start.6) | collective-permute-done | bytes 131104 | tf_op jit(solution)/shard_map/ppermute | solution.py:39
  20.9 1.0 %collective-permute-start.7 = (f32[2,2,32,128]{3,2,1,0:T(8,128)S(1)}, f32[2,2,32,128]{3,2,1,0:T(8,128)S(1)}, u32[]{:S(2)}, u32[]{:S(2)}) collective-permute-start(f32[2,2,32,128]{3,2,1,0:T(8,128)S(1)} %get-tuple-element.26), channel_id=1, source_target_pairs={{0,9},{1,8},{2,11},{3,10},{4,13},{5,12},{6,15},{7,14},{8,1},{9,0},... | collective-permute-start | bytes 196616 | tf_op jit(solution)/shard_map/ppermute | solution.py:50
  23.3 1.8 %collective-permute-done.7.even_ref = f32[2,2,32,128]{3,2,1,0:T(8,128)S(1)} collective-permute-done((f32[2,2,32,128]{3,2,1,0:T(8,128)S(1)}, f32[2,2,32,128]{3,2,1,0:T(8,128)S(1)}, u32[]{:S(2)}, u32[]{:S(2)}) %collective-permute-start.7) | collective-permute-done | bytes 65568 | tf_op jit(solution)/shard_map/ppermute | solution.py:50
  25.0 1.7 %collective-permute-done.8.odd_ref = f32[2,2,32,128]{3,2,1,0:T(8,128)S(1)} collective-permute-done((f32[2,2,32,128]{3,2,1,0:T(8,128)S(1)}, f32[2,2,32,128]{3,2,1,0:T(8,128)S(1)}, u32[]{:S(2)}, u32[]{:S(2)}) %collective-permute-start.8) | collective-permute-done | bytes 65568 | tf_op jit(solution)/shard_map/ppermute | solution.py:50
  27.1 1.0 %collective-permute-done.9.refs_1_ = bf16[2,2,2,32,128]{4,3,2,1,0:T(8,128)(2,1)S(1)} collective-permute-done((bf16[2,2,2,32,128]{4,3,2,1,0:T(8,128)(2,1)S(1)}, bf16[2,2,2,32,128]{4,3,2,1,0:T(8,128)(2,1)S(1)}, u32[]{:S(2)}, u32[]{:S(2)}) %collective-permute-start.9) | collective-permute-done | bytes 65568 | tf_op jit(solution)/shard_map/ppermute | solution.py:39
  28.1 1.9 %tiles.3 = (f32[2,2,2,32,128]{4,3,2,1,0:T(8,128)S(1)}, f32[2,2,2,32,128]{4,3,2,1,0:T(8,128)S(1)}) custom-call(s32[1]{0:T(128)S(6)} %copy.9.live_ref, s32[2,64]{1,0:T(2,128)S(1)} %get-tuple-element.20.index_ref, bf16[64,128,128]{2,1,0:T(8,128)(2,1)S(1)} %get-tuple-element.21.tile_ref, bf16[64,128,128]{2,1,0:T(8,128)(2,1)S(1)} %get-tuple-element.22.flipped_ref, ...), custom_call_target="tpu_custom_call" | custom-call | tf_op jit(solution)/shard_map/tiles/pallas_call | solution.py:23
  30.3 1.1 %collective-permute-done.10.got_ref = f32[2,2,2,32,128]{4,3,2,1,0:T(8,128)S(1)} collective-permute-done((f32[2,2,2,32,128]{4,3,2,1,0:T(8,128)S(1)}, f32[2,2,2,32,128]{4,3,2,1,0:T(8,128)S(1)}, u32[]{:S(2)}, u32[]{:S(2)}) %collective-permute-start.10) | collective-permute-done | bytes 131104 | tf_op jit(solution)/shard_map/ppermute | solution.py:39
  31.4 0.5 %collective-permute-start.11 = (f32[2,2,32,128]{3,2,1,0:T(8,128)S(1)}, f32[2,2,32,128]{3,2,1,0:T(8,128)S(1)}, u32[]{:S(2)}, u32[]{:S(2)}) collective-permute-start(f32[2,2,32,128]{3,2,1,0:T(8,128)S(1)} %get-tuple-element.31), channel_id=1, source_target_pairs={{0,24},{1,25},{2,26},{3,27},{4,28},{5,29},{6,30},{7,31},{8,16},{9,... | collective-permute-start | bytes 196616 | tf_op jit(solution)/shard_map/ppermute | solution.py:39
  31.9 3.5 %collective-permute-done.11.refs_1_ = f32[2,2,32,128]{3,2,1,0:T(8,128)S(1)} collective-permute-done((f32[2,2,32,128]{3,2,1,0:T(8,128)S(1)}, f32[2,2,32,128]{3,2,1,0:T(8,128)S(1)}, u32[]{:S(2)}, u32[]{:S(2)}) %collective-permute-start.11) | collective-permute-done | bytes 65568 | tf_op jit(solution)/shard_map/ppermute | solution.py:39
  35.5 0.9 %collective-permute-start.12 = (f32[2,32,128]{2,1,0:T(8,128)S(1)}, f32[2,32,128]{2,1,0:T(8,128)S(1)}, u32[]{:S(2)}, u32[]{:S(2)}) collective-permute-start(f32[2,32,128]{2,1,0:T(8,128)S(1)} %get-tuple-element.33), channel_id=1, source_target_pairs={{0,9},{1,8},{2,11},{3,10},{4,13},{5,12},{6,15},{7,14},{8,1},{9,0},... | collective-permute-start | bytes 98312 | tf_op jit(solution)/shard_map/ppermute | solution.py:50
  36.4 2.5 %collective-permute-done.12.even_ref = f32[2,32,128]{2,1,0:T(8,128)S(1)} collective-permute-done((f32[2,32,128]{2,1,0:T(8,128)S(1)}, f32[2,32,128]{2,1,0:T(8,128)S(1)}, u32[]{:S(2)}, u32[]{:S(2)}) %collective-permute-start.12) | collective-permute-done | bytes 32800 | tf_op jit(solution)/shard_map/ppermute | solution.py:50
  38.9 1.7 %collective-permute-done.13.odd_ref = f32[2,32,128]{2,1,0:T(8,128)S(1)} collective-permute-done((f32[2,32,128]{2,1,0:T(8,128)S(1)}, f32[2,32,128]{2,1,0:T(8,128)S(1)}, u32[]{:S(2)}, u32[]{:S(2)}) %collective-permute-start.13) | collective-permute-done | bytes 32800 | tf_op jit(solution)/shard_map/ppermute | solution.py:50
  40.6 0.6 %second.1 = (f32[32,256]{1,0:T(8,128)}, bf16[32,256]{1,0:T(8,128)(2,1)}) custom-call(f32[1]{0:T(128)S(6)} %copy.10.center_ref, f32[1]{0:T(128)S(6)} %copy.11.radius_ref, bf16[2,2,32,128]{3,2,1,0:T(8,128)(2,1)S(1)} %select.1.refs_0_.pair_ref, bf16[2,2,2,32,128]{4,3,2,1,0:T(8,128)(2,1)S(1)} %first.1.refs_0_.first_ref, ...), custom_call_target="tpu_custom_call" | custom-call | tf_op jit(solution)/shard_map/second/pallas_call | solution.py:23
  (14 shorter events, 1.0 us)
Async XLA Ops:
  0.6 3.9 %collective-permute-start = (bf16[32,256]{1,0:T(8,128)(2,1)}, bf16[32,256]{1,0:T(8,128)(2,1)S(1)}, u32[]{:S(2)}, u32[]{:S(2)}) collective-permute-start(bf16[32,256]{1,0:T(8,128)(2,1)} %vectors_hbm.1), channel_id=1, source_target_pairs={{0,9},{1,8},{2,11},{3,10},{4,13},{5,12},{6,15},{7,14},{8,1},{9,0},... | collective-permute-start | bytes 49160 | tf_op jit(solution)/shard_map/ppermute | solution.py:50
  2.5 4.3 %collective-permute-start.1 = (bf16[32,256]{1,0:T(8,128)(2,1)}, bf16[32,256]{1,0:T(8,128)(2,1)S(1)}, u32[]{:S(2)}, u32[]{:S(2)}) collective-permute-start(bf16[32,256]{1,0:T(8,128)(2,1)} %vectors_hbm.1), channel_id=1, source_target_pairs={{0,8},{1,10},{2,9},{3,12},{4,11},{5,14},{6,13},{7,15},{8,0},{9,2},... | collective-permute-start | bytes 49160 | tf_op jit(solution)/shard_map/ppermute | solution.py:50
  6.7 3.3 %collective-permute-start.4 = (bf16[2,2,32,128]{3,2,1,0:T(8,128)(2,1)S(1)}, bf16[2,2,32,128]{3,2,1,0:T(8,128)(2,1)S(1)}, u32[]{:S(2)}, u32[]{:S(2)}) collective-permute-start(bf16[2,2,32,128]{3,2,1,0:T(8,128)(2,1)S(1)} %select.1.refs_0_.pair_ref), channel_id=1, source_target_pairs={{0,24},{1,25},{2,26},{3,27},{4,28},{5,29},{6,30},{7,31},{8,16},{9,... | collective-permute-start | bytes 98312 | tf_op jit(solution)/shard_map/ppermute | solution.py:39
  7.7 2.4 %collective-permute-start.2 = (bf16[2,2,32,128]{3,2,1,0:T(8,128)(2,1)S(1)}, bf16[2,2,32,128]{3,2,1,0:T(8,128)(2,1)S(1)}, u32[]{:S(2)}, u32[]{:S(2)}) collective-permute-start(bf16[2,2,32,128]{3,2,1,0:T(8,128)(2,1)S(1)} %select.1.refs_0_.pair_ref), channel_id=1, source_target_pairs={{0,8},{1,9},{2,10},{3,11},{4,12},{5,13},{6,14},{7,15},{8,0},{9,1},... | collective-permute-start | bytes 98312 | tf_op jit(solution)/shard_map/ppermute | solution.py:39
  8.4 2.8 %collective-permute-start.3 = (bf16[2,2,32,128]{3,2,1,0:T(8,128)(2,1)S(1)}, bf16[2,2,32,128]{3,2,1,0:T(8,128)(2,1)S(1)}, u32[]{:S(2)}, u32[]{:S(2)}) collective-permute-start(bf16[2,2,32,128]{3,2,1,0:T(8,128)(2,1)S(1)} %select.1.refs_0_.pair_ref), channel_id=1, source_target_pairs={{0,16},{1,17},{2,18},{3,19},{4,20},{5,21},{6,22},{7,23},{8,24},{9,... | collective-permute-start | bytes 98312 | tf_op jit(solution)/shard_map/ppermute | solution.py:39
  13.0 2.3 %collective-permute-start.5 = (f32[2,2,2,32,128]{4,3,2,1,0:T(8,128)S(1)}, f32[2,2,2,32,128]{4,3,2,1,0:T(8,128)S(1)}, u32[]{:S(2)}, u32[]{:S(2)}) collective-permute-start(f32[2,2,2,32,128]{4,3,2,1,0:T(8,128)S(1)} %get-tuple-element.24), channel_id=1, source_target_pairs={{0,8},{1,9},{2,10},{3,11},{4,12},{5,13},{6,14},{7,15},{8,0},{9,1},... | collective-permute-start | bytes 393224 | tf_op jit(solution)/shard_map/ppermute | solution.py:39
  15.3 5.5 %collective-permute-start.6 = (f32[2,2,2,32,128]{4,3,2,1,0:T(8,128)S(1)}, f32[2,2,2,32,128]{4,3,2,1,0:T(8,128)S(1)}, u32[]{:S(2)}, u32[]{:S(2)}) collective-permute-start(f32[2,2,2,32,128]{4,3,2,1,0:T(8,128)S(1)} %add.1.own_ref), channel_id=1, source_target_pairs={{0,24},{1,25},{2,26},{3,27},{4,28},{5,29},{6,30},{7,31},{8,16},{9,... | collective-permute-start | bytes 393224 | tf_op jit(solution)/shard_map/ppermute | solution.py:39
  20.9 4.1 %collective-permute-start.7 = (f32[2,2,32,128]{3,2,1,0:T(8,128)S(1)}, f32[2,2,32,128]{3,2,1,0:T(8,128)S(1)}, u32[]{:S(2)}, u32[]{:S(2)}) collective-permute-start(f32[2,2,32,128]{3,2,1,0:T(8,128)S(1)} %get-tuple-element.26), channel_id=1, source_target_pairs={{0,9},{1,8},{2,11},{3,10},{4,13},{5,12},{6,15},{7,14},{8,1},{9,0},... | collective-permute-start | bytes 196616 | tf_op jit(solution)/shard_map/ppermute | solution.py:50
  21.9 4.8 %collective-permute-start.8 = (f32[2,2,32,128]{3,2,1,0:T(8,128)S(1)}, f32[2,2,32,128]{3,2,1,0:T(8,128)S(1)}, u32[]{:S(2)}, u32[]{:S(2)}) collective-permute-start(f32[2,2,32,128]{3,2,1,0:T(8,128)S(1)} %get-tuple-element.27), channel_id=1, source_target_pairs={{0,8},{1,10},{2,9},{3,12},{4,11},{5,14},{6,13},{7,15},{8,0},{9,2},... | collective-permute-start | bytes 196616 | tf_op jit(solution)/shard_map/ppermute | solution.py:50
  26.8 1.3 %collective-permute-start.9 = (bf16[2,2,2,32,128]{4,3,2,1,0:T(8,128)(2,1)S(1)}, bf16[2,2,2,32,128]{4,3,2,1,0:T(8,128)(2,1)S(1)}, u32[]{:S(2)}, u32[]{:S(2)}) collective-permute-start(bf16[2,2,2,32,128]{4,3,2,1,0:T(8,128)(2,1)S(1)} %first.1.refs_0_.first_ref), channel_id=1, source_target_pairs={{0,8},{1,9},{2,10},{3,11},{4,12},{5,13},{6,14},{7,15},{8,0},{9,1},... | collective-permute-start | bytes 196616 | tf_op jit(solution)/shard_map/ppermute | solution.py:39
  30.0 1.4 %collective-permute-start.10 = (f32[2,2,2,32,128]{4,3,2,1,0:T(8,128)S(1)}, f32[2,2,2,32,128]{4,3,2,1,0:T(8,128)S(1)}, u32[]{:S(2)}, u32[]{:S(2)}) collective-permute-start(f32[2,2,2,32,128]{4,3,2,1,0:T(8,128)S(1)} %get-tuple-element.29), channel_id=1, source_target_pairs={{0,8},{1,9},{2,10},{3,11},{4,12},{5,13},{6,14},{7,15},{8,0},{9,1},... | collective-permute-start | bytes 393224 | tf_op jit(solution)/shard_map/ppermute | solution.py:39
  31.4 4.1 %collective-permute-start.11 = (f32[2,2,32,128]{3,2,1,0:T(8,128)S(1)}, f32[2,2,32,128]{3,2,1,0:T(8,128)S(1)}, u32[]{:S(2)}, u32[]{:S(2)}) collective-permute-start(f32[2,2,32,128]{3,2,1,0:T(8,128)S(1)} %get-tuple-element.31), channel_id=1, source_target_pairs={{0,24},{1,25},{2,26},{3,27},{4,28},{5,29},{6,30},{7,31},{8,16},{9,... | collective-permute-start | bytes 196616 | tf_op jit(solution)/shard_map/ppermute | solution.py:39
  35.5 3.4 %collective-permute-start.12 = (f32[2,32,128]{2,1,0:T(8,128)S(1)}, f32[2,32,128]{2,1,0:T(8,128)S(1)}, u32[]{:S(2)}, u32[]{:S(2)}) collective-permute-start(f32[2,32,128]{2,1,0:T(8,128)S(1)} %get-tuple-element.33), channel_id=1, source_target_pairs={{0,9},{1,8},{2,11},{3,10},{4,13},{5,12},{6,15},{7,14},{8,1},{9,0},... | collective-permute-start | bytes 98312 | tf_op jit(solution)/shard_map/ppermute | solution.py:50
  36.4 4.2 %collective-permute-start.13 = (f32[2,32,128]{2,1,0:T(8,128)S(1)}, f32[2,32,128]{2,1,0:T(8,128)S(1)}, u32[]{:S(2)}, u32[]{:S(2)}) collective-permute-start(f32[2,32,128]{2,1,0:T(8,128)S(1)} %get-tuple-element.33), channel_id=1, source_target_pairs={{0,8},{1,10},{2,9},{3,12},{4,11},{5,14},{6,13},{7,15},{8,0},{9,2},... | collective-permute-start | bytes 98312 | tf_op jit(solution)/shard_map/ppermute | solution.py:50

commit v4 on v3

v4 whole, which is shorter than its diff:
```python
import functools

import jax
import jax.numpy as jnp
from jax import lax
from jax.experimental import pallas as pl
from jax.experimental.pallas import tpu as pltpu
from jax.sharding import PartitionSpec as P

VMEM = pl.BlockSpec(memory_space=pltpu.VMEM)
SMEM = pl.BlockSpec(memory_space=pltpu.SMEM)
HBM = pl.BlockSpec(memory_space=pltpu.HBM)
AXES = ("row", "col")
F32, BF16 = jnp.float32, jnp.bfloat16


def call(kernel, name, outs, places, args, scratch=(), cost=None):
    spaces = {id(VMEM): pltpu.VMEM, id(HBM): pltpu.HBM}
    args = [
        pltpu.with_memory_space_constraint(a, spaces[id(p)]) if id(p) in spaces else a
        for a, p in zip(args, places)
    ]
    results = pl.pallas_call(
        kernel,
        out_shape=list(outs),
        in_specs=list(places),
        out_specs=[SMEM if getattr(o, "memory_space", None) == pltpu.SMEM else VMEM for o in outs],
        scratch_shapes=list(scratch),
        compiler_params=pltpu.CompilerParams(vmem_limit_bytes=12 * 1024 * 1024),
        cost_estimate=cost,
        name=name,
    )(*args)
    return list(results)


def row_swap(block, distance):
    rows, cols = lax.axis_size("row"), lax.axis_size("col")
    route = [(r * cols + c, (r ^ distance) * cols + c) for r in range(rows) for c in range(cols)]
    return lax.ppermute(block, AXES, route)


def pair_swap(block, odd):
    rows, cols = lax.axis_size("row"), lax.axis_size("col")
    route = []
    for r in range(rows):
        for c in range(cols):
            other = c + 1 if c % 2 == odd else c - 1
            other = other if 0 <= other < cols else c
            route.append((r * cols + c, (r ^ 1) * cols + other))
    return lax.ppermute(block, AXES, route)


def by_parity(even_case, odd_case):
    parity = lax.rem(lax.axis_index("col"), 2)
    pl.when(parity == 0)(even_case)
    pl.when(parity == 1)(odd_case)


def load_kernel(chunk, span, blk, row_hbm, offset_hbm, vectors_hbm, tile_hbm, *refs):
    kept_ref, out_ref, flipped_ref, index_ref, row_ref, offset_ref, sems = refs
    count = tile_hbm.shape[0] // chunk
    small = [
        pltpu.make_async_copy(source, target, sems.at[count + n])
        for n, (source, target) in enumerate(
            [
                (row_hbm, row_ref),
                (offset_hbm, offset_ref),
                (vectors_hbm, kept_ref),
            ]
        )
    ]

    def copy(g):
        part = pl.ds(g * chunk, chunk)
        return pltpu.make_async_copy(tile_hbm.at[part], out_ref.at[part], sems.at[g])

    for one in small:
        one.start()
    for g in range(count):
        copy(g).start()
    for one in small:
        one.wait()
    me = lax.axis_index("row")
    for k in range(tile_hbm.shape[0]):
        i = row_ref[0, k]
        j = i + offset_ref[0, k]
        index_ref[0, k] = i ^ (me * blk)
        index_ref[1, k] = jnp.where(j < span, j ^ (me * blk), span + ((j - span) ^ ((me ^ 1) * blk)))
    for g in range(count):
        copy(g).wait()
        for k in range(g * chunk, (g + 1) * chunk):
            flipped_ref[k] = out_ref[k].T


def select_kernel(own_ref, even_ref, odd_ref, out_ref):
    col = lax.axis_index("col")
    size = out_ref.shape[-1]

    def lay(half, value):
        for b in range(out_ref.shape[1]):
            out_ref[half, b] = value[:, b * size : (b + 1) * size]

    lay(0, own_ref[...])

    def even_case():
        lay(1, even_ref[...])

    def odd_case():
        inside = col < lax.axis_size("col") - 1
        lay(1, jnp.where(inside, odd_ref[...], jnp.zeros_like(odd_ref)))

    by_parity(even_case, odd_case)


def fill(window, half, parts, slots):
    for part, wanted in zip(parts, slots):
        for n, s in enumerate(wanted):
            blk = part.shape[-3]
            for b in range(blk):
                value = part[half, n, b] if len(part.shape) == 5 else part[half, b]
                window[s * blk + b] = value


def split(total, first, evens, keep_ref, send_ref):
    blk = keep_ref.shape[1]
    for n, s in enumerate(evens):
        for b in range(blk):
            keep_ref[n, b] = total[first + s * blk + b]
            send_ref[n, b] = total[first + (s ^ 1) * blk + b]


def mirror_kernel(slots, evens, live_ref, index_ref, tile_ref, *refs):
    parts = refs[: len(slots)]
    keep_ref, send_ref, low_ref, window, total = refs[len(slots) :]
    span = window.shape[0]
    fill(window, 0, parts, slots)
    total[...] = jnp.zeros_like(total)
    for k in range(tile_ref.shape[0]):
        mirrored = jnp.dot(window[index_ref[0, k]], tile_ref[k], preferred_element_type=F32)
        total[jnp.where(k < live_ref[0], index_ref[1, k], 2 * span)] += mirrored
    split(total, span, evens, keep_ref, send_ref)
    low_ref[...] = total[0:span]


def direct_kernel(slots, evens, live_ref, index_ref, flipped_ref, low_ref, *refs):
    parts = refs[: len(slots)]
    keep_ref, send_ref, window, total = refs[len(slots) :]
    span = low_ref.shape[0]
    for half in range(2):
        fill(window.at[half * span : (half + 1) * span], half, parts, slots)
    total[0:span] = low_ref[...]
    total[span] = jnp.zeros(total.shape[1:], F32)
    for k in range(flipped_ref.shape[0]):
        direct = jnp.dot(window[index_ref[1, k]], flipped_ref[k], preferred_element_type=F32)
        total[jnp.where(k < live_ref[0], index_ref[0, k], span)] += direct
    split(total, 0, evens, keep_ref, send_ref)


def add_kernel(keep_ref, got_ref, out_ref):
    out_ref[...] = keep_ref[...] + got_ref[...]


def gather_kernel(evens, *refs):
    members = len(evens)
    halves = refs[:members], refs[members : 2 * members]
    even_ref, odd_ref, sum_ref = refs[2 * members :]
    place = {s: n for n, s in enumerate(evens)}
    for half, (own_ref, *others) in enumerate(halves):
        for n, s in enumerate(evens):
            value = own_ref[n]
            for other, g in zip(others, evens[1:]):
                value = value + other[place[s ^ g]]
            sum_ref[half, n] = value

    def even_case():
        even_ref[...] = sum_ref[1]
        odd_ref[...] = sum_ref[0]

    def odd_case():
        even_ref[...] = sum_ref[0]
        odd_ref[...] = sum_ref[1]

    by_parity(even_case, odd_case)


def first_kernel(evens, center_ref, radius_ref, sum_ref, odd_ref, even_ref, *refs):
    parts, out_ref = refs[:-1], refs[-1]
    col = lax.axis_index("col")
    center, radius = center_ref[0], radius_ref[0]

    def degree(image, vectors):
        return ((image - center * vectors.astype(F32)) / radius).astype(BF16)

    def both(from_previous, from_next):
        inside = col < lax.axis_size("col") - 1
        for n in range(len(evens)):
            arrived = jnp.where(col > 0, from_previous[n], 0.0)
            out_ref[0, n] = degree(sum_ref[0, n] + arrived, parts[n][0])
            beyond = degree(sum_ref[1, n] + from_next[n], parts[n][1])
            out_ref[1, n] = jnp.where(inside, beyond, jnp.zeros_like(beyond))

    by_parity(lambda: both(odd_ref, even_ref), lambda: both(even_ref, odd_ref))


def spread_kernel(keep_ref, got_ref, *outs):
    for n, out_ref in enumerate(outs):
        out_ref[...] = keep_ref[n] + got_ref[n]


def owner_kernel(*refs):
    parts, out_ref = refs[:-1], refs[-1]
    total = parts[0][...]
    for part in parts[1:]:
        total = total + part[...]
    out_ref[...] = total


def second_kernel(center_ref, radius_ref, pair_ref, first_ref, even_ref, odd_ref, *refs):
    parts, (out_ref, first_out_ref) = refs[:-2], refs[-2:]
    col = lax.axis_index("col")
    center, radius = center_ref[0], radius_ref[0]
    blk, _, size = even_ref.shape

    def finish(from_previous):
        for b in range(blk):
            image = jnp.where(col > 0, from_previous[b], 0.0)
            for part in parts:
                image = image + part[b]
            first = first_ref[0, 0, b].astype(F32)
            second = 2.0 * (image - center * first) / radius - pair_ref[0, b].astype(F32)
            out_ref[:, b * size : (b + 1) * size] = second

    for b in range(blk):
        first_out_ref[:, b * size : (b + 1) * size] = first_ref[0, 0, b]
    by_parity(lambda: finish(odd_ref), lambda: finish(even_ref))


def local(vectors, tile_data, tile_row, tile_offset, tile_live, damp_center, damp_radius):
    rows = lax.axis_size("row")
    count, width = vectors.shape
    tiles, size, _ = tile_data.shape
    blk = width // size
    span = rows * blk
    evens = [s for s in range(rows) if bin(s).count("1") % 2 == 0]
    members = len(evens)

    def shape(dtype, *lead):
        return pltpu.VMEM((*lead, count, size), dtype)

    sent = pair_swap(vectors, 0), pair_swap(vectors, 1)
    kept = pltpu.VMEM(tile_data.shape, BF16)
    chunk = 8
    vectors, tile_data, flipped, index = call(
        functools.partial(load_kernel, chunk, span, blk),
        "load",
        [pltpu.VMEM(vectors.shape, BF16), kept, kept, pltpu.SMEM((2, tiles), jnp.int32)],
        [HBM] * 4,
        [tile_row.reshape(1, tiles), tile_offset.reshape(1, tiles), vectors, tile_data],
        scratch=[
            pltpu.SMEM((1, tiles), jnp.int32),
            pltpu.SMEM((1, tiles), jnp.int32),
            pltpu.SemaphoreType.DMA((tiles // chunk + 3,)),
        ],
        cost=pl.CostEstimate(flops=0, bytes_accessed=6 * tile_data.size, transcendentals=0),
    )

    flops = 2 * tiles * count * size * size
    cost = pl.CostEstimate(flops=flops, bytes_accessed=2 * tile_data.size, transcendentals=0)

    def apply(parts, slots):
        half = shape(F32, members, blk)
        keep_up, send_up, low = call(
            functools.partial(mirror_kernel, slots, evens),
            "mirror",
            [half, half, shape(F32, span)],
            [SMEM] * 2 + [VMEM] * (1 + len(parts)),
            [tile_live, index, tile_data, *parts],
            scratch=[
                pltpu.VMEM((span, count, size), BF16),
                pltpu.VMEM((2 * span + 1, count, size), F32),
            ],
            cost=cost,
        )
        got_up = row_swap(send_up, 1)
        keep_low, send_low = call(
            functools.partial(direct_kernel, slots, evens),
            "direct",
            [half, half],
            [SMEM] * 2 + [VMEM] * (2 + len(parts)),
            [tile_live, index, flipped, low, *parts],
            scratch=[
                pltpu.VMEM((2 * span, count, size), BF16),
                pltpu.VMEM((span + 1, count, size), F32),
            ],
            cost=cost,
        )
        return (keep_up, got_up), (keep_low, row_swap(send_low, 1))

    (pair,) = call(select_kernel, "select", [shape(BF16, 2, blk)], [VMEM] * 3, [vectors, *sent])
    gathered = [pair] + [row_swap(pair, s) for s in range(1, rows)]
    up, low = apply(gathered, [[s] for s in range(rows)])

    def pair_sum(ours):
        (paired,) = call(add_kernel, "add", [shape(F32, members, blk)], [VMEM] * 2, ours)
        return [paired] + [row_swap(paired, g) for g in evens[1:]]

    up = pair_sum(up)
    low = pair_sum(low)
    even, odd, total = call(
        functools.partial(gather_kernel, evens),
        "gather",
        [shape(F32, members, blk)] * 2 + [shape(F32, 2, members, blk)],
        [VMEM] * (2 * members),
        low + up,
    )
    (first,) = call(
        functools.partial(first_kernel, evens),
        "first",
        [shape(BF16, 2, members, blk)],
        [SMEM] * 2 + [VMEM] * (3 + members),
        [damp_center, damp_radius, total, pair_swap(odd, 1), pair_swap(even, 0)]
        + [gathered[s] for s in evens],
    )
    up, low = apply([first, row_swap(first, 1)], [evens, [s ^ 1 for s in evens]])

    def pieces(ours):
        parts = call(spread_kernel, "spread", [shape(F32, blk)] * members, [VMEM] * 2, ours)
        return parts[:1] + [row_swap(p, g) for p, g in zip(parts[1:], evens[1:])]

    up = pieces(up)
    low = pieces(low)
    (up,) = call(owner_kernel, "owner", [shape(F32, blk)], [VMEM] * members, up)
    second, first = call(
        second_kernel,
        "second",
        [jax.ShapeDtypeStruct((count, width), F32), jax.ShapeDtypeStruct((count, width), BF16)],
        [SMEM] * 2 + [VMEM] * (4 + members),
        [damp_center, damp_radius, pair, first, pair_swap(up, 0), pair_swap(up, 1), *low],
    )
    return first, second


def solution(mesh):
    placed = (
        P(None, ("col", "row")),
        P(("col", "row"), None, None),
        P(("col", "row")),
        P(("col", "row")),
        P(("col", "row")),
        P(),
        P(),
    )
    return jax.shard_map(
        local,
        mesh=mesh,
        in_specs=placed,
        out_specs=(P(None, ("col", "row")), P(None, ("col", "row"))),
        check_vma=False,
    )
```

time: 41.4 us -> 38.2 us (0.923)
  waiting for transfers between devices: 23.2 us -> 18.6 us
  starting transfers between devices: 8.85 us -> 11.1 us
  Pallas kernels: 6.6 us -> 5.61 us
    ppermute x8 -> x12, waiting for transfers between devices: 13.3 us -> 8.92 us  [row_swap(): return lax.ppermute(block, AXES, route)]
    ppermute x8 -> x12, starting transfers between devices: 5.05 us -> 7.25 us  [row_swap(): return lax.ppermute(block, AXES, route)]
    pallas_call x10 -> x14, Pallas kernels: 6.6 us -> 5.61 us  [call(): pl.pallas_call(kernel, out_shape=list(outs), in_specs=list(places), out_s...]
  transfers between devices with their start and end apart: 14 -> 18, of which waited for: 12 -> 15; matrix products, arithmetic and copies ran while one was open for 0% -> 0% of each run, Pallas kernels for 5% -> 9%
where the time goes in v4:
time: 38.2 us; the launch traced here: 38 us
  waiting for transfers between devices  18.6 us (49%)
  starting transfers between devices  11.1 us (29%)
  Pallas kernels  5.61 us (15%)
  between operations  2.67 us (7%)
    ppermute x6, waiting for transfers between devices, pair_swap(): return lax.ppermute(block, AXES, route)  9.68 us
    ppermute x12, waiting for transfers between devices, row_swap(): return lax.ppermute(block, AXES, route)  8.92 us
    ppermute x12, starting transfers between devices, row_swap(): return lax.ppermute(block, AXES, route)  7.25 us
    pallas_call x14, Pallas kernels, call(): pl.pallas_call(kernel, out_shape=list(outs), in_specs=list(places), out_s...  5.61 us
    ppermute x6, starting transfers between devices, pair_swap(): return lax.ppermute(block, AXES, route)  3.89 us
  transfers between devices with their start and end apart: 18, of which 15 were waited for; matrix products, arithmetic and copies ran while one was open for 0% of the time, Pallas kernels for 9%

profile of v4, /device:TPU:9, one launch (start us, length us, event | category | flops | bytes accessed | tf_op | source)
XLA Modules:
  0.0 38.0 jit_solution(12423048863199987286)
XLA Ops:
  0.6 1.8 %collective-permute-start = (bf16[32,256]{1,0:T(8,128)(2,1)}, bf16[32,256]{1,0:T(8,128)(2,1)S(1)}, u32[]{:S(2)}, u32[]{:S(2)}) collective-permute-start(bf16[32,256]{1,0:T(8,128)(2,1)} %vectors_hbm.1), channel_id=1, source_target_pairs={{0,9},{1,8},{2,11},{3,10},{4,13},{5,12},{6,15},{7,14},{8,1},{9,0},... | collective-permute-start | bytes 49160 | tf_op jit(solution)/shard_map/ppermute | solution.py:50
  2.5 2.0 %load.1 = (bf16[32,256]{1,0:T(8,128)(2,1)S(1)}, bf16[64,128,128]{2,1,0:T(8,128)(2,1)S(1)}, bf16[64,128,128]{2,1,0:T(8,128)(2,1)S(1)}, s32[2,64]{1,0:T(2,128)S(4)}) custom-call(s32[1,64]{1,0:T(1,128)} %bitcast.2, s32[1,64]{1,0:T(1,128)} %bitcast.3, bf16[32,256]{1,0:T(8,128)(2,1)} %vectors_hbm.1, bf16[64,128,128]{2,1,0:T(8,128)(2,1)} %tile_hbm.1), custom_call_target="tpu_custom_call" | custom-call | bytes 6291456 | tf_op jit(solution)/shard_map/load/pallas_call | solution.py:23
  4.5 2.2 %collective-permute-done.1.odd_ref = bf16[32,256]{1,0:T(8,128)(2,1)S(1)} collective-permute-done((bf16[32,256]{1,0:T(8,128)(2,1)}, bf16[32,256]{1,0:T(8,128)(2,1)S(1)}, u32[]{:S(2)}, u32[]{:S(2)}) %collective-permute-start.1) | collective-permute-done | bytes 16416 | tf_op jit(solution)/shard_map/ppermute | solution.py:50
  6.7 1.0 %collective-permute-start.4 = (bf16[2,2,32,128]{3,2,1,0:T(8,128)(2,1)S(1)}, bf16[2,2,32,128]{3,2,1,0:T(8,128)(2,1)S(1)}, u32[]{:S(2)}, u32[]{:S(2)}) collective-permute-start(bf16[2,2,32,128]{3,2,1,0:T(8,128)(2,1)S(1)} %select.1.refs_0_.pair_ref), channel_id=1, source_target_pairs={{0,24},{1,25},{2,26},{3,27},{4,28},{5,29},{6,30},{7,31},{8,16},{9,... | collective-permute-start | bytes 98312 | tf_op jit(solution)/shard_map/ppermute | solution.py:39
  9.3 0.8 %collective-permute-done.4.refs_3_.refs_1_ = bf16[2,2,32,128]{3,2,1,0:T(8,128)(2,1)S(1)} collective-permute-done((bf16[2,2,32,128]{3,2,1,0:T(8,128)(2,1)S(1)}, bf16[2,2,32,128]{3,2,1,0:T(8,128)(2,1)S(1)}, u32[]{:S(2)}, u32[]{:S(2)}) %collective-permute-start.4) | collective-permute-done | bytes 32800 | tf_op jit(solution)/shard_map/ppermute | solution.py:39
  10.1 1.1 %collective-permute-done.3.refs_2_ = bf16[2,2,32,128]{3,2,1,0:T(8,128)(2,1)S(1)} collective-permute-done((bf16[2,2,32,128]{3,2,1,0:T(8,128)(2,1)S(1)}, bf16[2,2,32,128]{3,2,1,0:T(8,128)(2,1)S(1)}, u32[]{:S(2)}, u32[]{:S(2)}) %collective-permute-start.3) | collective-permute-done | bytes 32800 | tf_op jit(solution)/shard_map/ppermute | solution.py:39
  11.1 0.7 %mirror.2 = (f32[2,2,32,128]{3,2,1,0:T(8,128)S(1)}, f32[2,2,32,128]{3,2,1,0:T(8,128)S(1)}, f32[8,32,128]{2,1,0:T(8,128)S(1)}) custom-call(s32[1]{0:T(128)S(6)} %copy.9.live_ref, s32[2,64]{1,0:T(2,128)S(4)} %get-tuple-element.26.index_ref, bf16[64,128,128]{2,1,0:T(8,128)(2,1)S(1)} %get-tuple-element.28.tile_ref, ...), custom_call_target="tpu_custom_call" | custom-call | flops 67108864 | bytes 2097152 | tf_op jit(solution)/shard_map/mirror/pallas_call | solution.py:23
  11.9 1.2 %collective-permute-start.7 = (f32[2,2,32,128]{3,2,1,0:T(8,128)S(1)}, f32[2,2,32,128]{3,2,1,0:T(8,128)S(1)}, u32[]{:S(2)}, u32[]{:S(2)}) collective-permute-start(f32[2,2,32,128]{3,2,1,0:T(8,128)S(1)} %get-tuple-element.33), channel_id=1, source_target_pairs={{0,8},{1,9},{2,10},{3,11},{4,12},{5,13},{6,14},{7,15},{8,0},{9,1},... | collective-permute-start | bytes 196616 | tf_op jit(solution)/shard_map/ppermute | solution.py:39
  13.1 0.7 %direct.2 = (f32[2,2,32,128]{3,2,1,0:T(8,128)S(1)}, f32[2,2,32,128]{3,2,1,0:T(8,128)S(1)}) custom-call(s32[1]{0:T(128)S(6)} %copy.9.live_ref, s32[2,64]{1,0:T(2,128)S(4)} %get-tuple-element.26.index_ref, bf16[64,128,128]{2,1,0:T(8,128)(2,1)S(1)} %get-tuple-element.27.flipped_ref, f32[8,32,128]{2,1,0:T(8,128)S(1)} %get-tuple-element.29.low_ref, ...), custom_call_target="tpu_custom_call" | custom-call | flops 67108864 | bytes 2097152 | tf_op jit(solution)/shard_map/direct/pallas_call | solution.py:23
  14.0 0.8 %collective-permute-start.8 = (f32[2,2,32,128]{3,2,1,0:T(8,128)S(1)}, f32[2,2,32,128]{3,2,1,0:T(8,128)S(1)}, u32[]{:S(2)}, u32[]{:S(2)}) collective-permute-start(f32[2,2,32,128]{3,2,1,0:T(8,128)S(1)} %add.3.refs_2_), channel_id=1, source_target_pairs={{0,24},{1,25},{2,26},{3,27},{4,28},{5,29},{6,30},{7,31},{8,16},{9,... | collective-permute-start | bytes 196616 | tf_op jit(solution)/shard_map/ppermute | solution.py:39
  15.2 0.8 %collective-permute-start.6 = (f32[2,2,32,128]{3,2,1,0:T(8,128)S(1)}, f32[2,2,32,128]{3,2,1,0:T(8,128)S(1)}, u32[]{:S(2)}, u32[]{:S(2)}) collective-permute-start(f32[2,2,32,128]{3,2,1,0:T(8,128)S(1)} %add.2.refs_0_), channel_id=1, source_target_pairs={{0,24},{1,25},{2,26},{3,27},{4,28},{5,29},{6,30},{7,31},{8,16},{9,... | collective-permute-start | bytes 196616 | tf_op jit(solution)/shard_map/ppermute | solution.py:39
  15.9 2.8 %collective-permute-done.8.refs_3_ = f32[2,2,32,128]{3,2,1,0:T(8,128)S(1)} collective-permute-done((f32[2,2,32,128]{3,2,1,0:T(8,128)S(1)}, f32[2,2,32,128]{3,2,1,0:T(8,128)S(1)}, u32[]{:S(2)}, u32[]{:S(2)}) %collective-permute-start.8) | collective-permute-done | bytes 65568 | tf_op jit(solution)/shard_map/ppermute | solution.py:39
  18.8 0.8 %collective-permute-done.6.refs_1_ = f32[2,2,32,128]{3,2,1,0:T(8,128)S(1)} collective-permute-done((f32[2,2,32,128]{3,2,1,0:T(8,128)S(1)}, f32[2,2,32,128]{3,2,1,0:T(8,128)S(1)}, u32[]{:S(2)}, u32[]{:S(2)}) %collective-permute-start.6) | collective-permute-done | bytes 65568 | tf_op jit(solution)/shard_map/ppermute | solution.py:39
  19.6 1.1 %collective-permute-start.10 = (f32[2,2,32,128]{3,2,1,0:T(8,128)S(1)}, f32[2,2,32,128]{3,2,1,0:T(8,128)S(1)}, u32[]{:S(2)}, u32[]{:S(2)}) collective-permute-start(f32[2,2,32,128]{3,2,1,0:T(8,128)S(1)} %get-tuple-element.36), channel_id=1, source_target_pairs={{0,9},{1,8},{2,11},{3,10},{4,13},{5,12},{6,15},{7,14},{8,1},{9,0},... | collective-permute-start | bytes 196616 | tf_op jit(solution)/shard_map/ppermute | solution.py:50
  22.1 1.7 %collective-permute-done.10.even_ref = f32[2,2,32,128]{3,2,1,0:T(8,128)S(1)} collective-permute-done((f32[2,2,32,128]{3,2,1,0:T(8,128)S(1)}, f32[2,2,32,128]{3,2,1,0:T(8,128)S(1)}, u32[]{:S(2)}, u32[]{:S(2)}) %collective-permute-start.10) | collective-permute-done | bytes 65568 | tf_op jit(solution)/shard_map/ppermute | solution.py:50
  23.8 1.7 %collective-permute-done.9.odd_ref = f32[2,2,32,128]{3,2,1,0:T(8,128)S(1)} collective-permute-done((f32[2,2,32,128]{3,2,1,0:T(8,128)S(1)}, f32[2,2,32,128]{3,2,1,0:T(8,128)S(1)}, u32[]{:S(2)}, u32[]{:S(2)}) %collective-permute-start.9) | collective-permute-done | bytes 65568 | tf_op jit(solution)/shard_map/ppermute | solution.py:50
  25.8 1.0 %collective-permute-done.11.refs_1_ = bf16[2,2,2,32,128]{4,3,2,1,0:T(8,128)(2,1)S(1)} collective-permute-done((bf16[2,2,2,32,128]{4,3,2,1,0:T(8,128)(2,1)S(1)}, bf16[2,2,2,32,128]{4,3,2,1,0:T(8,128)(2,1)S(1)}, u32[]{:S(2)}, u32[]{:S(2)}) %collective-permute-start.11) | collective-permute-done | bytes 65568 | tf_op jit(solution)/shard_map/ppermute | solution.py:39
  26.8 0.7 %mirror.3 = (f32[2,2,32,128]{3,2,1,0:T(8,128)S(1)}, f32[2,2,32,128]{3,2,1,0:T(8,128)S(1)}, f32[8,32,128]{2,1,0:T(8,128)S(1)}) custom-call(s32[1]{0:T(128)S(6)} %copy.9.live_ref, s32[2,64]{1,0:T(2,128)S(4)} %get-tuple-element.26.index_ref, bf16[64,128,128]{2,1,0:T(8,128)(2,1)S(1)} %get-tuple-element.28.tile_ref, ...), custom_call_target="tpu_custom_call" | custom-call | flops 67108864 | bytes 2097152 | tf_op jit(solution)/shard_map/mirror/pallas_call | solution.py:23
  27.9 0.7 %direct.3 = (f32[2,2,32,128]{3,2,1,0:T(8,128)S(1)}, f32[2,2,32,128]{3,2,1,0:T(8,128)S(1)}) custom-call(s32[1]{0:T(128)S(6)} %copy.9.live_ref, s32[2,64]{1,0:T(2,128)S(4)} %get-tuple-element.26.index_ref, bf16[64,128,128]{2,1,0:T(8,128)(2,1)S(1)} %get-tuple-element.27.flipped_ref, f32[8,32,128]{2,1,0:T(8,128)S(1)} %get-tuple-element.41.low_ref, ...), custom_call_target="tpu_custom_call" | custom-call | flops 67108864 | bytes 2097152 | tf_op jit(solution)/shard_map/direct/pallas_call | solution.py:23
  29.9 0.9 %collective-permute-start.17 = (f32[2,32,128]{2,1,0:T(8,128)S(1)}, f32[2,32,128]{2,1,0:T(8,128)S(1)}, u32[]{:S(2)}, u32[]{:S(2)}) collective-permute-start(f32[2,32,128]{2,1,0:T(8,128)S(1)} %get-tuple-element.45), channel_id=1, source_target_pairs={{0,24},{1,25},{2,26},{3,27},{4,28},{5,29},{6,30},{7,31},{8,16},{9,... | collective-permute-start | bytes 98312 | tf_op jit(solution)/shard_map/ppermute | solution.py:39
  30.8 1.5 %collective-permute-done.13.refs_1_ = f32[2,32,128]{2,1,0:T(8,128)S(1)} collective-permute-done((f32[2,32,128]{2,1,0:T(8,128)S(1)}, f32[2,32,128]{2,1,0:T(8,128)S(1)}, u32[]{:S(2)}, u32[]{:S(2)}) %collective-permute-start.13) | collective-permute-done | bytes 32800 | tf_op jit(solution)/shard_map/ppermute | solution.py:39
  32.3 0.8 %collective-permute-start.14 = (f32[2,32,128]{2,1,0:T(8,128)S(1)}, f32[2,32,128]{2,1,0:T(8,128)S(1)}, u32[]{:S(2)}, u32[]{:S(2)}) collective-permute-start(f32[2,32,128]{2,1,0:T(8,128)S(1)} %owner.1), channel_id=1, source_target_pairs={{0,9},{1,8},{2,11},{3,10},{4,13},{5,12},{6,15},{7,14},{8,1},{9,0},... | collective-permute-start | bytes 98312 | tf_op jit(solution)/shard_map/ppermute | solution.py:50
  33.3 2.4 %collective-permute-done.14.even_ref = f32[2,32,128]{2,1,0:T(8,128)S(1)} collective-permute-done((f32[2,32,128]{2,1,0:T(8,128)S(1)}, f32[2,32,128]{2,1,0:T(8,128)S(1)}, u32[]{:S(2)}, u32[]{:S(2)}) %collective-permute-start.14) | collective-permute-done | bytes 32800 | tf_op jit(solution)/shard_map/ppermute | solution.py:50
  35.7 1.7 %collective-permute-done.15.odd_ref = f32[2,32,128]{2,1,0:T(8,128)S(1)} collective-permute-done((f32[2,32,128]{2,1,0:T(8,128)S(1)}, f32[2,32,128]{2,1,0:T(8,128)S(1)}, u32[]{:S(2)}, u32[]{:S(2)}) %collective-permute-start.15) | collective-permute-done | bytes 32800 | tf_op jit(solution)/shard_map/ppermute | solution.py:50
  (26 shorter events, 4.2 us)
Async XLA Ops:
  0.6 3.9 %collective-permute-start = (bf16[32,256]{1,0:T(8,128)(2,1)}, bf16[32,256]{1,0:T(8,128)(2,1)S(1)}, u32[]{:S(2)}, u32[]{:S(2)}) collective-permute-start(bf16[32,256]{1,0:T(8,128)(2,1)} %vectors_hbm.1), channel_id=1, source_target_pairs={{0,9},{1,8},{2,11},{3,10},{4,13},{5,12},{6,15},{7,14},{8,1},{9,0},... | collective-permute-start | bytes 49160 | tf_op jit(solution)/shard_map/ppermute | solution.py:50
  2.5 4.3 %collective-permute-start.1 = (bf16[32,256]{1,0:T(8,128)(2,1)}, bf16[32,256]{1,0:T(8,128)(2,1)S(1)}, u32[]{:S(2)}, u32[]{:S(2)}) collective-permute-start(bf16[32,256]{1,0:T(8,128)(2,1)} %vectors_hbm.1), channel_id=1, source_target_pairs={{0,8},{1,10},{2,9},{3,12},{4,11},{5,14},{6,13},{7,15},{8,0},{9,2},... | collective-permute-start | bytes 49160 | tf_op jit(solution)/shard_map/ppermute | solution.py:50
  6.7 3.3 %collective-permute-start.4 = (bf16[2,2,32,128]{3,2,1,0:T(8,128)(2,1)S(1)}, bf16[2,2,32,128]{3,2,1,0:T(8,128)(2,1)S(1)}, u32[]{:S(2)}, u32[]{:S(2)}) collective-permute-start(bf16[2,2,32,128]{3,2,1,0:T(8,128)(2,1)S(1)} %select.1.refs_0_.pair_ref), channel_id=1, source_target_pairs={{0,24},{1,25},{2,26},{3,27},{4,28},{5,29},{6,30},{7,31},{8,16},{9,... | collective-permute-start | bytes 98312 | tf_op jit(solution)/shard_map/ppermute | solution.py:39
  7.7 2.4 %collective-permute-start.2 = (bf16[2,2,32,128]{3,2,1,0:T(8,128)(2,1)S(1)}, bf16[2,2,32,128]{3,2,1,0:T(8,128)(2,1)S(1)}, u32[]{:S(2)}, u32[]{:S(2)}) collective-permute-start(bf16[2,2,32,128]{3,2,1,0:T(8,128)(2,1)S(1)} %select.1.refs_0_.pair_ref), channel_id=1, source_target_pairs={{0,8},{1,9},{2,10},{3,11},{4,12},{5,13},{6,14},{7,15},{8,0},{9,1},... | collective-permute-start | bytes 98312 | tf_op jit(solution)/shard_map/ppermute | solution.py:39
  8.4 2.8 %collective-permute-start.3 = (bf16[2,2,32,128]{3,2,1,0:T(8,128)(2,1)S(1)}, bf16[2,2,32,128]{3,2,1,0:T(8,128)(2,1)S(1)}, u32[]{:S(2)}, u32[]{:S(2)}) collective-permute-start(bf16[2,2,32,128]{3,2,1,0:T(8,128)(2,1)S(1)} %select.1.refs_0_.pair_ref), channel_id=1, source_target_pairs={{0,16},{1,17},{2,18},{3,19},{4,20},{5,21},{6,22},{7,23},{8,24},{9,... | collective-permute-start | bytes 98312 | tf_op jit(solution)/shard_map/ppermute | solution.py:39
  11.9 2.2 %collective-permute-start.7 = (f32[2,2,32,128]{3,2,1,0:T(8,128)S(1)}, f32[2,2,32,128]{3,2,1,0:T(8,128)S(1)}, u32[]{:S(2)}, u32[]{:S(2)}) collective-permute-start(f32[2,2,32,128]{3,2,1,0:T(8,128)S(1)} %get-tuple-element.33), channel_id=1, source_target_pairs={{0,8},{1,9},{2,10},{3,11},{4,12},{5,13},{6,14},{7,15},{8,0},{9,1},... | collective-permute-start | bytes 196616 | tf_op jit(solution)/shard_map/ppermute | solution.py:39
  13.8 1.3 %collective-permute-start.5 = (f32[2,2,32,128]{3,2,1,0:T(8,128)S(1)}, f32[2,2,32,128]{3,2,1,0:T(8,128)S(1)}, u32[]{:S(2)}, u32[]{:S(2)}) collective-permute-start(f32[2,2,32,128]{3,2,1,0:T(8,128)S(1)} %get-tuple-element.31), channel_id=1, source_target_pairs={{0,8},{1,9},{2,10},{3,11},{4,12},{5,13},{6,14},{7,15},{8,0},{9,1},... | collective-permute-start | bytes 196616 | tf_op jit(solution)/shard_map/ppermute | solution.py:39
  14.0 4.8 %collective-permute-start.8 = (f32[2,2,32,128]{3,2,1,0:T(8,128)S(1)}, f32[2,2,32,128]{3,2,1,0:T(8,128)S(1)}, u32[]{:S(2)}, u32[]{:S(2)}) collective-permute-start(f32[2,2,32,128]{3,2,1,0:T(8,128)S(1)} %add.3.refs_2_), channel_id=1, source_target_pairs={{0,24},{1,25},{2,26},{3,27},{4,28},{5,29},{6,30},{7,31},{8,16},{9,... | collective-permute-start | bytes 196616 | tf_op jit(solution)/shard_map/ppermute | solution.py:39
  15.2 4.4 %collective-permute-start.6 = (f32[2,2,32,128]{3,2,1,0:T(8,128)S(1)}, f32[2,2,32,128]{3,2,1,0:T(8,128)S(1)}, u32[]{:S(2)}, u32[]{:S(2)}) collective-permute-start(f32[2,2,32,128]{3,2,1,0:T(8,128)S(1)} %add.2.refs_0_), channel_id=1, source_target_pairs={{0,24},{1,25},{2,26},{3,27},{4,28},{5,29},{6,30},{7,31},{8,16},{9,... | collective-permute-start | bytes 196616 | tf_op jit(solution)/shard_map/ppermute | solution.py:39
  19.6 4.2 %collective-permute-start.10 = (f32[2,2,32,128]{3,2,1,0:T(8,128)S(1)}, f32[2,2,32,128]{3,2,1,0:T(8,128)S(1)}, u32[]{:S(2)}, u32[]{:S(2)}) collective-permute-start(f32[2,2,32,128]{3,2,1,0:T(8,128)S(1)} %get-tuple-element.36), channel_id=1, source_target_pairs={{0,9},{1,8},{2,11},{3,10},{4,13},{5,12},{6,15},{7,14},{8,1},{9,0},... | collective-permute-start | bytes 196616 | tf_op jit(solution)/shard_map/ppermute | solution.py:50
  20.7 4.8 %collective-permute-start.9 = (f32[2,2,32,128]{3,2,1,0:T(8,128)S(1)}, f32[2,2,32,128]{3,2,1,0:T(8,128)S(1)}, u32[]{:S(2)}, u32[]{:S(2)}) collective-permute-start(f32[2,2,32,128]{3,2,1,0:T(8,128)S(1)} %get-tuple-element.35), channel_id=1, source_target_pairs={{0,8},{1,10},{2,9},{3,12},{4,11},{5,14},{6,13},{7,15},{8,0},{9,2},... | collective-permute-start | bytes 196616 | tf_op jit(solution)/shard_map/ppermute | solution.py:50
  25.5 1.3 %collective-permute-start.11 = (bf16[2,2,2,32,128]{4,3,2,1,0:T(8,128)(2,1)S(1)}, bf16[2,2,2,32,128]{4,3,2,1,0:T(8,128)(2,1)S(1)}, u32[]{:S(2)}, u32[]{:S(2)}) collective-permute-start(bf16[2,2,2,32,128]{4,3,2,1,0:T(8,128)(2,1)S(1)} %first.1.refs_0_.first_ref), channel_id=1, source_target_pairs={{0,8},{1,9},{2,10},{3,11},{4,12},{5,13},{6,14},{7,15},{8,0},{9,1},... | collective-permute-start | bytes 196616 | tf_op jit(solution)/shard_map/ppermute | solution.py:39
  27.5 1.4 %collective-permute-start.12 = (f32[2,2,32,128]{3,2,1,0:T(8,128)S(1)}, f32[2,2,32,128]{3,2,1,0:T(8,128)S(1)}, u32[]{:S(2)}, u32[]{:S(2)}) collective-permute-start(f32[2,2,32,128]{3,2,1,0:T(8,128)S(1)} %get-tuple-element.38), channel_id=1, source_target_pairs={{0,8},{1,9},{2,10},{3,11},{4,12},{5,13},{6,14},{7,15},{8,0},{9,1},... | collective-permute-start | bytes 196616 | tf_op jit(solution)/shard_map/ppermute | solution.py:39
  28.6 1.3 %collective-permute-start.16 = (f32[2,2,32,128]{3,2,1,0:T(8,128)S(1)}, f32[2,2,32,128]{3,2,1,0:T(8,128)S(1)}, u32[]{:S(2)}, u32[]{:S(2)}) collective-permute-start(f32[2,2,32,128]{3,2,1,0:T(8,128)S(1)} %get-tuple-element.43), channel_id=1, source_target_pairs={{0,8},{1,9},{2,10},{3,11},{4,12},{5,13},{6,14},{7,15},{8,0},{9,1},... | collective-permute-start | bytes 196616 | tf_op jit(solution)/shard_map/ppermute | solution.py:39
  28.9 3.4 %collective-permute-start.13 = (f32[2,32,128]{2,1,0:T(8,128)S(1)}, f32[2,32,128]{2,1,0:T(8,128)S(1)}, u32[]{:S(2)}, u32[]{:S(2)}) collective-permute-start(f32[2,32,128]{2,1,0:T(8,128)S(1)} %get-tuple-element.40), channel_id=1, source_target_pairs={{0,24},{1,25},{2,26},{3,27},{4,28},{5,29},{6,30},{7,31},{8,16},{9,... | collective-permute-start | bytes 98312 | tf_op jit(solution)/shard_map/ppermute | solution.py:39
  29.9 3.4 %collective-permute-start.17 = (f32[2,32,128]{2,1,0:T(8,128)S(1)}, f32[2,32,128]{2,1,0:T(8,128)S(1)}, u32[]{:S(2)}, u32[]{:S(2)}) collective-permute-start(f32[2,32,128]{2,1,0:T(8,128)S(1)} %get-tuple-element.45), channel_id=1, source_target_pairs={{0,24},{1,25},{2,26},{3,27},{4,28},{5,29},{6,30},{7,31},{8,16},{9,... | collective-permute-start | bytes 98312 | tf_op jit(solution)/shard_map/ppermute | solution.py:39
  32.3 3.3 %collective-permute-start.14 = (f32[2,32,128]{2,1,0:T(8,128)S(1)}, f32[2,32,128]{2,1,0:T(8,128)S(1)}, u32[]{:S(2)}, u32[]{:S(2)}) collective-permute-start(f32[2,32,128]{2,1,0:T(8,128)S(1)} %owner.1), channel_id=1, source_target_pairs={{0,9},{1,8},{2,11},{3,10},{4,13},{5,12},{6,15},{7,14},{8,1},{9,0},... | collective-permute-start | bytes 98312 | tf_op jit(solution)/shard_map/ppermute | solution.py:50
  33.1 4.2 %collective-permute-start.15 = (f32[2,32,128]{2,1,0:T(8,128)S(1)}, f32[2,32,128]{2,1,0:T(8,128)S(1)}, u32[]{:S(2)}, u32[]{:S(2)}) collective-permute-start(f32[2,32,128]{2,1,0:T(8,128)S(1)} %owner.1), channel_id=1, source_target_pairs={{0,8},{1,10},{2,9},{3,12},{4,11},{5,14},{6,13},{7,15},{8,0},{9,2},... | collective-permute-start | bytes 98312 | tf_op jit(solution)/shard_map/ppermute | solution.py:50

commit v5 on v4

--- a/solution.py
+++ b/solution.py
@@ -56,6 +56,28 @@
     pl.when(parity == 1)(odd_case)
 
 
+def encode(blocks, out_ref):
+    most = jnp.abs(blocks[0])
+    for block in blocks[1:]:
+        most = jnp.maximum(most, jnp.abs(block))
+    most = jnp.broadcast_to(jnp.max(most, axis=1, keepdims=True), most.shape)
+    exponent = jnp.ceil(jnp.log2(jnp.maximum(most, 1e-30)))
+    scale = jnp.exp2(-exponent) * 32767.0
+    for n, block in enumerate(blocks):
+        code = jnp.clip(jnp.round(block * scale), -32767.0, 32767.0)
+        out_ref[n] = code.astype(jnp.int32).astype(jnp.int16)
+    out_ref[len(blocks)] = exponent.astype(jnp.int32).astype(jnp.int16)
+
+
+def step_of(code_ref):
+    exponent = code_ref[code_ref.shape[0] - 1].astype(jnp.int32).astype(F32)
+    return jnp.exp2(exponent) * (1.0 / 32767.0)
+
+
+def decode(code_ref, n, step):
+    return code_ref[n].astype(jnp.int32).astype(F32) * step
+
+
 def load_kernel(chunk, span, blk, row_hbm, offset_hbm, vectors_hbm, tile_hbm, *refs):
     kept_ref, out_ref, flipped_ref, index_ref, row_ref, offset_ref, sems = refs
     count = tile_hbm.shape[0] // chunk
@@ -156,29 +178,37 @@
     split(total, 0, evens, keep_ref, send_ref)
 
 
-def add_kernel(keep_ref, got_ref, out_ref):
+def add_kernel(keep_ref, got_ref, out_ref, code_ref):
+    members, blk = out_ref.shape[:2]
     out_ref[...] = keep_ref[...] + got_ref[...]
+    encode([out_ref[n, b] for n in range(members) for b in range(blk)], code_ref)
 
 
 def gather_kernel(evens, *refs):
     members = len(evens)
     halves = refs[:members], refs[members : 2 * members]
     even_ref, odd_ref, sum_ref = refs[2 * members :]
+    blk = sum_ref.shape[2]
     place = {s: n for n, s in enumerate(evens)}
     for half, (own_ref, *others) in enumerate(halves):
+        steps = [step_of(other) for other in others]
         for n, s in enumerate(evens):
-            value = own_ref[n]
-            for other, g in zip(others, evens[1:]):
-                value = value + other[place[s ^ g]]
-            sum_ref[half, n] = value
+            for b in range(blk):
+                value = own_ref[n, b]
+                for other, step, g in zip(others, steps, evens[1:]):
+                    value = value + decode(other, place[s ^ g] * blk + b, step)
+                sum_ref[half, n, b] = value
+
+    def code(half, out_ref):
+        encode([sum_ref[half, n, b] for n in range(members) for b in range(blk)], out_ref)
 
     def even_case():
-        even_ref[...] = sum_ref[1]
-        odd_ref[...] = sum_ref[0]
+        code(1, even_ref)
+        code(0, odd_ref)
 
     def odd_case():
-        even_ref[...] = sum_ref[0]
-        odd_ref[...] = sum_ref[1]
+        code(0, even_ref)
+        code(1, odd_ref)
 
     by_parity(even_case, odd_case)
 
@@ -193,11 +223,16 @@
 
     def both(from_previous, from_next):
         inside = col < lax.axis_size("col") - 1
+        blk = out_ref.shape[2]
+        previous_step, next_step = step_of(from_previous), step_of(from_next)
         for n in range(len(evens)):
-            arrived = jnp.where(col > 0, from_previous[n], 0.0)
-            out_ref[0, n] = degree(sum_ref[0, n] + arrived, parts[n][0])
-            beyond = degree(sum_ref[1, n] + from_next[n], parts[n][1])
-            out_ref[1, n] = jnp.where(inside, beyond, jnp.zeros_like(beyond))
+            for b in range(blk):
+                arrived = decode(from_previous, n * blk + b, previous_step)
+                arrived = jnp.where(col > 0, arrived, 0.0)
+                out_ref[0, n, b] = degree(sum_ref[0, n, b] + arrived, parts[n][0, b])
+                arrived = decode(from_next, n * blk + b, next_step)
+                beyond = degree(sum_ref[1, n, b] + arrived, parts[n][1, b])
+                out_ref[1, n, b] = jnp.where(inside, beyond, jnp.zeros_like(beyond))
 
     by_parity(lambda: both(odd_ref, even_ref), lambda: both(even_ref, odd_ref))
 
@@ -300,16 +335,20 @@
     gathered = [pair] + [row_swap(pair, s) for s in range(1, rows)]
     up, low = apply(gathered, [[s] for s in range(rows)])
 
+    code = shape(jnp.int16, members * blk + 1)
+
     def pair_sum(ours):
-        (paired,) = call(add_kernel, "add", [shape(F32, members, blk)], [VMEM] * 2, ours)
-        return [paired] + [row_swap(paired, g) for g in evens[1:]]
+        paired, coded = call(
+            add_kernel, "add", [shape(F32, members, blk), code], [VMEM] * 2, ours
+        )
+        return [paired] + [row_swap(coded, g) for g in evens[1:]]
 
     up = pair_sum(up)
     low = pair_sum(low)
     even, odd, total = call(
         functools.partial(gather_kernel, evens),
         "gather",
-        [shape(F32, members, blk)] * 2 + [shape(F32, 2, members, blk)],
+        [code] * 2 + [shape(F32, 2, members, blk)],
         [VMEM] * (2 * members),
         low + up,
     )

time: 38.2 us -> 37.2 us (0.974)
  waiting for transfers between devices: 18.6 us -> 16.8 us
  Pallas kernels: 5.61 us -> 6.16 us
    ppermute x12, waiting for transfers between devices: 8.92 us -> 7.4 us  [row_swap(): return lax.ppermute(block, AXES, route)]
    pallas_call x14, Pallas kernels: 5.61 us -> 6.16 us  [call(): pl.pallas_call(kernel, out_shape=list(outs), in_specs=list(places), out_s...]
    ppermute x12, starting transfers between devices: 7.25 us -> 7.74 us  [row_swap(): return lax.ppermute(block, AXES, route)]
  transfers between devices with their start and end apart: 18 -> 18, of which waited for: 15 -> 14; matrix products, arithmetic and copies ran while one was open for 0% -> 0% of each run, Pallas kernels for 9% -> 10%
where the time goes in v5:
time: 37.2 us; the launch traced here: 37 us
  waiting for transfers between devices  16.8 us (45%)
  starting transfers between devices  11.3 us (30%)
  Pallas kernels  6.16 us (17%)
  between operations  2.68 us (7%)
    ppermute x6, waiting for transfers between devices, pair_swap(): return lax.ppermute(block, AXES, route)  9.41 us
    ppermute x12, starting transfers between devices, row_swap(): return lax.ppermute(block, AXES, route)  7.74 us
    ppermute x12, waiting for transfers between devices, row_swap(): return lax.ppermute(block, AXES, route)  7.4 us
    pallas_call x14, Pallas kernels, call(): pl.pallas_call(kernel, out_shape=list(outs), in_specs=list(places), out_s...  6.16 us
    ppermute x6, starting transfers between devices, pair_swap(): return lax.ppermute(block, AXES, route)  3.57 us
  transfers between devices with their start and end apart: 18, of which 14 were waited for; matrix products, arithmetic and copies ran while one was open for 0% of the time, Pallas kernels for 10%

profile of v5, /device:TPU:9, one launch (start us, length us, event | category | flops | bytes accessed | tf_op | source)
XLA Modules:
  0.0 37.0 jit_solution(17239836186350604664)
XLA Ops:
  0.6 1.8 %collective-permute-start = (bf16[32,256]{1,0:T(8,128)(2,1)}, bf16[32,256]{1,0:T(8,128)(2,1)S(1)}, u32[]{:S(2)}, u32[]{:S(2)}) collective-permute-start(bf16[32,256]{1,0:T(8,128)(2,1)} %vectors_hbm.1), channel_id=1, source_target_pairs={{0,9},{1,8},{2,11},{3,10},{4,13},{5,12},{6,15},{7,14},{8,1},{9,0},... | collective-permute-start | bytes 49160 | tf_op jit(solution)/shard_map/ppermute | solution.py:50
  2.5 2.0 %load.1 = (bf16[32,256]{1,0:T(8,128)(2,1)S(1)}, bf16[64,128,128]{2,1,0:T(8,128)(2,1)S(1)}, bf16[64,128,128]{2,1,0:T(8,128)(2,1)S(1)}, s32[2,64]{1,0:T(2,128)S(4)}) custom-call(s32[1,64]{1,0:T(1,128)} %bitcast.2, s32[1,64]{1,0:T(1,128)} %bitcast.3, bf16[32,256]{1,0:T(8,128)(2,1)} %vectors_hbm.1, bf16[64,128,128]{2,1,0:T(8,128)(2,1)} %tile_hbm.1), custom_call_target="tpu_custom_call" | custom-call | bytes 6291456 | tf_op jit(solution)/shard_map/load/pallas_call | solution.py:23
  4.5 2.2 %collective-permute-done.1.odd_ref = bf16[32,256]{1,0:T(8,128)(2,1)S(1)} collective-permute-done((bf16[32,256]{1,0:T(8,128)(2,1)}, bf16[32,256]{1,0:T(8,128)(2,1)S(1)}, u32[]{:S(2)}, u32[]{:S(2)}) %collective-permute-start.1) | collective-permute-done | bytes 16416 | tf_op jit(solution)/shard_map/ppermute | solution.py:50
  6.7 1.0 %collective-permute-start.4 = (bf16[2,2,32,128]{3,2,1,0:T(8,128)(2,1)S(1)}, bf16[2,2,32,128]{3,2,1,0:T(8,128)(2,1)S(1)}, u32[]{:S(2)}, u32[]{:S(2)}) collective-permute-start(bf16[2,2,32,128]{3,2,1,0:T(8,128)(2,1)S(1)} %select.1.refs_0_.pair_ref), channel_id=1, source_target_pairs={{0,24},{1,25},{2,26},{3,27},{4,28},{5,29},{6,30},{7,31},{8,16},{9,... | collective-permute-start | bytes 98312 | tf_op jit(solution)/shard_map/ppermute | solution.py:39
  9.3 0.8 %collective-permute-done.4.refs_3_.refs_1_ = bf16[2,2,32,128]{3,2,1,0:T(8,128)(2,1)S(1)} collective-permute-done((bf16[2,2,32,128]{3,2,1,0:T(8,128)(2,1)S(1)}, bf16[2,2,32,128]{3,2,1,0:T(8,128)(2,1)S(1)}, u32[]{:S(2)}, u32[]{:S(2)}) %collective-permute-start.4) | collective-permute-done | bytes 32800 | tf_op jit(solution)/shard_map/ppermute | solution.py:39
  10.1 1.1 %collective-permute-done.3.refs_2_ = bf16[2,2,32,128]{3,2,1,0:T(8,128)(2,1)S(1)} collective-permute-done((bf16[2,2,32,128]{3,2,1,0:T(8,128)(2,1)S(1)}, bf16[2,2,32,128]{3,2,1,0:T(8,128)(2,1)S(1)}, u32[]{:S(2)}, u32[]{:S(2)}) %collective-permute-start.3) | collective-permute-done | bytes 32800 | tf_op jit(solution)/shard_map/ppermute | solution.py:39
  11.1 0.8 %mirror.2 = (f32[2,2,32,128]{3,2,1,0:T(8,128)S(1)}, f32[2,2,32,128]{3,2,1,0:T(8,128)S(1)}, f32[8,32,128]{2,1,0:T(8,128)S(1)}) custom-call(s32[1]{0:T(128)S(6)} %copy.9.live_ref, s32[2,64]{1,0:T(2,128)S(4)} %get-tuple-element.30.index_ref, bf16[64,128,128]{2,1,0:T(8,128)(2,1)S(1)} %get-tuple-element.32.tile_ref, ...), custom_call_target="tpu_custom_call" | custom-call | flops 67108864 | bytes 2097152 | tf_op jit(solution)/shard_map/mirror/pallas_call | solution.py:23
  11.9 1.2 %collective-permute-start.7 = (f32[2,2,32,128]{3,2,1,0:T(8,128)S(1)}, f32[2,2,32,128]{3,2,1,0:T(8,128)S(1)}, u32[]{:S(2)}, u32[]{:S(2)}) collective-permute-start(f32[2,2,32,128]{3,2,1,0:T(8,128)S(1)} %get-tuple-element.39), channel_id=1, source_target_pairs={{0,8},{1,9},{2,10},{3,11},{4,12},{5,13},{6,14},{7,15},{8,0},{9,1},... | collective-permute-start | bytes 196616 | tf_op jit(solution)/shard_map/ppermute | solution.py:39
  14.1 0.8 %collective-permute-start.8 = (s16[5,32,128]{2,1,0:T(8,128)(2,1)S(1)}, s16[5,32,128]{2,1,0:T(8,128)(2,1)S(1)}, u32[]{:S(2)}, u32[]{:S(2)}) collective-permute-start(s16[5,32,128]{2,1,0:T(8,128)(2,1)S(1)} %get-tuple-element.41), channel_id=1, source_target_pairs={{0,24},{1,25},{2,26},{3,27},{4,28},{5,29},{6,30},{7,31},{8,16},{9,... | collective-permute-start | bytes 122888 | tf_op jit(solution)/shard_map/ppermute | solution.py:39
  15.3 0.8 %collective-permute-start.6 = (s16[5,32,128]{2,1,0:T(8,128)(2,1)S(1)}, s16[5,32,128]{2,1,0:T(8,128)(2,1)S(1)}, u32[]{:S(2)}, u32[]{:S(2)}) collective-permute-start(s16[5,32,128]{2,1,0:T(8,128)(2,1)S(1)} %get-tuple-element.37), channel_id=1, source_target_pairs={{0,24},{1,25},{2,26},{3,27},{4,28},{5,29},{6,30},{7,31},{8,16},{9,... | collective-permute-start | bytes 122888 | tf_op jit(solution)/shard_map/ppermute | solution.py:39
  16.1 1.7 %collective-permute-done.8.refs_3_ = s16[5,32,128]{2,1,0:T(8,128)(2,1)S(1)} collective-permute-done((s16[5,32,128]{2,1,0:T(8,128)(2,1)S(1)}, s16[5,32,128]{2,1,0:T(8,128)(2,1)S(1)}, u32[]{:S(2)}, u32[]{:S(2)}) %collective-permute-start.8) | collective-permute-done | bytes 40992 | tf_op jit(solution)/shard_map/ppermute | solution.py:39
  17.9 1.0 %collective-permute-done.6.refs_1_ = s16[5,32,128]{2,1,0:T(8,128)(2,1)S(1)} collective-permute-done((s16[5,32,128]{2,1,0:T(8,128)(2,1)S(1)}, s16[5,32,128]{2,1,0:T(8,128)(2,1)S(1)}, u32[]{:S(2)}, u32[]{:S(2)}) %collective-permute-start.6) | collective-permute-done | bytes 40992 | tf_op jit(solution)/shard_map/ppermute | solution.py:39
  19.0 0.8 %collective-permute-start.10 = (s16[5,32,128]{2,1,0:T(8,128)(2,1)S(1)}, s16[5,32,128]{2,1,0:T(8,128)(2,1)S(1)}, u32[]{:S(2)}, u32[]{:S(2)}) collective-permute-start(s16[5,32,128]{2,1,0:T(8,128)(2,1)S(1)} %get-tuple-element.44), channel_id=1, source_target_pairs={{0,9},{1,8},{2,11},{3,10},{4,13},{5,12},{6,15},{7,14},{8,1},{9,0},... | collective-permute-start | bytes 122888 | tf_op jit(solution)/shard_map/ppermute | solution.py:50
  21.1 1.4 %collective-permute-done.10.even_ref = s16[5,32,128]{2,1,0:T(8,128)(2,1)S(1)} collective-permute-done((s16[5,32,128]{2,1,0:T(8,128)(2,1)S(1)}, s16[5,32,128]{2,1,0:T(8,128)(2,1)S(1)}, u32[]{:S(2)}, u32[]{:S(2)}) %collective-permute-start.10) | collective-permute-done | bytes 40992 | tf_op jit(solution)/shard_map/ppermute | solution.py:50
  22.5 1.7 %collective-permute-done.9.odd_ref = s16[5,32,128]{2,1,0:T(8,128)(2,1)S(1)} collective-permute-done((s16[5,32,128]{2,1,0:T(8,128)(2,1)S(1)}, s16[5,32,128]{2,1,0:T(8,128)(2,1)S(1)}, u32[]{:S(2)}, u32[]{:S(2)}) %collective-permute-start.9) | collective-permute-done | bytes 40992 | tf_op jit(solution)/shard_map/ppermute | solution.py:50
  24.6 0.9 %collective-permute-done.11.refs_1_ = bf16[2,2,2,32,128]{4,3,2,1,0:T(8,128)(2,1)S(1)} collective-permute-done((bf16[2,2,2,32,128]{4,3,2,1,0:T(8,128)(2,1)S(1)}, bf16[2,2,2,32,128]{4,3,2,1,0:T(8,128)(2,1)S(1)}, u32[]{:S(2)}, u32[]{:S(2)}) %collective-permute-start.11) | collective-permute-done | bytes 65568 | tf_op jit(solution)/shard_map/ppermute | solution.py:39
  25.5 0.8 %mirror.3 = (f32[2,2,32,128]{3,2,1,0:T(8,128)S(1)}, f32[2,2,32,128]{3,2,1,0:T(8,128)S(1)}, f32[8,32,128]{2,1,0:T(8,128)S(1)}) custom-call(s32[1]{0:T(128)S(6)} %copy.9.live_ref, s32[2,64]{1,0:T(2,128)S(4)} %get-tuple-element.30.index_ref, bf16[64,128,128]{2,1,0:T(8,128)(2,1)S(1)} %get-tuple-element.32.tile_ref, ...), custom_call_target="tpu_custom_call" | custom-call | flops 67108864 | bytes 2097152 | tf_op jit(solution)/shard_map/mirror/pallas_call | solution.py:23
  26.7 0.7 %direct.3 = (f32[2,2,32,128]{3,2,1,0:T(8,128)S(1)}, f32[2,2,32,128]{3,2,1,0:T(8,128)S(1)}) custom-call(s32[1]{0:T(128)S(6)} %copy.9.live_ref, s32[2,64]{1,0:T(2,128)S(4)} %get-tuple-element.30.index_ref, bf16[64,128,128]{2,1,0:T(8,128)(2,1)S(1)} %get-tuple-element.31.flipped_ref, f32[8,32,128]{2,1,0:T(8,128)S(1)} %get-tuple-element.49.low_ref, ...), custom_call_target="tpu_custom_call" | custom-call | flops 67108864 | bytes 2097152 | tf_op jit(solution)/shard_map/direct/pallas_call | solution.py:23
  27.7 1.1 %collective-permute-start.13 = (f32[2,32,128]{2,1,0:T(8,128)S(1)}, f32[2,32,128]{2,1,0:T(8,128)S(1)}, u32[]{:S(2)}, u32[]{:S(2)}) collective-permute-start(f32[2,32,128]{2,1,0:T(8,128)S(1)} %get-tuple-element.48), channel_id=1, source_target_pairs={{0,24},{1,25},{2,26},{3,27},{4,28},{5,29},{6,30},{7,31},{8,16},{9,... | collective-permute-start | bytes 98312 | tf_op jit(solution)/shard_map/ppermute | solution.py:39
  28.8 0.9 %collective-permute-start.17 = (f32[2,32,128]{2,1,0:T(8,128)S(1)}, f32[2,32,128]{2,1,0:T(8,128)S(1)}, u32[]{:S(2)}, u32[]{:S(2)}) collective-permute-start(f32[2,32,128]{2,1,0:T(8,128)S(1)} %get-tuple-element.53), channel_id=1, source_target_pairs={{0,24},{1,25},{2,26},{3,27},{4,28},{5,29},{6,30},{7,31},{8,16},{9,... | collective-permute-start | bytes 98312 | tf_op jit(solution)/shard_map/ppermute | solution.py:39
  29.7 1.4 %collective-permute-done.13.refs_1_ = f32[2,32,128]{2,1,0:T(8,128)S(1)} collective-permute-done((f32[2,32,128]{2,1,0:T(8,128)S(1)}, f32[2,32,128]{2,1,0:T(8,128)S(1)}, u32[]{:S(2)}, u32[]{:S(2)}) %collective-permute-start.13) | collective-permute-done | bytes 32800 | tf_op jit(solution)/shard_map/ppermute | solution.py:39
  31.1 0.9 %collective-permute-start.14 = (f32[2,32,128]{2,1,0:T(8,128)S(1)}, f32[2,32,128]{2,1,0:T(8,128)S(1)}, u32[]{:S(2)}, u32[]{:S(2)}) collective-permute-start(f32[2,32,128]{2,1,0:T(8,128)S(1)} %owner.1), channel_id=1, source_target_pairs={{0,9},{1,8},{2,11},{3,10},{4,13},{5,12},{6,15},{7,14},{8,1},{9,0},... | collective-permute-start | bytes 98312 | tf_op jit(solution)/shard_map/ppermute | solution.py:50
  32.2 2.3 %collective-permute-done.14.even_ref = f32[2,32,128]{2,1,0:T(8,128)S(1)} collective-permute-done((f32[2,32,128]{2,1,0:T(8,128)S(1)}, f32[2,32,128]{2,1,0:T(8,128)S(1)}, u32[]{:S(2)}, u32[]{:S(2)}) %collective-permute-start.14) | collective-permute-done | bytes 32800 | tf_op jit(solution)/shard_map/ppermute | solution.py:50
  34.5 1.8 %collective-permute-done.15.odd_ref = f32[2,32,128]{2,1,0:T(8,128)S(1)} collective-permute-done((f32[2,32,128]{2,1,0:T(8,128)S(1)}, f32[2,32,128]{2,1,0:T(8,128)S(1)}, u32[]{:S(2)}, u32[]{:S(2)}) %collective-permute-start.15) | collective-permute-done | bytes 32800 | tf_op jit(solution)/shard_map/ppermute | solution.py:50
  (26 shorter events, 4.4 us)
Async XLA Ops:
  0.6 3.9 %collective-permute-start = (bf16[32,256]{1,0:T(8,128)(2,1)}, bf16[32,256]{1,0:T(8,128)(2,1)S(1)}, u32[]{:S(2)}, u32[]{:S(2)}) collective-permute-start(bf16[32,256]{1,0:T(8,128)(2,1)} %vectors_hbm.1), channel_id=1, source_target_pairs={{0,9},{1,8},{2,11},{3,10},{4,13},{5,12},{6,15},{7,14},{8,1},{9,0},... | collective-permute-start | bytes 49160 | tf_op jit(solution)/shard_map/ppermute | solution.py:50
  2.5 4.3 %collective-permute-start.1 = (bf16[32,256]{1,0:T(8,128)(2,1)}, bf16[32,256]{1,0:T(8,128)(2,1)S(1)}, u32[]{:S(2)}, u32[]{:S(2)}) collective-permute-start(bf16[32,256]{1,0:T(8,128)(2,1)} %vectors_hbm.1), channel_id=1, source_target_pairs={{0,8},{1,10},{2,9},{3,12},{4,11},{5,14},{6,13},{7,15},{8,0},{9,2},... | collective-permute-start | bytes 49160 | tf_op jit(solution)/shard_map/ppermute | solution.py:50
  6.7 3.3 %collective-permute-start.4 = (bf16[2,2,32,128]{3,2,1,0:T(8,128)(2,1)S(1)}, bf16[2,2,32,128]{3,2,1,0:T(8,128)(2,1)S(1)}, u32[]{:S(2)}, u32[]{:S(2)}) collective-permute-start(bf16[2,2,32,128]{3,2,1,0:T(8,128)(2,1)S(1)} %select.1.refs_0_.pair_ref), channel_id=1, source_target_pairs={{0,24},{1,25},{2,26},{3,27},{4,28},{5,29},{6,30},{7,31},{8,16},{9,... | collective-permute-start | bytes 98312 | tf_op jit(solution)/shard_map/ppermute | solution.py:39
  7.7 2.4 %collective-permute-start.2 = (bf16[2,2,32,128]{3,2,1,0:T(8,128)(2,1)S(1)}, bf16[2,2,32,128]{3,2,1,0:T(8,128)(2,1)S(1)}, u32[]{:S(2)}, u32[]{:S(2)}) collective-permute-start(bf16[2,2,32,128]{3,2,1,0:T(8,128)(2,1)S(1)} %select.1.refs_0_.pair_ref), channel_id=1, source_target_pairs={{0,8},{1,9},{2,10},{3,11},{4,12},{5,13},{6,14},{7,15},{8,0},{9,1},... | collective-permute-start | bytes 98312 | tf_op jit(solution)/shard_map/ppermute | solution.py:39
  8.4 2.8 %collective-permute-start.3 = (bf16[2,2,32,128]{3,2,1,0:T(8,128)(2,1)S(1)}, bf16[2,2,32,128]{3,2,1,0:T(8,128)(2,1)S(1)}, u32[]{:S(2)}, u32[]{:S(2)}) collective-permute-start(bf16[2,2,32,128]{3,2,1,0:T(8,128)(2,1)S(1)} %select.1.refs_0_.pair_ref), channel_id=1, source_target_pairs={{0,16},{1,17},{2,18},{3,19},{4,20},{5,21},{6,22},{7,23},{8,24},{9,... | collective-permute-start | bytes 98312 | tf_op jit(solution)/shard_map/ppermute | solution.py:39
  11.9 2.1 %collective-permute-start.7 = (f32[2,2,32,128]{3,2,1,0:T(8,128)S(1)}, f32[2,2,32,128]{3,2,1,0:T(8,128)S(1)}, u32[]{:S(2)}, u32[]{:S(2)}) collective-permute-start(f32[2,2,32,128]{3,2,1,0:T(8,128)S(1)} %get-tuple-element.39), channel_id=1, source_target_pairs={{0,8},{1,9},{2,10},{3,11},{4,12},{5,13},{6,14},{7,15},{8,0},{9,1},... | collective-permute-start | bytes 196616 | tf_op jit(solution)/shard_map/ppermute | solution.py:39
  13.9 1.3 %collective-permute-start.5 = (f32[2,2,32,128]{3,2,1,0:T(8,128)S(1)}, f32[2,2,32,128]{3,2,1,0:T(8,128)S(1)}, u32[]{:S(2)}, u32[]{:S(2)}) collective-permute-start(f32[2,2,32,128]{3,2,1,0:T(8,128)S(1)} %get-tuple-element.35), channel_id=1, source_target_pairs={{0,8},{1,9},{2,10},{3,11},{4,12},{5,13},{6,14},{7,15},{8,0},{9,1},... | collective-permute-start | bytes 196616 | tf_op jit(solution)/shard_map/ppermute | solution.py:39
  14.1 3.7 %collective-permute-start.8 = (s16[5,32,128]{2,1,0:T(8,128)(2,1)S(1)}, s16[5,32,128]{2,1,0:T(8,128)(2,1)S(1)}, u32[]{:S(2)}, u32[]{:S(2)}) collective-permute-start(s16[5,32,128]{2,1,0:T(8,128)(2,1)S(1)} %get-tuple-element.41), channel_id=1, source_target_pairs={{0,24},{1,25},{2,26},{3,27},{4,28},{5,29},{6,30},{7,31},{8,16},{9,... | collective-permute-start | bytes 122888 | tf_op jit(solution)/shard_map/ppermute | solution.py:39
  15.3 3.5 %collective-permute-start.6 = (s16[5,32,128]{2,1,0:T(8,128)(2,1)S(1)}, s16[5,32,128]{2,1,0:T(8,128)(2,1)S(1)}, u32[]{:S(2)}, u32[]{:S(2)}) collective-permute-start(s16[5,32,128]{2,1,0:T(8,128)(2,1)S(1)} %get-tuple-element.37), channel_id=1, source_target_pairs={{0,24},{1,25},{2,26},{3,27},{4,28},{5,29},{6,30},{7,31},{8,16},{9,... | collective-permute-start | bytes 122888 | tf_op jit(solution)/shard_map/ppermute | solution.py:39
  19.0 3.5 %collective-permute-start.10 = (s16[5,32,128]{2,1,0:T(8,128)(2,1)S(1)}, s16[5,32,128]{2,1,0:T(8,128)(2,1)S(1)}, u32[]{:S(2)}, u32[]{:S(2)}) collective-permute-start(s16[5,32,128]{2,1,0:T(8,128)(2,1)S(1)} %get-tuple-element.44), channel_id=1, source_target_pairs={{0,9},{1,8},{2,11},{3,10},{4,13},{5,12},{6,15},{7,14},{8,1},{9,0},... | collective-permute-start | bytes 122888 | tf_op jit(solution)/shard_map/ppermute | solution.py:50
  19.7 4.4 %collective-permute-start.9 = (s16[5,32,128]{2,1,0:T(8,128)(2,1)S(1)}, s16[5,32,128]{2,1,0:T(8,128)(2,1)S(1)}, u32[]{:S(2)}, u32[]{:S(2)}) collective-permute-start(s16[5,32,128]{2,1,0:T(8,128)(2,1)S(1)} %get-tuple-element.43), channel_id=1, source_target_pairs={{0,8},{1,10},{2,9},{3,12},{4,11},{5,14},{6,13},{7,15},{8,0},{9,2},... | collective-permute-start | bytes 122888 | tf_op jit(solution)/shard_map/ppermute | solution.py:50
  24.2 1.3 %collective-permute-start.11 = (bf16[2,2,2,32,128]{4,3,2,1,0:T(8,128)(2,1)S(1)}, bf16[2,2,2,32,128]{4,3,2,1,0:T(8,128)(2,1)S(1)}, u32[]{:S(2)}, u32[]{:S(2)}) collective-permute-start(bf16[2,2,2,32,128]{4,3,2,1,0:T(8,128)(2,1)S(1)} %first.1.refs_0_.first_ref), channel_id=1, source_target_pairs={{0,8},{1,9},{2,10},{3,11},{4,12},{5,13},{6,14},{7,15},{8,0},{9,1},... | collective-permute-start | bytes 196616 | tf_op jit(solution)/shard_map/ppermute | solution.py:39
  26.3 1.4 %collective-permute-start.12 = (f32[2,2,32,128]{3,2,1,0:T(8,128)S(1)}, f32[2,2,32,128]{3,2,1,0:T(8,128)S(1)}, u32[]{:S(2)}, u32[]{:S(2)}) collective-permute-start(f32[2,2,32,128]{3,2,1,0:T(8,128)S(1)} %get-tuple-element.46), channel_id=1, source_target_pairs={{0,8},{1,9},{2,10},{3,11},{4,12},{5,13},{6,14},{7,15},{8,0},{9,1},... | collective-permute-start | bytes 196616 | tf_op jit(solution)/shard_map/ppermute | solution.py:39
  27.5 1.3 %collective-permute-start.16 = (f32[2,2,32,128]{3,2,1,0:T(8,128)S(1)}, f32[2,2,32,128]{3,2,1,0:T(8,128)S(1)}, u32[]{:S(2)}, u32[]{:S(2)}) collective-permute-start(f32[2,2,32,128]{3,2,1,0:T(8,128)S(1)} %get-tuple-element.51), channel_id=1, source_target_pairs={{0,8},{1,9},{2,10},{3,11},{4,12},{5,13},{6,14},{7,15},{8,0},{9,1},... | collective-permute-start | bytes 196616 | tf_op jit(solution)/shard_map/ppermute | solution.py:39
  27.7 3.4 %collective-permute-start.13 = (f32[2,32,128]{2,1,0:T(8,128)S(1)}, f32[2,32,128]{2,1,0:T(8,128)S(1)}, u32[]{:S(2)}, u32[]{:S(2)}) collective-permute-start(f32[2,32,128]{2,1,0:T(8,128)S(1)} %get-tuple-element.48), channel_id=1, source_target_pairs={{0,24},{1,25},{2,26},{3,27},{4,28},{5,29},{6,30},{7,31},{8,16},{9,... | collective-permute-start | bytes 98312 | tf_op jit(solution)/shard_map/ppermute | solution.py:39
  28.8 3.4 %collective-permute-start.17 = (f32[2,32,128]{2,1,0:T(8,128)S(1)}, f32[2,32,128]{2,1,0:T(8,128)S(1)}, u32[]{:S(2)}, u32[]{:S(2)}) collective-permute-start(f32[2,32,128]{2,1,0:T(8,128)S(1)} %get-tuple-element.53), channel_id=1, source_target_pairs={{0,24},{1,25},{2,26},{3,27},{4,28},{5,29},{6,30},{7,31},{8,16},{9,... | collective-permute-start | bytes 98312 | tf_op jit(solution)/shard_map/ppermute | solution.py:39
  31.1 3.3 %collective-permute-start.14 = (f32[2,32,128]{2,1,0:T(8,128)S(1)}, f32[2,32,128]{2,1,0:T(8,128)S(1)}, u32[]{:S(2)}, u32[]{:S(2)}) collective-permute-start(f32[2,32,128]{2,1,0:T(8,128)S(1)} %owner.1), channel_id=1, source_target_pairs={{0,9},{1,8},{2,11},{3,10},{4,13},{5,12},{6,15},{7,14},{8,1},{9,0},... | collective-permute-start | bytes 98312 | tf_op jit(solution)/shard_map/ppermute | solution.py:50
  32.1 4.2 %collective-permute-start.15 = (f32[2,32,128]{2,1,0:T(8,128)S(1)}, f32[2,32,128]{2,1,0:T(8,128)S(1)}, u32[]{:S(2)}, u32[]{:S(2)}) collective-permute-start(f32[2,32,128]{2,1,0:T(8,128)S(1)} %owner.1), channel_id=1, source_target_pairs={{0,8},{1,10},{2,9},{3,12},{4,11},{5,14},{6,13},{7,15},{8,0},{9,2},... | collective-permute-start | bytes 98312 | tf_op jit(solution)/shard_map/ppermute | solution.py:50

commit v6 on v5

--- a/solution.py
+++ b/solution.py
@@ -114,24 +114,12 @@
             flipped_ref[k] = out_ref[k].T
 
 
-def select_kernel(own_ref, even_ref, odd_ref, out_ref):
-    col = lax.axis_index("col")
+def stack_kernel(*refs):
+    parts, out_ref = refs[:-1], refs[-1]
     size = out_ref.shape[-1]
-
-    def lay(half, value):
+    for s, part in enumerate(parts):
         for b in range(out_ref.shape[1]):
-            out_ref[half, b] = value[:, b * size : (b + 1) * size]
-
-    lay(0, own_ref[...])
-
-    def even_case():
-        lay(1, even_ref[...])
-
-    def odd_case():
-        inside = col < lax.axis_size("col") - 1
-        lay(1, jnp.where(inside, odd_ref[...], jnp.zeros_like(odd_ref)))
-
-    by_parity(even_case, odd_case)
+            out_ref[s, b] = part[:, b * size : (b + 1) * size]
 
 
 def fill(window, half, parts, slots):
@@ -139,7 +127,7 @@
         for n, s in enumerate(wanted):
             blk = part.shape[-3]
             for b in range(blk):
-                value = part[half, n, b] if len(part.shape) == 5 else part[half, b]
+                value = part[half, n, b] if len(part.shape) == 5 else part[n, b]
                 window[s * blk + b] = value
 
 
@@ -165,11 +153,25 @@
 
 
 def direct_kernel(slots, evens, live_ref, index_ref, flipped_ref, low_ref, *refs):
-    parts = refs[: len(slots)]
-    keep_ref, send_ref, window, total = refs[len(slots) :]
+    parts = refs[:-4]
+    keep_ref, send_ref, window, total = refs[-4:]
     span = low_ref.shape[0]
-    for half in range(2):
-        fill(window.at[half * span : (half + 1) * span], half, parts, slots)
+    fill(window, 0, parts[: len(slots)], slots)
+    beyond = window.at[span : 2 * span]
+    if len(parts) == len(slots):
+        fill(beyond, 1, parts, slots)
+    else:
+        even_ref, odd_ref = parts[len(slots) :]
+        inside = lax.axis_index("col") < lax.axis_size("col") - 1
+
+        def odd_case():
+            fill(beyond, 1, [odd_ref], slots)
+
+            @pl.when(jnp.logical_not(inside))
+            def _():
+                beyond[...] = jnp.zeros_like(beyond)
+
+        by_parity(lambda: fill(beyond, 1, [even_ref], slots), odd_case)
     total[0:span] = low_ref[...]
     total[span] = jnp.zeros(total.shape[1:], F32)
     for k in range(flipped_ref.shape[0]):
@@ -213,28 +215,29 @@
     by_parity(even_case, odd_case)
 
 
-def first_kernel(evens, center_ref, radius_ref, sum_ref, odd_ref, even_ref, *refs):
-    parts, out_ref = refs[:-1], refs[-1]
+def first_kernel(evens, center_ref, radius_ref, own_ref, own_even_ref, own_odd_ref, sum_ref, odd_ref, even_ref, out_ref):
     col = lax.axis_index("col")
     center, radius = center_ref[0], radius_ref[0]
 
     def degree(image, vectors):
         return ((image - center * vectors.astype(F32)) / radius).astype(BF16)
 
-    def both(from_previous, from_next):
+    def both(from_previous, from_next, next_ref):
         inside = col < lax.axis_size("col") - 1
         blk = out_ref.shape[2]
         previous_step, next_step = step_of(from_previous), step_of(from_next)
-        for n in range(len(evens)):
+        for n, s in enumerate(evens):
             for b in range(blk):
                 arrived = decode(from_previous, n * blk + b, previous_step)
                 arrived = jnp.where(col > 0, arrived, 0.0)
-                out_ref[0, n, b] = degree(sum_ref[0, n, b] + arrived, parts[n][0, b])
+                out_ref[0, n, b] = degree(sum_ref[0, n, b] + arrived, own_ref[s, b])
                 arrived = decode(from_next, n * blk + b, next_step)
-                beyond = degree(sum_ref[1, n, b] + arrived, parts[n][1, b])
+                beyond = degree(sum_ref[1, n, b] + arrived, next_ref[s, b])
                 out_ref[1, n, b] = jnp.where(inside, beyond, jnp.zeros_like(beyond))
 
-    by_parity(lambda: both(odd_ref, even_ref), lambda: both(even_ref, odd_ref))
+    by_parity(
+        lambda: both(odd_ref, even_ref, own_even_ref), lambda: both(even_ref, odd_ref, own_odd_ref)
+    )
 
 
 def spread_kernel(keep_ref, got_ref, *outs):
@@ -250,7 +253,7 @@
     out_ref[...] = total
 
 
-def second_kernel(center_ref, radius_ref, pair_ref, first_ref, even_ref, odd_ref, *refs):
+def second_kernel(center_ref, radius_ref, own_ref, first_ref, even_ref, odd_ref, *refs):
     parts, (out_ref, first_out_ref) = refs[:-2], refs[-2:]
     col = lax.axis_index("col")
     center, radius = center_ref[0], radius_ref[0]
@@ -262,7 +265,7 @@
             for part in parts:
                 image = image + part[b]
             first = first_ref[0, 0, b].astype(F32)
-            second = 2.0 * (image - center * first) / radius - pair_ref[0, b].astype(F32)
+            second = 2.0 * (image - center * first) / radius - own_ref[0, b].astype(F32)
             out_ref[:, b * size : (b + 1) * size] = second
 
     for b in range(blk):
@@ -282,7 +285,7 @@
     def shape(dtype, *lead):
         return pltpu.VMEM((*lead, count, size), dtype)
 
-    sent = pair_swap(vectors, 0), pair_swap(vectors, 1)
+    sent = [row_swap(vectors, s) for s in range(1, rows)]
     kept = pltpu.VMEM(tile_data.shape, BF16)
     chunk = 8
     vectors, tile_data, flipped, index = call(
@@ -302,7 +305,7 @@
     flops = 2 * tiles * count * size * size
     cost = pl.CostEstimate(flops=flops, bytes_accessed=2 * tile_data.size, transcendentals=0)
 
-    def apply(parts, slots):
+    def apply(parts, slots, arrived=()):
         half = shape(F32, members, blk)
         keep_up, send_up, low = call(
             functools.partial(mirror_kernel, slots, evens),
@@ -321,8 +324,8 @@
             functools.partial(direct_kernel, slots, evens),
             "direct",
             [half, half],
-            [SMEM] * 2 + [VMEM] * (2 + len(parts)),
-            [tile_live, index, flipped, low, *parts],
+            [SMEM] * 2 + [VMEM] * (2 + len(parts) + len(arrived)),
+            [tile_live, index, flipped, low, *parts, *arrived],
             scratch=[
                 pltpu.VMEM((2 * span, count, size), BF16),
                 pltpu.VMEM((span + 1, count, size), F32),
@@ -331,10 +334,11 @@
         )
         return (keep_up, got_up), (keep_low, row_swap(send_low, 1))
 
-    (pair,) = call(select_kernel, "select", [shape(BF16, 2, blk)], [VMEM] * 3, [vectors, *sent])
-    gathered = [pair] + [row_swap(pair, s) for s in range(1, rows)]
-    up, low = apply(gathered, [[s] for s in range(rows)])
-
+    (own,) = call(
+        stack_kernel, "stack", [shape(BF16, rows, blk)], [VMEM] * rows, [vectors, *sent]
+    )
+    arrived = [pair_swap(own, 0), pair_swap(own, 1)]
+    up, low = apply([own], [list(range(rows))], arrived)
     code = shape(jnp.int16, members * blk + 1)
 
     def pair_sum(ours):
@@ -356,9 +360,8 @@
         functools.partial(first_kernel, evens),
         "first",
         [shape(BF16, 2, members, blk)],
-        [SMEM] * 2 + [VMEM] * (3 + members),
-        [damp_center, damp_radius, total, pair_swap(odd, 1), pair_swap(even, 0)]
-        + [gathered[s] for s in evens],
+        [SMEM] * 2 + [VMEM] * 6,
+        [damp_center, damp_radius, own, *arrived, total, pair_swap(odd, 1), pair_swap(even, 0)],
     )
     up, low = apply([first, row_swap(first, 1)], [evens, [s ^ 1 for s in evens]])
 
@@ -374,7 +377,7 @@
         "second",
         [jax.ShapeDtypeStruct((count, width), F32), jax.ShapeDtypeStruct((count, width), BF16)],
         [SMEM] * 2 + [VMEM] * (4 + members),
-        [damp_center, damp_radius, pair, first, pair_swap(up, 0), pair_swap(up, 1), *low],
+        [damp_center, damp_radius, own, first, pair_swap(up, 0), pair_swap(up, 1), *low],
     )
     return first, second
 

time: 37.2 us -> 36.4 us (0.978)
  waiting for transfers between devices: 16.8 us -> 16.2 us
    ppermute x12, waiting for transfers between devices: 7.4 us -> 6.04 us  [row_swap(): return lax.ppermute(block, AXES, route)]
    ppermute x6, waiting for transfers between devices: 9.41 us -> 10.1 us  [pair_swap(): return lax.ppermute(block, AXES, route)]
  transfers between devices with their start and end apart: 18 -> 18, of which waited for: 14 -> 12; matrix products, arithmetic and copies ran while one was open for 0% -> 0% of each run, Pallas kernels for 10% -> 13%
where the time goes in v6:
time: 36.4 us; the launch traced here: 36.3 us
  waiting for transfers between devices  16.2 us (45%)
  starting transfers between devices  11.3 us (31%)
  Pallas kernels  6.16 us (17%)
  between operations  2.69 us (7%)
    ppermute x6, waiting for transfers between devices, pair_swap(): return lax.ppermute(block, AXES, route)  10.1 us
    ppermute x12, starting transfers between devices, row_swap(): return lax.ppermute(block, AXES, route)  7.63 us
    pallas_call x14, Pallas kernels, call(): pl.pallas_call(kernel, out_shape=list(outs), in_specs=list(places), out_s...  6.16 us
    ppermute x12, waiting for transfers between devices, row_swap(): return lax.ppermute(block, AXES, route)  6.04 us
    ppermute x6, starting transfers between devices, pair_swap(): return lax.ppermute(block, AXES, route)  3.63 us
  transfers between devices with their start and end apart: 18, of which 12 were waited for; matrix products, arithmetic and copies ran while one was open for 0% of the time, Pallas kernels for 13%

profile of v6, /device:TPU:9, one launch (start us, length us, event | category | flops | bytes accessed | tf_op | source)
XLA Modules:
  0.0 36.3 jit_solution(2827064735955416323)
XLA Ops:
  0.6 0.7 %collective-permute-start = (bf16[32,256]{1,0:T(8,128)(2,1)}, bf16[32,256]{1,0:T(8,128)(2,1)S(1)}, u32[]{:S(2)}, u32[]{:S(2)}) collective-permute-start(bf16[32,256]{1,0:T(8,128)(2,1)} %vectors_hbm.1), channel_id=1, source_target_pairs={{0,8},{1,9},{2,10},{3,11},{4,12},{5,13},{6,14},{7,15},{8,0},{9,1},... | collective-permute-start | bytes 49160 | tf_op jit(solution)/shard_map/ppermute | solution.py:39
  1.4 1.3 %collective-permute-start.1 = (bf16[32,256]{1,0:T(8,128)(2,1)}, bf16[32,256]{1,0:T(8,128)(2,1)S(1)}, u32[]{:S(2)}, u32[]{:S(2)}) collective-permute-start(bf16[32,256]{1,0:T(8,128)(2,1)} %vectors_hbm.1), channel_id=1, source_target_pairs={{0,16},{1,17},{2,18},{3,19},{4,20},{5,21},{6,22},{7,23},{8,24},{9,... | collective-permute-start | bytes 49160 | tf_op jit(solution)/shard_map/ppermute | solution.py:39
  3.1 2.0 %load.1 = (bf16[32,256]{1,0:T(8,128)(2,1)S(1)}, bf16[64,128,128]{2,1,0:T(8,128)(2,1)S(1)}, bf16[64,128,128]{2,1,0:T(8,128)(2,1)S(1)}, s32[2,64]{1,0:T(2,128)S(4)}) custom-call(s32[1,64]{1,0:T(1,128)} %bitcast.2, s32[1,64]{1,0:T(1,128)} %bitcast.3, bf16[32,256]{1,0:T(8,128)(2,1)} %vectors_hbm.1, bf16[64,128,128]{2,1,0:T(8,128)(2,1)} %tile_hbm.1), custom_call_target="tpu_custom_call" | custom-call | bytes 6291456 | tf_op jit(solution)/shard_map/load/pallas_call | solution.py:23
  5.2 0.8 %collective-permute-done.2.refs_3_ = bf16[32,256]{1,0:T(8,128)(2,1)S(1)} collective-permute-done((bf16[32,256]{1,0:T(8,128)(2,1)}, bf16[32,256]{1,0:T(8,128)(2,1)S(1)}, u32[]{:S(2)}, u32[]{:S(2)}) %collective-permute-start.2) | collective-permute-done | bytes 16416 | tf_op jit(solution)/shard_map/ppermute | solution.py:39
  6.0 1.5 %collective-permute-start.3 = (bf16[4,2,32,128]{3,2,1,0:T(8,128)(2,1)S(1)}, bf16[4,2,32,128]{3,2,1,0:T(8,128)(2,1)S(1)}, u32[]{:S(2)}, u32[]{:S(2)}) collective-permute-start(bf16[4,2,32,128]{3,2,1,0:T(8,128)(2,1)S(1)} %stack.1.refs_0_.own_ref), channel_id=1, source_target_pairs={{0,9},{1,8},{2,11},{3,10},{4,13},{5,12},{6,15},{7,14},{8,1},{9,0},... | collective-permute-start | bytes 196616 | tf_op jit(solution)/shard_map/ppermute | solution.py:50
  8.4 0.8 %mirror.2 = (f32[2,2,32,128]{3,2,1,0:T(8,128)S(1)}, f32[2,2,32,128]{3,2,1,0:T(8,128)S(1)}, f32[8,32,128]{2,1,0:T(8,128)S(1)}) custom-call(s32[1]{0:T(128)S(6)} %copy.9.live_ref, s32[2,64]{1,0:T(2,128)S(4)} %get-tuple-element.30.index_ref, bf16[64,128,128]{2,1,0:T(8,128)(2,1)S(1)} %get-tuple-element.32.tile_ref, bf16[4,2,32,128]{3,2,1,0:T(8,128)(2,1)S(1)} %stack.1.refs_0_.own_ref), custom_call_target="tpu_custom_call" | custom-call | flops 67108864 | bytes 2097152 | tf_op jit(solution)/shard_map/mirror/pallas_call | solution.py:23
  9.5 0.7 %collective-permute-done.3.refs_1_.own_even_ref = bf16[4,2,32,128]{3,2,1,0:T(8,128)(2,1)S(1)} collective-permute-done((bf16[4,2,32,128]{3,2,1,0:T(8,128)(2,1)S(1)}, bf16[4,2,32,128]{3,2,1,0:T(8,128)(2,1)S(1)}, u32[]{:S(2)}, u32[]{:S(2)}) %collective-permute-start.3) | collective-permute-done | bytes 65568 | tf_op jit(solution)/shard_map/ppermute | solution.py:50
  10.2 2.1 %collective-permute-done.4.refs_2_.own_odd_ref = bf16[4,2,32,128]{3,2,1,0:T(8,128)(2,1)S(1)} collective-permute-done((bf16[4,2,32,128]{3,2,1,0:T(8,128)(2,1)S(1)}, bf16[4,2,32,128]{3,2,1,0:T(8,128)(2,1)S(1)}, u32[]{:S(2)}, u32[]{:S(2)}) %collective-permute-start.4) | collective-permute-done | bytes 65568 | tf_op jit(solution)/shard_map/ppermute | solution.py:50
  12.3 0.7 %direct.2 = (f32[2,2,32,128]{3,2,1,0:T(8,128)S(1)}, f32[2,2,32,128]{3,2,1,0:T(8,128)S(1)}) custom-call(s32[1]{0:T(128)S(6)} %copy.9.live_ref, s32[2,64]{1,0:T(2,128)S(4)} %get-tuple-element.30.index_ref, bf16[64,128,128]{2,1,0:T(8,128)(2,1)S(1)} %get-tuple-element.31.flipped_ref, f32[8,32,128]{2,1,0:T(8,128)S(1)} %get-tuple-element.33.low_ref, ...), custom_call_target="tpu_custom_call" | custom-call | flops 67108864 | bytes 2097152 | tf_op jit(solution)/shard_map/direct/pallas_call | solution.py:23
  13.4 0.7 %collective-permute-start.8 = (s16[5,32,128]{2,1,0:T(8,128)(2,1)S(1)}, s16[5,32,128]{2,1,0:T(8,128)(2,1)S(1)}, u32[]{:S(2)}, u32[]{:S(2)}) collective-permute-start(s16[5,32,128]{2,1,0:T(8,128)(2,1)S(1)} %get-tuple-element.41), channel_id=1, source_target_pairs={{0,24},{1,25},{2,26},{3,27},{4,28},{5,29},{6,30},{7,31},{8,16},{9,... | collective-permute-start | bytes 122888 | tf_op jit(solution)/shard_map/ppermute | solution.py:39
  14.5 0.9 %collective-permute-start.6 = (s16[5,32,128]{2,1,0:T(8,128)(2,1)S(1)}, s16[5,32,128]{2,1,0:T(8,128)(2,1)S(1)}, u32[]{:S(2)}, u32[]{:S(2)}) collective-permute-start(s16[5,32,128]{2,1,0:T(8,128)(2,1)S(1)} %get-tuple-element.37), channel_id=1, source_target_pairs={{0,24},{1,25},{2,26},{3,27},{4,28},{5,29},{6,30},{7,31},{8,16},{9,... | collective-permute-start | bytes 122888 | tf_op jit(solution)/shard_map/ppermute | solution.py:39
  15.4 1.6 %collective-permute-done.8.refs_3_ = s16[5,32,128]{2,1,0:T(8,128)(2,1)S(1)} collective-permute-done((s16[5,32,128]{2,1,0:T(8,128)(2,1)S(1)}, s16[5,32,128]{2,1,0:T(8,128)(2,1)S(1)}, u32[]{:S(2)}, u32[]{:S(2)}) %collective-permute-start.8) | collective-permute-done | bytes 40992 | tf_op jit(solution)/shard_map/ppermute | solution.py:39
  17.0 1.0 %collective-permute-done.6.refs_1_ = s16[5,32,128]{2,1,0:T(8,128)(2,1)S(1)} collective-permute-done((s16[5,32,128]{2,1,0:T(8,128)(2,1)S(1)}, s16[5,32,128]{2,1,0:T(8,128)(2,1)S(1)}, u32[]{:S(2)}, u32[]{:S(2)}) %collective-permute-start.6) | collective-permute-done | bytes 40992 | tf_op jit(solution)/shard_map/ppermute | solution.py:39
  20.0 1.6 %collective-permute-done.10.even_ref = s16[5,32,128]{2,1,0:T(8,128)(2,1)S(1)} collective-permute-done((s16[5,32,128]{2,1,0:T(8,128)(2,1)S(1)}, s16[5,32,128]{2,1,0:T(8,128)(2,1)S(1)}, u32[]{:S(2)}, u32[]{:S(2)}) %collective-permute-start.10) | collective-permute-done | bytes 40992 | tf_op jit(solution)/shard_map/ppermute | solution.py:50
  21.6 1.5 %collective-permute-done.9.odd_ref = s16[5,32,128]{2,1,0:T(8,128)(2,1)S(1)} collective-permute-done((s16[5,32,128]{2,1,0:T(8,128)(2,1)S(1)}, s16[5,32,128]{2,1,0:T(8,128)(2,1)S(1)}, u32[]{:S(2)}, u32[]{:S(2)}) %collective-permute-start.9) | collective-permute-done | bytes 40992 | tf_op jit(solution)/shard_map/ppermute | solution.py:50
  23.6 0.9 %collective-permute-done.11.refs_1_ = bf16[2,2,2,32,128]{4,3,2,1,0:T(8,128)(2,1)S(1)} collective-permute-done((bf16[2,2,2,32,128]{4,3,2,1,0:T(8,128)(2,1)S(1)}, bf16[2,2,2,32,128]{4,3,2,1,0:T(8,128)(2,1)S(1)}, u32[]{:S(2)}, u32[]{:S(2)}) %collective-permute-start.11) | collective-permute-done | bytes 65568 | tf_op jit(solution)/shard_map/ppermute | solution.py:39
  24.5 0.8 %mirror.3 = (f32[2,2,32,128]{3,2,1,0:T(8,128)S(1)}, f32[2,2,32,128]{3,2,1,0:T(8,128)S(1)}, f32[8,32,128]{2,1,0:T(8,128)S(1)}) custom-call(s32[1]{0:T(128)S(6)} %copy.9.live_ref, s32[2,64]{1,0:T(2,128)S(4)} %get-tuple-element.30.index_ref, bf16[64,128,128]{2,1,0:T(8,128)(2,1)S(1)} %get-tuple-element.32.tile_ref, ...), custom_call_target="tpu_custom_call" | custom-call | flops 67108864 | bytes 2097152 | tf_op jit(solution)/shard_map/mirror/pallas_call | solution.py:23
  25.6 0.7 %direct.3 = (f32[2,2,32,128]{3,2,1,0:T(8,128)S(1)}, f32[2,2,32,128]{3,2,1,0:T(8,128)S(1)}) custom-call(s32[1]{0:T(128)S(6)} %copy.9.live_ref, s32[2,64]{1,0:T(2,128)S(4)} %get-tuple-element.30.index_ref, bf16[64,128,128]{2,1,0:T(8,128)(2,1)S(1)} %get-tuple-element.31.flipped_ref, f32[8,32,128]{2,1,0:T(8,128)S(1)} %get-tuple-element.49.low_ref, ...), custom_call_target="tpu_custom_call" | custom-call | flops 67108864 | bytes 2097152 | tf_op jit(solution)/shard_map/direct/pallas_call | solution.py:23
  26.6 1.1 %collective-permute-start.13 = (f32[2,32,128]{2,1,0:T(8,128)S(1)}, f32[2,32,128]{2,1,0:T(8,128)S(1)}, u32[]{:S(2)}, u32[]{:S(2)}) collective-permute-start(f32[2,32,128]{2,1,0:T(8,128)S(1)} %get-tuple-element.48), channel_id=1, source_target_pairs={{0,24},{1,25},{2,26},{3,27},{4,28},{5,29},{6,30},{7,31},{8,16},{9,... | collective-permute-start | bytes 98312 | tf_op jit(solution)/shard_map/ppermute | solution.py:39
  27.8 0.9 %collective-permute-start.17 = (f32[2,32,128]{2,1,0:T(8,128)S(1)}, f32[2,32,128]{2,1,0:T(8,128)S(1)}, u32[]{:S(2)}, u32[]{:S(2)}) collective-permute-start(f32[2,32,128]{2,1,0:T(8,128)S(1)} %get-tuple-element.53), channel_id=1, source_target_pairs={{0,24},{1,25},{2,26},{3,27},{4,28},{5,29},{6,30},{7,31},{8,16},{9,... | collective-permute-start | bytes 98312 | tf_op jit(solution)/shard_map/ppermute | solution.py:39
  28.6 1.4 %collective-permute-done.13.refs_1_ = f32[2,32,128]{2,1,0:T(8,128)S(1)} collective-permute-done((f32[2,32,128]{2,1,0:T(8,128)S(1)}, f32[2,32,128]{2,1,0:T(8,128)S(1)}, u32[]{:S(2)}, u32[]{:S(2)}) %collective-permute-start.13) | collective-permute-done | bytes 32800 | tf_op jit(solution)/shard_map/ppermute | solution.py:39
  30.1 1.4 %collective-permute-start.14 = (f32[2,32,128]{2,1,0:T(8,128)S(1)}, f32[2,32,128]{2,1,0:T(8,128)S(1)}, u32[]{:S(2)}, u32[]{:S(2)}) collective-permute-start(f32[2,32,128]{2,1,0:T(8,128)S(1)} %owner.1), channel_id=1, source_target_pairs={{0,9},{1,8},{2,11},{3,10},{4,13},{5,12},{6,15},{7,14},{8,1},{9,0},... | collective-permute-start | bytes 98312 | tf_op jit(solution)/shard_map/ppermute | solution.py:50
  31.4 2.0 %collective-permute-done.14.even_ref = f32[2,32,128]{2,1,0:T(8,128)S(1)} collective-permute-done((f32[2,32,128]{2,1,0:T(8,128)S(1)}, f32[2,32,128]{2,1,0:T(8,128)S(1)}, u32[]{:S(2)}, u32[]{:S(2)}) %collective-permute-start.14) | collective-permute-done | bytes 32800 | tf_op jit(solution)/shard_map/ppermute | solution.py:50
  33.4 2.3 %collective-permute-done.15.odd_ref = f32[2,32,128]{2,1,0:T(8,128)S(1)} collective-permute-done((f32[2,32,128]{2,1,0:T(8,128)S(1)}, f32[2,32,128]{2,1,0:T(8,128)S(1)}, u32[]{:S(2)}, u32[]{:S(2)}) %collective-permute-start.15) | collective-permute-done | bytes 32800 | tf_op jit(solution)/shard_map/ppermute | solution.py:50
  (26 shorter events, 4.2 us)
Async XLA Ops:
  0.6 4.5 %collective-permute-start = (bf16[32,256]{1,0:T(8,128)(2,1)}, bf16[32,256]{1,0:T(8,128)(2,1)S(1)}, u32[]{:S(2)}, u32[]{:S(2)}) collective-permute-start(bf16[32,256]{1,0:T(8,128)(2,1)} %vectors_hbm.1), channel_id=1, source_target_pairs={{0,8},{1,9},{2,10},{3,11},{4,12},{5,13},{6,14},{7,15},{8,0},{9,1},... | collective-permute-start | bytes 49160 | tf_op jit(solution)/shard_map/ppermute | solution.py:39
  1.4 3.8 %collective-permute-start.1 = (bf16[32,256]{1,0:T(8,128)(2,1)}, bf16[32,256]{1,0:T(8,128)(2,1)S(1)}, u32[]{:S(2)}, u32[]{:S(2)}) collective-permute-start(bf16[32,256]{1,0:T(8,128)(2,1)} %vectors_hbm.1), channel_id=1, source_target_pairs={{0,16},{1,17},{2,18},{3,19},{4,20},{5,21},{6,22},{7,23},{8,24},{9,... | collective-permute-start | bytes 49160 | tf_op jit(solution)/shard_map/ppermute | solution.py:39
  2.6 3.4 %collective-permute-start.2 = (bf16[32,256]{1,0:T(8,128)(2,1)}, bf16[32,256]{1,0:T(8,128)(2,1)S(1)}, u32[]{:S(2)}, u32[]{:S(2)}) collective-permute-start(bf16[32,256]{1,0:T(8,128)(2,1)} %vectors_hbm.1), channel_id=1, source_target_pairs={{0,24},{1,25},{2,26},{3,27},{4,28},{5,29},{6,30},{7,31},{8,16},{9,... | collective-permute-start | bytes 49160 | tf_op jit(solution)/shard_map/ppermute | solution.py:39
  6.0 4.1 %collective-permute-start.3 = (bf16[4,2,32,128]{3,2,1,0:T(8,128)(2,1)S(1)}, bf16[4,2,32,128]{3,2,1,0:T(8,128)(2,1)S(1)}, u32[]{:S(2)}, u32[]{:S(2)}) collective-permute-start(bf16[4,2,32,128]{3,2,1,0:T(8,128)(2,1)S(1)} %stack.1.refs_0_.own_ref), channel_id=1, source_target_pairs={{0,9},{1,8},{2,11},{3,10},{4,13},{5,12},{6,15},{7,14},{8,1},{9,0},... | collective-permute-start | bytes 196616 | tf_op jit(solution)/shard_map/ppermute | solution.py:50
  7.5 4.8 %collective-permute-start.4 = (bf16[4,2,32,128]{3,2,1,0:T(8,128)(2,1)S(1)}, bf16[4,2,32,128]{3,2,1,0:T(8,128)(2,1)S(1)}, u32[]{:S(2)}, u32[]{:S(2)}) collective-permute-start(bf16[4,2,32,128]{3,2,1,0:T(8,128)(2,1)S(1)} %stack.1.refs_0_.own_ref), channel_id=1, source_target_pairs={{0,8},{1,10},{2,9},{3,12},{4,11},{5,14},{6,13},{7,15},{8,0},{9,2},... | collective-permute-start | bytes 196616 | tf_op jit(solution)/shard_map/ppermute | solution.py:50
  9.1 4.2 %collective-permute-start.7 = (f32[2,2,32,128]{3,2,1,0:T(8,128)S(1)}, f32[2,2,32,128]{3,2,1,0:T(8,128)S(1)}, u32[]{:S(2)}, u32[]{:S(2)}) collective-permute-start(f32[2,2,32,128]{3,2,1,0:T(8,128)S(1)} %get-tuple-element.39), channel_id=1, source_target_pairs={{0,8},{1,9},{2,10},{3,11},{4,12},{5,13},{6,14},{7,15},{8,0},{9,1},... | collective-permute-start | bytes 196616 | tf_op jit(solution)/shard_map/ppermute | solution.py:39
  13.0 1.3 %collective-permute-start.5 = (f32[2,2,32,128]{3,2,1,0:T(8,128)S(1)}, f32[2,2,32,128]{3,2,1,0:T(8,128)S(1)}, u32[]{:S(2)}, u32[]{:S(2)}) collective-permute-start(f32[2,2,32,128]{3,2,1,0:T(8,128)S(1)} %get-tuple-element.35), channel_id=1, source_target_pairs={{0,8},{1,9},{2,10},{3,11},{4,12},{5,13},{6,14},{7,15},{8,0},{9,1},... | collective-permute-start | bytes 196616 | tf_op jit(solution)/shard_map/ppermute | solution.py:39
  13.4 3.6 %collective-permute-start.8 = (s16[5,32,128]{2,1,0:T(8,128)(2,1)S(1)}, s16[5,32,128]{2,1,0:T(8,128)(2,1)S(1)}, u32[]{:S(2)}, u32[]{:S(2)}) collective-permute-start(s16[5,32,128]{2,1,0:T(8,128)(2,1)S(1)} %get-tuple-element.41), channel_id=1, source_target_pairs={{0,24},{1,25},{2,26},{3,27},{4,28},{5,29},{6,30},{7,31},{8,16},{9,... | collective-permute-start | bytes 122888 | tf_op jit(solution)/shard_map/ppermute | solution.py:39
  14.5 3.5 %collective-permute-start.6 = (s16[5,32,128]{2,1,0:T(8,128)(2,1)S(1)}, s16[5,32,128]{2,1,0:T(8,128)(2,1)S(1)}, u32[]{:S(2)}, u32[]{:S(2)}) collective-permute-start(s16[5,32,128]{2,1,0:T(8,128)(2,1)S(1)} %get-tuple-element.37), channel_id=1, source_target_pairs={{0,24},{1,25},{2,26},{3,27},{4,28},{5,29},{6,30},{7,31},{8,16},{9,... | collective-permute-start | bytes 122888 | tf_op jit(solution)/shard_map/ppermute | solution.py:39
  18.1 3.5 %collective-permute-start.10 = (s16[5,32,128]{2,1,0:T(8,128)(2,1)S(1)}, s16[5,32,128]{2,1,0:T(8,128)(2,1)S(1)}, u32[]{:S(2)}, u32[]{:S(2)}) collective-permute-start(s16[5,32,128]{2,1,0:T(8,128)(2,1)S(1)} %get-tuple-element.44), channel_id=1, source_target_pairs={{0,9},{1,8},{2,11},{3,10},{4,13},{5,12},{6,15},{7,14},{8,1},{9,0},... | collective-permute-start | bytes 122888 | tf_op jit(solution)/shard_map/ppermute | solution.py:50
  18.7 4.4 %collective-permute-start.9 = (s16[5,32,128]{2,1,0:T(8,128)(2,1)S(1)}, s16[5,32,128]{2,1,0:T(8,128)(2,1)S(1)}, u32[]{:S(2)}, u32[]{:S(2)}) collective-permute-start(s16[5,32,128]{2,1,0:T(8,128)(2,1)S(1)} %get-tuple-element.43), channel_id=1, source_target_pairs={{0,8},{1,10},{2,9},{3,12},{4,11},{5,14},{6,13},{7,15},{8,0},{9,2},... | collective-permute-start | bytes 122888 | tf_op jit(solution)/shard_map/ppermute | solution.py:50
  23.2 1.3 %collective-permute-start.11 = (bf16[2,2,2,32,128]{4,3,2,1,0:T(8,128)(2,1)S(1)}, bf16[2,2,2,32,128]{4,3,2,1,0:T(8,128)(2,1)S(1)}, u32[]{:S(2)}, u32[]{:S(2)}) collective-permute-start(bf16[2,2,2,32,128]{4,3,2,1,0:T(8,128)(2,1)S(1)} %first.1.refs_0_.first_ref), channel_id=1, source_target_pairs={{0,8},{1,9},{2,10},{3,11},{4,12},{5,13},{6,14},{7,15},{8,0},{9,1},... | collective-permute-start | bytes 196616 | tf_op jit(solution)/shard_map/ppermute | solution.py:39
  25.3 1.4 %collective-permute-start.12 = (f32[2,2,32,128]{3,2,1,0:T(8,128)S(1)}, f32[2,2,32,128]{3,2,1,0:T(8,128)S(1)}, u32[]{:S(2)}, u32[]{:S(2)}) collective-permute-start(f32[2,2,32,128]{3,2,1,0:T(8,128)S(1)} %get-tuple-element.46), channel_id=1, source_target_pairs={{0,8},{1,9},{2,10},{3,11},{4,12},{5,13},{6,14},{7,15},{8,0},{9,1},... | collective-permute-start | bytes 196616 | tf_op jit(solution)/shard_map/ppermute | solution.py:39
  26.4 1.4 %collective-permute-start.16 = (f32[2,2,32,128]{3,2,1,0:T(8,128)S(1)}, f32[2,2,32,128]{3,2,1,0:T(8,128)S(1)}, u32[]{:S(2)}, u32[]{:S(2)}) collective-permute-start(f32[2,2,32,128]{3,2,1,0:T(8,128)S(1)} %get-tuple-element.51), channel_id=1, source_target_pairs={{0,8},{1,9},{2,10},{3,11},{4,12},{5,13},{6,14},{7,15},{8,0},{9,1},... | collective-permute-start | bytes 196616 | tf_op jit(solution)/shard_map/ppermute | solution.py:39
  26.6 3.4 %collective-permute-start.13 = (f32[2,32,128]{2,1,0:T(8,128)S(1)}, f32[2,32,128]{2,1,0:T(8,128)S(1)}, u32[]{:S(2)}, u32[]{:S(2)}) collective-permute-start(f32[2,32,128]{2,1,0:T(8,128)S(1)} %get-tuple-element.48), channel_id=1, source_target_pairs={{0,24},{1,25},{2,26},{3,27},{4,28},{5,29},{6,30},{7,31},{8,16},{9,... | collective-permute-start | bytes 98312 | tf_op jit(solution)/shard_map/ppermute | solution.py:39
  27.8 3.7 %collective-permute-start.17 = (f32[2,32,128]{2,1,0:T(8,128)S(1)}, f32[2,32,128]{2,1,0:T(8,128)S(1)}, u32[]{:S(2)}, u32[]{:S(2)}) collective-permute-start(f32[2,32,128]{2,1,0:T(8,128)S(1)} %get-tuple-element.53), channel_id=1, source_target_pairs={{0,24},{1,25},{2,26},{3,27},{4,28},{5,29},{6,30},{7,31},{8,16},{9,... | collective-permute-start | bytes 98312 | tf_op jit(solution)/shard_map/ppermute | solution.py:39
  30.1 3.3 %collective-permute-start.14 = (f32[2,32,128]{2,1,0:T(8,128)S(1)}, f32[2,32,128]{2,1,0:T(8,128)S(1)}, u32[]{:S(2)}, u32[]{:S(2)}) collective-permute-start(f32[2,32,128]{2,1,0:T(8,128)S(1)} %owner.1), channel_id=1, source_target_pairs={{0,9},{1,8},{2,11},{3,10},{4,13},{5,12},{6,15},{7,14},{8,1},{9,0},... | collective-permute-start | bytes 98312 | tf_op jit(solution)/shard_map/ppermute | solution.py:50
  31.4 4.2 %collective-permute-start.15 = (f32[2,32,128]{2,1,0:T(8,128)S(1)}, f32[2,32,128]{2,1,0:T(8,128)S(1)}, u32[]{:S(2)}, u32[]{:S(2)}) collective-permute-start(f32[2,32,128]{2,1,0:T(8,128)S(1)} %owner.1), channel_id=1, source_target_pairs={{0,8},{1,10},{2,9},{3,12},{4,11},{5,14},{6,13},{7,15},{8,0},{9,2},... | collective-permute-start | bytes 98312 | tf_op jit(solution)/shard_map/ppermute | solution.py:50

commit v7 on v6

--- a/solution.py
+++ b/solution.py
@@ -81,8 +81,9 @@
 def load_kernel(chunk, span, blk, row_hbm, offset_hbm, vectors_hbm, tile_hbm, *refs):
     kept_ref, out_ref, flipped_ref, index_ref, row_ref, offset_ref, sems = refs
     count = tile_hbm.shape[0] // chunk
+    size = tile_hbm.shape[-1]
     small = [
-        pltpu.make_async_copy(source, target, sems.at[count + n])
+        pltpu.make_async_copy(source, target, sems.at[2 * count + n])
         for n, (source, target) in enumerate(
             [
                 (row_hbm, row_ref),
@@ -92,26 +93,37 @@
         )
     ]
 
-    def copy(g):
+    def copies(g):
         part = pl.ds(g * chunk, chunk)
-        return pltpu.make_async_copy(tile_hbm.at[part], out_ref.at[part], sems.at[g])
+        return [
+            pltpu.make_async_copy(
+                tile_hbm.at[part, side],
+                out_ref.at[part, :, side * size : (side + 1) * size],
+                sems.at[2 * g + side],
+            )
+            for side in range(2)
+        ]
 
     for one in small:
         one.start()
     for g in range(count):
-        copy(g).start()
+        for one in copies(g):
+            one.start()
     for one in small:
         one.wait()
     me = lax.axis_index("row")
-    for k in range(tile_hbm.shape[0]):
+    for k in range(row_ref.shape[1]):
         i = row_ref[0, k]
         j = i + offset_ref[0, k]
         index_ref[0, k] = i ^ (me * blk)
         index_ref[1, k] = jnp.where(j < span, j ^ (me * blk), span + ((j - span) ^ ((me ^ 1) * blk)))
     for g in range(count):
-        copy(g).wait()
-        for k in range(g * chunk, (g + 1) * chunk):
-            flipped_ref[k] = out_ref[k].T
+        for one in copies(g):
+            one.wait()
+        for p in range(g * chunk, (g + 1) * chunk):
+            for side in range(2):
+                place = slice(side * size, (side + 1) * size)
+                flipped_ref[p, :, place] = out_ref[p, :, place].T
 
 
 def stack_kernel(*refs):
@@ -131,30 +143,42 @@
                 window[s * blk + b] = value
 
 
-def split(total, first, evens, keep_ref, send_ref):
+def split(total, other, first, evens, keep_ref, send_ref):
     blk = keep_ref.shape[1]
     for n, s in enumerate(evens):
         for b in range(blk):
-            keep_ref[n, b] = total[first + s * blk + b]
-            send_ref[n, b] = total[first + (s ^ 1) * blk + b]
+            kept, sent = first + s * blk + b, first + (s ^ 1) * blk + b
+            keep_ref[n, b] = total[kept] + other[kept]
+            send_ref[n, b] = total[sent] + other[sent]
+
+
+def products(pairs_ref, window, index_ref, source, target, live_ref, *totals):
+    spare = totals[0].shape[0] - 1
+    for p in range(pairs_ref.shape[0]):
+        stacked = jnp.concatenate([window[index_ref[source, 2 * p + side]] for side in range(2)], axis=0)
+        result = jnp.dot(stacked, pairs_ref[p], preferred_element_type=F32)
+        count, size = result.shape[0] // 2, result.shape[1] // 2
+        for side in range(2):
+            k = 2 * p + side
+            to = jnp.where(k < live_ref[0], index_ref[target, k], spare)
+            totals[side][to] += result[side * count : (side + 1) * count, side * size : (side + 1) * size]
 
 
 def mirror_kernel(slots, evens, live_ref, index_ref, tile_ref, *refs):
     parts = refs[: len(slots)]
-    keep_ref, send_ref, low_ref, window, total = refs[len(slots) :]
+    keep_ref, send_ref, low_ref, window, total, other = refs[len(slots) :]
     span = window.shape[0]
     fill(window, 0, parts, slots)
     total[...] = jnp.zeros_like(total)
-    for k in range(tile_ref.shape[0]):
-        mirrored = jnp.dot(window[index_ref[0, k]], tile_ref[k], preferred_element_type=F32)
-        total[jnp.where(k < live_ref[0], index_ref[1, k], 2 * span)] += mirrored
-    split(total, span, evens, keep_ref, send_ref)
-    low_ref[...] = total[0:span]
+    other[...] = jnp.zeros_like(other)
+    products(tile_ref, window, index_ref, 0, 1, live_ref, total, other)
+    split(total, other, span, evens, keep_ref, send_ref)
+    low_ref[...] = total[0:span] + other[0:span]
 
 
 def direct_kernel(slots, evens, live_ref, index_ref, flipped_ref, low_ref, *refs):
-    parts = refs[:-4]
-    keep_ref, send_ref, window, total = refs[-4:]
+    parts = refs[:-5]
+    keep_ref, send_ref, window, total, other = refs[-5:]
     span = low_ref.shape[0]
     fill(window, 0, parts[: len(slots)], slots)
     beyond = window.at[span : 2 * span]
@@ -174,10 +198,9 @@
         by_parity(lambda: fill(beyond, 1, [even_ref], slots), odd_case)
     total[0:span] = low_ref[...]
     total[span] = jnp.zeros(total.shape[1:], F32)
-    for k in range(flipped_ref.shape[0]):
-        direct = jnp.dot(window[index_ref[1, k]], flipped_ref[k], preferred_element_type=F32)
-        total[jnp.where(k < live_ref[0], index_ref[0, k], span)] += direct
-    split(total, 0, evens, keep_ref, send_ref)
+    other[...] = jnp.zeros_like(other)
+    products(flipped_ref, window, index_ref, 1, 0, live_ref, total, other)
+    split(total, other, 0, evens, keep_ref, send_ref)
 
 
 def add_kernel(keep_ref, got_ref, out_ref, code_ref):
@@ -286,14 +309,15 @@
         return pltpu.VMEM((*lead, count, size), dtype)
 
     sent = [row_swap(vectors, s) for s in range(1, rows)]
-    kept = pltpu.VMEM(tile_data.shape, BF16)
-    chunk = 8
+    kept = pltpu.VMEM((tiles // 2, size, 2 * size), BF16)
+    chunk = 4
     vectors, tile_data, flipped, index = call(
         functools.partial(load_kernel, chunk, span, blk),
         "load",
         [pltpu.VMEM(vectors.shape, BF16), kept, kept, pltpu.SMEM((2, tiles), jnp.int32)],
         [HBM] * 4,
-        [tile_row.reshape(1, tiles), tile_offset.reshape(1, tiles), vectors, tile_data],
+        [tile_row.reshape(1, tiles), tile_offset.reshape(1, tiles), vectors]
+        + [tile_data.reshape(tiles // 2, 2, size, size)],
         scratch=[
             pltpu.SMEM((1, tiles), jnp.int32),
             pltpu.SMEM((1, tiles), jnp.int32),
@@ -315,6 +339,7 @@
             [tile_live, index, tile_data, *parts],
             scratch=[
                 pltpu.VMEM((span, count, size), BF16),
+                pltpu.VMEM((2 * span + 1, count, size), F32),
                 pltpu.VMEM((2 * span + 1, count, size), F32),
             ],
             cost=cost,
@@ -329,6 +354,7 @@
             scratch=[
                 pltpu.VMEM((2 * span, count, size), BF16),
                 pltpu.VMEM((span + 1, count, size), F32),
+                pltpu.VMEM((span + 1, count, size), F32),
             ],
             cost=cost,
         )

time: 36.4 us -> 35.8 us (0.984)
  Pallas kernels: 6.16 us -> 5.13 us
    pallas_call x14, Pallas kernels: 6.16 us -> 5.13 us  [call(): pl.pallas_call(kernel, out_shape=list(outs), in_specs=list(places), out_s...]
  transfers between devices with their start and end apart: 18 -> 18, of which waited for: 12 -> 14; matrix products, arithmetic and copies ran while one was open for 0% -> 0% of each run, Pallas kernels for 13% -> 11%
where the time goes in v7:
time: 35.8 us; the launch traced here: 35.5 us
  waiting for transfers between devices  16.4 us (46%)
  starting transfers between devices  11.4 us (32%)
  Pallas kernels  5.13 us (14%)
  between operations  2.69 us (8%)
    ppermute x6, waiting for transfers between devices, pair_swap(): return lax.ppermute(block, AXES, route)  10.3 us
    ppermute x12, starting transfers between devices, row_swap(): return lax.ppermute(block, AXES, route)  7.96 us
    ppermute x12, waiting for transfers between devices, row_swap(): return lax.ppermute(block, AXES, route)  6.09 us
    pallas_call x14, Pallas kernels, call(): pl.pallas_call(kernel, out_shape=list(outs), in_specs=list(places), out_s...  5.13 us
    ppermute x6, starting transfers between devices, pair_swap(): return lax.ppermute(block, AXES, route)  3.39 us
  transfers between devices with their start and end apart: 18, of which 14 were waited for; matrix products, arithmetic and copies ran while one was open for 0% of the time, Pallas kernels for 11%

profile of v7, /device:TPU:9, one launch (start us, length us, event | category | flops | bytes accessed | tf_op | source)
XLA Modules:
  0.0 35.5 jit_solution(10748156590942402273)
XLA Ops:
  0.6 0.7 %collective-permute-start = (bf16[32,256]{1,0:T(8,128)(2,1)}, bf16[32,256]{1,0:T(8,128)(2,1)S(1)}, u32[]{:S(2)}, u32[]{:S(2)}) collective-permute-start(bf16[32,256]{1,0:T(8,128)(2,1)} %vectors_hbm.1), channel_id=1, source_target_pairs={{0,8},{1,9},{2,10},{3,11},{4,12},{5,13},{6,14},{7,15},{8,0},{9,1},... | collective-permute-start | bytes 49160 | tf_op jit(solution)/shard_map/ppermute | solution.py:39
  1.4 1.3 %collective-permute-start.1 = (bf16[32,256]{1,0:T(8,128)(2,1)}, bf16[32,256]{1,0:T(8,128)(2,1)S(1)}, u32[]{:S(2)}, u32[]{:S(2)}) collective-permute-start(bf16[32,256]{1,0:T(8,128)(2,1)} %vectors_hbm.1), channel_id=1, source_target_pairs={{0,16},{1,17},{2,18},{3,19},{4,20},{5,21},{6,22},{7,23},{8,24},{9,... | collective-permute-start | bytes 49160 | tf_op jit(solution)/shard_map/ppermute | solution.py:39
  3.1 2.2 %load.1 = (bf16[32,256]{1,0:T(8,128)(2,1)S(1)}, bf16[32,128,256]{2,1,0:T(8,128)(2,1)S(1)}, bf16[32,128,256]{2,1,0:T(8,128)(2,1)S(1)}, s32[2,64]{1,0:T(2,128)S(4)}) custom-call(s32[1,64]{1,0:T(1,128)} %bitcast.4, s32[1,64]{1,0:T(1,128)} %bitcast.5, bf16[32,256]{1,0:T(8,128)(2,1)} %vectors_hbm.1, bf16[32,2,128,128]{3,2,1,0:T(8,128)(2,1)} %bitcast.3), custom_call_target="tpu_custom_call" | custom-call | bytes 6291456 | tf_op jit(solution)/shard_map/load/pallas_call | solution.py:23
  5.3 0.7 %collective-permute-done.2.refs_3_ = bf16[32,256]{1,0:T(8,128)(2,1)S(1)} collective-permute-done((bf16[32,256]{1,0:T(8,128)(2,1)}, bf16[32,256]{1,0:T(8,128)(2,1)S(1)}, u32[]{:S(2)}, u32[]{:S(2)}) %collective-permute-start.2) | collective-permute-done | bytes 16416 | tf_op jit(solution)/shard_map/ppermute | solution.py:39
  6.0 1.5 %collective-permute-start.3 = (bf16[4,2,32,128]{3,2,1,0:T(8,128)(2,1)S(1)}, bf16[4,2,32,128]{3,2,1,0:T(8,128)(2,1)S(1)}, u32[]{:S(2)}, u32[]{:S(2)}) collective-permute-start(bf16[4,2,32,128]{3,2,1,0:T(8,128)(2,1)S(1)} %stack.1.refs_0_.own_ref), channel_id=1, source_target_pairs={{0,9},{1,8},{2,11},{3,10},{4,13},{5,12},{6,15},{7,14},{8,1},{9,0},... | collective-permute-start | bytes 196616 | tf_op jit(solution)/shard_map/ppermute | solution.py:50
  8.4 0.5 %mirror.2 = (f32[2,2,32,128]{3,2,1,0:T(8,128)S(1)}, f32[2,2,32,128]{3,2,1,0:T(8,128)S(1)}, f32[8,32,128]{2,1,0:T(8,128)S(1)}) custom-call(s32[1]{0:T(128)S(6)} %copy.9.live_ref, s32[2,64]{1,0:T(2,128)S(4)} %get-tuple-element.30.index_ref, bf16[32,128,256]{2,1,0:T(8,128)(2,1)S(1)} %get-tuple-element.32.tile_ref, bf16[4,2,32,128]{3,2,1,0:T(8,128)(2,1)S(1)} %stack.1.refs_0_.own_ref), custom_call_target="tpu_custom_call" | custom-call | flops 67108864 | bytes 2097152 | tf_op jit(solution)/shard_map/mirror/pallas_call | solution.py:23
  9.3 0.9 %collective-permute-done.3.refs_1_.own_even_ref = bf16[4,2,32,128]{3,2,1,0:T(8,128)(2,1)S(1)} collective-permute-done((bf16[4,2,32,128]{3,2,1,0:T(8,128)(2,1)S(1)}, bf16[4,2,32,128]{3,2,1,0:T(8,128)(2,1)S(1)}, u32[]{:S(2)}, u32[]{:S(2)}) %collective-permute-start.3) | collective-permute-done | bytes 65568 | tf_op jit(solution)/shard_map/ppermute | solution.py:50
  10.2 2.1 %collective-permute-done.4.refs_2_.own_odd_ref = bf16[4,2,32,128]{3,2,1,0:T(8,128)(2,1)S(1)} collective-permute-done((bf16[4,2,32,128]{3,2,1,0:T(8,128)(2,1)S(1)}, bf16[4,2,32,128]{3,2,1,0:T(8,128)(2,1)S(1)}, u32[]{:S(2)}, u32[]{:S(2)}) %collective-permute-start.4) | collective-permute-done | bytes 65568 | tf_op jit(solution)/shard_map/ppermute | solution.py:50
  13.2 0.7 %collective-permute-start.8 = (s16[5,32,128]{2,1,0:T(8,128)(2,1)S(1)}, s16[5,32,128]{2,1,0:T(8,128)(2,1)S(1)}, u32[]{:S(2)}, u32[]{:S(2)}) collective-permute-start(s16[5,32,128]{2,1,0:T(8,128)(2,1)S(1)} %get-tuple-element.41), channel_id=1, source_target_pairs={{0,24},{1,25},{2,26},{3,27},{4,28},{5,29},{6,30},{7,31},{8,16},{9,... | collective-permute-start | bytes 122888 | tf_op jit(solution)/shard_map/ppermute | solution.py:39
  14.2 1.0 %collective-permute-start.6 = (s16[5,32,128]{2,1,0:T(8,128)(2,1)S(1)}, s16[5,32,128]{2,1,0:T(8,128)(2,1)S(1)}, u32[]{:S(2)}, u32[]{:S(2)}) collective-permute-start(s16[5,32,128]{2,1,0:T(8,128)(2,1)S(1)} %get-tuple-element.37), channel_id=1, source_target_pairs={{0,24},{1,25},{2,26},{3,27},{4,28},{5,29},{6,30},{7,31},{8,16},{9,... | collective-permute-start | bytes 122888 | tf_op jit(solution)/shard_map/ppermute | solution.py:39
  15.2 1.5 %collective-permute-done.8.refs_3_ = s16[5,32,128]{2,1,0:T(8,128)(2,1)S(1)} collective-permute-done((s16[5,32,128]{2,1,0:T(8,128)(2,1)S(1)}, s16[5,32,128]{2,1,0:T(8,128)(2,1)S(1)}, u32[]{:S(2)}, u32[]{:S(2)}) %collective-permute-start.8) | collective-permute-done | bytes 40992 | tf_op jit(solution)/shard_map/ppermute | solution.py:39
  16.7 1.0 %collective-permute-done.6.refs_1_ = s16[5,32,128]{2,1,0:T(8,128)(2,1)S(1)} collective-permute-done((s16[5,32,128]{2,1,0:T(8,128)(2,1)S(1)}, s16[5,32,128]{2,1,0:T(8,128)(2,1)S(1)}, u32[]{:S(2)}, u32[]{:S(2)}) %collective-permute-start.6) | collective-permute-done | bytes 40992 | tf_op jit(solution)/shard_map/ppermute | solution.py:39
  17.9 0.6 %collective-permute-start.10 = (s16[5,32,128]{2,1,0:T(8,128)(2,1)S(1)}, s16[5,32,128]{2,1,0:T(8,128)(2,1)S(1)}, u32[]{:S(2)}, u32[]{:S(2)}) collective-permute-start(s16[5,32,128]{2,1,0:T(8,128)(2,1)S(1)} %get-tuple-element.44), channel_id=1, source_target_pairs={{0,9},{1,8},{2,11},{3,10},{4,13},{5,12},{6,15},{7,14},{8,1},{9,0},... | collective-permute-start | bytes 122888 | tf_op jit(solution)/shard_map/ppermute | solution.py:50
  19.8 1.7 %collective-permute-done.10.even_ref = s16[5,32,128]{2,1,0:T(8,128)(2,1)S(1)} collective-permute-done((s16[5,32,128]{2,1,0:T(8,128)(2,1)S(1)}, s16[5,32,128]{2,1,0:T(8,128)(2,1)S(1)}, u32[]{:S(2)}, u32[]{:S(2)}) %collective-permute-start.10) | collective-permute-done | bytes 40992 | tf_op jit(solution)/shard_map/ppermute | solution.py:50
  21.5 1.4 %collective-permute-done.9.odd_ref = s16[5,32,128]{2,1,0:T(8,128)(2,1)S(1)} collective-permute-done((s16[5,32,128]{2,1,0:T(8,128)(2,1)S(1)}, s16[5,32,128]{2,1,0:T(8,128)(2,1)S(1)}, u32[]{:S(2)}, u32[]{:S(2)}) %collective-permute-start.9) | collective-permute-done | bytes 40992 | tf_op jit(solution)/shard_map/ppermute | solution.py:50
  23.4 0.9 %collective-permute-done.11.refs_1_ = bf16[2,2,2,32,128]{4,3,2,1,0:T(8,128)(2,1)S(1)} collective-permute-done((bf16[2,2,2,32,128]{4,3,2,1,0:T(8,128)(2,1)S(1)}, bf16[2,2,2,32,128]{4,3,2,1,0:T(8,128)(2,1)S(1)}, u32[]{:S(2)}, u32[]{:S(2)}) %collective-permute-start.11) | collective-permute-done | bytes 65568 | tf_op jit(solution)/shard_map/ppermute | solution.py:39
  24.3 0.5 %mirror.3 = (f32[2,2,32,128]{3,2,1,0:T(8,128)S(1)}, f32[2,2,32,128]{3,2,1,0:T(8,128)S(1)}, f32[8,32,128]{2,1,0:T(8,128)S(1)}) custom-call(s32[1]{0:T(128)S(6)} %copy.9.live_ref, s32[2,64]{1,0:T(2,128)S(4)} %get-tuple-element.30.index_ref, bf16[32,128,256]{2,1,0:T(8,128)(2,1)S(1)} %get-tuple-element.32.tile_ref, ...), custom_call_target="tpu_custom_call" | custom-call | flops 67108864 | bytes 2097152 | tf_op jit(solution)/shard_map/mirror/pallas_call | solution.py:23
  26.1 1.2 %collective-permute-start.13 = (f32[2,32,128]{2,1,0:T(8,128)S(1)}, f32[2,32,128]{2,1,0:T(8,128)S(1)}, u32[]{:S(2)}, u32[]{:S(2)}) collective-permute-start(f32[2,32,128]{2,1,0:T(8,128)S(1)} %get-tuple-element.48), channel_id=1, source_target_pairs={{0,24},{1,25},{2,26},{3,27},{4,28},{5,29},{6,30},{7,31},{8,16},{9,... | collective-permute-start | bytes 98312 | tf_op jit(solution)/shard_map/ppermute | solution.py:39
  27.3 0.7 %collective-permute-start.17 = (f32[2,32,128]{2,1,0:T(8,128)S(1)}, f32[2,32,128]{2,1,0:T(8,128)S(1)}, u32[]{:S(2)}, u32[]{:S(2)}) collective-permute-start(f32[2,32,128]{2,1,0:T(8,128)S(1)} %get-tuple-element.53), channel_id=1, source_target_pairs={{0,24},{1,25},{2,26},{3,27},{4,28},{5,29},{6,30},{7,31},{8,16},{9,... | collective-permute-start | bytes 98312 | tf_op jit(solution)/shard_map/ppermute | solution.py:39
  28.0 1.5 %collective-permute-done.13.refs_1_ = f32[2,32,128]{2,1,0:T(8,128)S(1)} collective-permute-done((f32[2,32,128]{2,1,0:T(8,128)S(1)}, f32[2,32,128]{2,1,0:T(8,128)S(1)}, u32[]{:S(2)}, u32[]{:S(2)}) %collective-permute-start.13) | collective-permute-done | bytes 32800 | tf_op jit(solution)/shard_map/ppermute | solution.py:39
  29.6 1.1 %collective-permute-start.14 = (f32[2,32,128]{2,1,0:T(8,128)S(1)}, f32[2,32,128]{2,1,0:T(8,128)S(1)}, u32[]{:S(2)}, u32[]{:S(2)}) collective-permute-start(f32[2,32,128]{2,1,0:T(8,128)S(1)} %owner.1), channel_id=1, source_target_pairs={{0,9},{1,8},{2,11},{3,10},{4,13},{5,12},{6,15},{7,14},{8,1},{9,0},... | collective-permute-start | bytes 98312 | tf_op jit(solution)/shard_map/ppermute | solution.py:50
  30.7 2.2 %collective-permute-done.14.even_ref = f32[2,32,128]{2,1,0:T(8,128)S(1)} collective-permute-done((f32[2,32,128]{2,1,0:T(8,128)S(1)}, f32[2,32,128]{2,1,0:T(8,128)S(1)}, u32[]{:S(2)}, u32[]{:S(2)}) %collective-permute-start.14) | collective-permute-done | bytes 32800 | tf_op jit(solution)/shard_map/ppermute | solution.py:50
  32.9 2.0 %collective-permute-done.15.odd_ref = f32[2,32,128]{2,1,0:T(8,128)S(1)} collective-permute-done((f32[2,32,128]{2,1,0:T(8,128)S(1)}, f32[2,32,128]{2,1,0:T(8,128)S(1)}, u32[]{:S(2)}, u32[]{:S(2)}) %collective-permute-start.15) | collective-permute-done | bytes 32800 | tf_op jit(solution)/shard_map/ppermute | solution.py:50
  34.9 0.6 %second.1 = (f32[32,256]{1,0:T(8,128)}, bf16[32,256]{1,0:T(8,128)(2,1)}) custom-call(f32[1]{0:T(128)S(6)} %copy.10.center_ref, f32[1]{0:T(128)S(6)} %copy.11.radius_ref, bf16[4,2,32,128]{3,2,1,0:T(8,128)(2,1)S(1)} %stack.1.refs_0_.own_ref, bf16[2,2,2,32,128]{4,3,2,1,0:T(8,128)(2,1)S(1)} %first.1.refs_0_.first_ref, ...), custom_call_target="tpu_custom_call" | custom-call | tf_op jit(solution)/shard_map/second/pallas_call | solution.py:23
  (26 shorter events, 4.3 us)
Async XLA Ops:
  0.6 4.6 %collective-permute-start = (bf16[32,256]{1,0:T(8,128)(2,1)}, bf16[32,256]{1,0:T(8,128)(2,1)S(1)}, u32[]{:S(2)}, u32[]{:S(2)}) collective-permute-start(bf16[32,256]{1,0:T(8,128)(2,1)} %vectors_hbm.1), channel_id=1, source_target_pairs={{0,8},{1,9},{2,10},{3,11},{4,12},{5,13},{6,14},{7,15},{8,0},{9,1},... | collective-permute-start | bytes 49160 | tf_op jit(solution)/shard_map/ppermute | solution.py:39
  1.4 3.9 %collective-permute-start.1 = (bf16[32,256]{1,0:T(8,128)(2,1)}, bf16[32,256]{1,0:T(8,128)(2,1)S(1)}, u32[]{:S(2)}, u32[]{:S(2)}) collective-permute-start(bf16[32,256]{1,0:T(8,128)(2,1)} %vectors_hbm.1), channel_id=1, source_target_pairs={{0,16},{1,17},{2,18},{3,19},{4,20},{5,21},{6,22},{7,23},{8,24},{9,... | collective-permute-start | bytes 49160 | tf_op jit(solution)/shard_map/ppermute | solution.py:39
  2.6 3.4 %collective-permute-start.2 = (bf16[32,256]{1,0:T(8,128)(2,1)}, bf16[32,256]{1,0:T(8,128)(2,1)S(1)}, u32[]{:S(2)}, u32[]{:S(2)}) collective-permute-start(bf16[32,256]{1,0:T(8,128)(2,1)} %vectors_hbm.1), channel_id=1, source_target_pairs={{0,24},{1,25},{2,26},{3,27},{4,28},{5,29},{6,30},{7,31},{8,16},{9,... | collective-permute-start | bytes 49160 | tf_op jit(solution)/shard_map/ppermute | solution.py:39
  6.0 4.1 %collective-permute-start.3 = (bf16[4,2,32,128]{3,2,1,0:T(8,128)(2,1)S(1)}, bf16[4,2,32,128]{3,2,1,0:T(8,128)(2,1)S(1)}, u32[]{:S(2)}, u32[]{:S(2)}) collective-permute-start(bf16[4,2,32,128]{3,2,1,0:T(8,128)(2,1)S(1)} %stack.1.refs_0_.own_ref), channel_id=1, source_target_pairs={{0,9},{1,8},{2,11},{3,10},{4,13},{5,12},{6,15},{7,14},{8,1},{9,0},... | collective-permute-start | bytes 196616 | tf_op jit(solution)/shard_map/ppermute | solution.py:50
  7.5 4.8 %collective-permute-start.4 = (bf16[4,2,32,128]{3,2,1,0:T(8,128)(2,1)S(1)}, bf16[4,2,32,128]{3,2,1,0:T(8,128)(2,1)S(1)}, u32[]{:S(2)}, u32[]{:S(2)}) collective-permute-start(bf16[4,2,32,128]{3,2,1,0:T(8,128)(2,1)S(1)} %stack.1.refs_0_.own_ref), channel_id=1, source_target_pairs={{0,8},{1,10},{2,9},{3,12},{4,11},{5,14},{6,13},{7,15},{8,0},{9,2},... | collective-permute-start | bytes 196616 | tf_op jit(solution)/shard_map/ppermute | solution.py:50
  8.9 4.3 %collective-permute-start.7 = (f32[2,2,32,128]{3,2,1,0:T(8,128)S(1)}, f32[2,2,32,128]{3,2,1,0:T(8,128)S(1)}, u32[]{:S(2)}, u32[]{:S(2)}) collective-permute-start(f32[2,2,32,128]{3,2,1,0:T(8,128)S(1)} %get-tuple-element.39), channel_id=1, source_target_pairs={{0,8},{1,9},{2,10},{3,11},{4,12},{5,13},{6,14},{7,15},{8,0},{9,1},... | collective-permute-start | bytes 196616 | tf_op jit(solution)/shard_map/ppermute | solution.py:39
  12.8 1.3 %collective-permute-start.5 = (f32[2,2,32,128]{3,2,1,0:T(8,128)S(1)}, f32[2,2,32,128]{3,2,1,0:T(8,128)S(1)}, u32[]{:S(2)}, u32[]{:S(2)}) collective-permute-start(f32[2,2,32,128]{3,2,1,0:T(8,128)S(1)} %get-tuple-element.35), channel_id=1, source_target_pairs={{0,8},{1,9},{2,10},{3,11},{4,12},{5,13},{6,14},{7,15},{8,0},{9,1},... | collective-permute-start | bytes 196616 | tf_op jit(solution)/shard_map/ppermute | solution.py:39
  13.2 3.5 %collective-permute-start.8 = (s16[5,32,128]{2,1,0:T(8,128)(2,1)S(1)}, s16[5,32,128]{2,1,0:T(8,128)(2,1)S(1)}, u32[]{:S(2)}, u32[]{:S(2)}) collective-permute-start(s16[5,32,128]{2,1,0:T(8,128)(2,1)S(1)} %get-tuple-element.41), channel_id=1, source_target_pairs={{0,24},{1,25},{2,26},{3,27},{4,28},{5,29},{6,30},{7,31},{8,16},{9,... | collective-permute-start | bytes 122888 | tf_op jit(solution)/shard_map/ppermute | solution.py:39
  14.2 3.5 %collective-permute-start.6 = (s16[5,32,128]{2,1,0:T(8,128)(2,1)S(1)}, s16[5,32,128]{2,1,0:T(8,128)(2,1)S(1)}, u32[]{:S(2)}, u32[]{:S(2)}) collective-permute-start(s16[5,32,128]{2,1,0:T(8,128)(2,1)S(1)} %get-tuple-element.37), channel_id=1, source_target_pairs={{0,24},{1,25},{2,26},{3,27},{4,28},{5,29},{6,30},{7,31},{8,16},{9,... | collective-permute-start | bytes 122888 | tf_op jit(solution)/shard_map/ppermute | solution.py:39
  17.9 3.6 %collective-permute-start.10 = (s16[5,32,128]{2,1,0:T(8,128)(2,1)S(1)}, s16[5,32,128]{2,1,0:T(8,128)(2,1)S(1)}, u32[]{:S(2)}, u32[]{:S(2)}) collective-permute-start(s16[5,32,128]{2,1,0:T(8,128)(2,1)S(1)} %get-tuple-element.44), channel_id=1, source_target_pairs={{0,9},{1,8},{2,11},{3,10},{4,13},{5,12},{6,15},{7,14},{8,1},{9,0},... | collective-permute-start | bytes 122888 | tf_op jit(solution)/shard_map/ppermute | solution.py:50
  18.5 4.4 %collective-permute-start.9 = (s16[5,32,128]{2,1,0:T(8,128)(2,1)S(1)}, s16[5,32,128]{2,1,0:T(8,128)(2,1)S(1)}, u32[]{:S(2)}, u32[]{:S(2)}) collective-permute-start(s16[5,32,128]{2,1,0:T(8,128)(2,1)S(1)} %get-tuple-element.43), channel_id=1, source_target_pairs={{0,8},{1,10},{2,9},{3,12},{4,11},{5,14},{6,13},{7,15},{8,0},{9,2},... | collective-permute-start | bytes 122888 | tf_op jit(solution)/shard_map/ppermute | solution.py:50
  22.9 1.3 %collective-permute-start.11 = (bf16[2,2,2,32,128]{4,3,2,1,0:T(8,128)(2,1)S(1)}, bf16[2,2,2,32,128]{4,3,2,1,0:T(8,128)(2,1)S(1)}, u32[]{:S(2)}, u32[]{:S(2)}) collective-permute-start(bf16[2,2,2,32,128]{4,3,2,1,0:T(8,128)(2,1)S(1)} %first.1.refs_0_.first_ref), channel_id=1, source_target_pairs={{0,8},{1,9},{2,10},{3,11},{4,12},{5,13},{6,14},{7,15},{8,0},{9,1},... | collective-permute-start | bytes 196616 | tf_op jit(solution)/shard_map/ppermute | solution.py:39
  24.8 1.4 %collective-permute-start.12 = (f32[2,2,32,128]{3,2,1,0:T(8,128)S(1)}, f32[2,2,32,128]{3,2,1,0:T(8,128)S(1)}, u32[]{:S(2)}, u32[]{:S(2)}) collective-permute-start(f32[2,2,32,128]{3,2,1,0:T(8,128)S(1)} %get-tuple-element.46), channel_id=1, source_target_pairs={{0,8},{1,9},{2,10},{3,11},{4,12},{5,13},{6,14},{7,15},{8,0},{9,1},... | collective-permute-start | bytes 196616 | tf_op jit(solution)/shard_map/ppermute | solution.py:39
  25.7 1.6 %collective-permute-start.16 = (f32[2,2,32,128]{3,2,1,0:T(8,128)S(1)}, f32[2,2,32,128]{3,2,1,0:T(8,128)S(1)}, u32[]{:S(2)}, u32[]{:S(2)}) collective-permute-start(f32[2,2,32,128]{3,2,1,0:T(8,128)S(1)} %get-tuple-element.51), channel_id=1, source_target_pairs={{0,8},{1,9},{2,10},{3,11},{4,12},{5,13},{6,14},{7,15},{8,0},{9,1},... | collective-permute-start | bytes 196616 | tf_op jit(solution)/shard_map/ppermute | solution.py:39
  26.1 3.4 %collective-permute-start.13 = (f32[2,32,128]{2,1,0:T(8,128)S(1)}, f32[2,32,128]{2,1,0:T(8,128)S(1)}, u32[]{:S(2)}, u32[]{:S(2)}) collective-permute-start(f32[2,32,128]{2,1,0:T(8,128)S(1)} %get-tuple-element.48), channel_id=1, source_target_pairs={{0,24},{1,25},{2,26},{3,27},{4,28},{5,29},{6,30},{7,31},{8,16},{9,... | collective-permute-start | bytes 98312 | tf_op jit(solution)/shard_map/ppermute | solution.py:39
  27.3 3.4 %collective-permute-start.17 = (f32[2,32,128]{2,1,0:T(8,128)S(1)}, f32[2,32,128]{2,1,0:T(8,128)S(1)}, u32[]{:S(2)}, u32[]{:S(2)}) collective-permute-start(f32[2,32,128]{2,1,0:T(8,128)S(1)} %get-tuple-element.53), channel_id=1, source_target_pairs={{0,24},{1,25},{2,26},{3,27},{4,28},{5,29},{6,30},{7,31},{8,16},{9,... | collective-permute-start | bytes 98312 | tf_op jit(solution)/shard_map/ppermute | solution.py:39
  29.6 3.4 %collective-permute-start.14 = (f32[2,32,128]{2,1,0:T(8,128)S(1)}, f32[2,32,128]{2,1,0:T(8,128)S(1)}, u32[]{:S(2)}, u32[]{:S(2)}) collective-permute-start(f32[2,32,128]{2,1,0:T(8,128)S(1)} %owner.1), channel_id=1, source_target_pairs={{0,9},{1,8},{2,11},{3,10},{4,13},{5,12},{6,15},{7,14},{8,1},{9,0},... | collective-permute-start | bytes 98312 | tf_op jit(solution)/shard_map/ppermute | solution.py:50
  30.7 4.3 %collective-permute-start.15 = (f32[2,32,128]{2,1,0:T(8,128)S(1)}, f32[2,32,128]{2,1,0:T(8,128)S(1)}, u32[]{:S(2)}, u32[]{:S(2)}) collective-permute-start(f32[2,32,128]{2,1,0:T(8,128)S(1)} %owner.1), channel_id=1, source_target_pairs={{0,8},{1,10},{2,9},{3,12},{4,11},{5,14},{6,13},{7,15},{8,0},{9,2},... | collective-permute-start | bytes 98312 | tf_op jit(solution)/shard_map/ppermute | solution.py:50

commit v8 on v7

--- a/solution.py
+++ b/solution.py
@@ -56,26 +56,30 @@
     pl.when(parity == 1)(odd_case)
 
 
+ROWS = 16
+
+
 def encode(blocks, out_ref):
-    most = jnp.abs(blocks[0])
-    for block in blocks[1:]:
-        most = jnp.maximum(most, jnp.abs(block))
-    most = jnp.broadcast_to(jnp.max(most, axis=1, keepdims=True), most.shape)
+    parts = [block[r : r + ROWS] for block in blocks for r in range(0, block.shape[0], ROWS)]
+    most = jnp.abs(parts[0])
+    for part in parts[1:]:
+        most = jnp.maximum(most, jnp.abs(part))
     exponent = jnp.ceil(jnp.log2(jnp.maximum(most, 1e-30)))
     scale = jnp.exp2(-exponent) * 32767.0
-    for n, block in enumerate(blocks):
-        code = jnp.clip(jnp.round(block * scale), -32767.0, 32767.0)
-        out_ref[n] = code.astype(jnp.int32).astype(jnp.int16)
-    out_ref[len(blocks)] = exponent.astype(jnp.int32).astype(jnp.int16)
-
-
-def step_of(code_ref):
-    exponent = code_ref[code_ref.shape[0] - 1].astype(jnp.int32).astype(F32)
-    return jnp.exp2(exponent) * (1.0 / 32767.0)
+    for n, part in enumerate(parts):
+        code = jnp.clip(jnp.round(part * scale), -32767.0, 32767.0)
+        out_ref[n * ROWS : (n + 1) * ROWS] = code.astype(jnp.int32).astype(jnp.int16)
+    out_ref[len(parts) * ROWS :] = exponent.astype(jnp.int32).astype(jnp.int16)
+
+
+def step_of(code_ref, height):
+    exponent = code_ref[code_ref.shape[0] - ROWS :].astype(jnp.int32).astype(F32)
+    return jnp.concatenate([jnp.exp2(exponent) * (1.0 / 32767.0)] * (height // ROWS), axis=0)
 
 
 def decode(code_ref, n, step):
-    return code_ref[n].astype(jnp.int32).astype(F32) * step
+    height = step.shape[0]
+    return code_ref[n * height : (n + 1) * height].astype(jnp.int32).astype(F32) * step
 
 
 def load_kernel(chunk, span, blk, row_hbm, offset_hbm, vectors_hbm, tile_hbm, *refs):
@@ -216,7 +220,7 @@
     blk = sum_ref.shape[2]
     place = {s: n for n, s in enumerate(evens)}
     for half, (own_ref, *others) in enumerate(halves):
-        steps = [step_of(other) for other in others]
+        steps = [step_of(other, own_ref.shape[2]) for other in others]
         for n, s in enumerate(evens):
             for b in range(blk):
                 value = own_ref[n, b]
@@ -248,7 +252,8 @@
     def both(from_previous, from_next, next_ref):
         inside = col < lax.axis_size("col") - 1
         blk = out_ref.shape[2]
-        previous_step, next_step = step_of(from_previous), step_of(from_next)
+        height = out_ref.shape[3]
+        previous_step, next_step = step_of(from_previous, height), step_of(from_next, height)
         for n, s in enumerate(evens):
             for b in range(blk):
                 arrived = decode(from_previous, n * blk + b, previous_step)
@@ -263,30 +268,34 @@
     )
 
 
-def spread_kernel(keep_ref, got_ref, *outs):
-    for n, out_ref in enumerate(outs):
-        out_ref[...] = keep_ref[n] + got_ref[n]
-
-
-def owner_kernel(*refs):
-    parts, out_ref = refs[:-1], refs[-1]
-    total = parts[0][...]
-    for part in parts[1:]:
-        total = total + part[...]
-    out_ref[...] = total
+def spread_kernel(keep_ref, got_ref, own_ref, *outs):
+    own_ref[...] = keep_ref[0] + got_ref[0]
+    for n, out_ref in enumerate(outs, 1):
+        encode([keep_ref[n, b] + got_ref[n, b] for b in range(keep_ref.shape[1])], out_ref)
+
+
+def total_of(own_ref, others, b):
+    value = own_ref[b]
+    for other in others:
+        value = value + decode(other, b, step_of(other, own_ref.shape[1]))
+    return value
+
+
+def owner_kernel(own_ref, *refs):
+    encode([total_of(own_ref, refs[:-1], b) for b in range(own_ref.shape[0])], refs[-1])
 
 
 def second_kernel(center_ref, radius_ref, own_ref, first_ref, even_ref, odd_ref, *refs):
-    parts, (out_ref, first_out_ref) = refs[:-2], refs[-2:]
+    (low_ref, *others), (out_ref, first_out_ref) = refs[:-2], refs[-2:]
     col = lax.axis_index("col")
     center, radius = center_ref[0], radius_ref[0]
-    blk, _, size = even_ref.shape
+    blk, height, size = low_ref.shape
 
     def finish(from_previous):
+        step = step_of(from_previous, height)
         for b in range(blk):
-            image = jnp.where(col > 0, from_previous[b], 0.0)
-            for part in parts:
-                image = image + part[b]
+            arrived = jnp.where(col > 0, decode(from_previous, b, step), 0.0)
+            image = total_of(low_ref, others, b) + arrived
             first = first_ref[0, 0, b].astype(F32)
             second = 2.0 * (image - center * first) / radius - own_ref[0, b].astype(F32)
             out_ref[:, b * size : (b + 1) * size] = second
@@ -365,7 +374,11 @@
     )
     arrived = [pair_swap(own, 0), pair_swap(own, 1)]
     up, low = apply([own], [list(range(rows))], arrived)
-    code = shape(jnp.int16, members * blk + 1)
+
+    def coded_shape(blocks):
+        return pltpu.VMEM((blocks * count + ROWS, size), jnp.int16)
+
+    code = coded_shape(members * blk)
 
     def pair_sum(ours):
         paired, coded = call(
@@ -391,13 +404,15 @@
     )
     up, low = apply([first, row_swap(first, 1)], [evens, [s ^ 1 for s in evens]])
 
+    spread = [shape(F32, blk)] + [coded_shape(blk)] * (members - 1)
+
     def pieces(ours):
-        parts = call(spread_kernel, "spread", [shape(F32, blk)] * members, [VMEM] * 2, ours)
+        parts = call(spread_kernel, "spread", spread, [VMEM] * 2, ours)
         return parts[:1] + [row_swap(p, g) for p, g in zip(parts[1:], evens[1:])]
 
     up = pieces(up)
     low = pieces(low)
-    (up,) = call(owner_kernel, "owner", [shape(F32, blk)], [VMEM] * members, up)
+    (up,) = call(owner_kernel, "owner", [coded_shape(blk)], [VMEM] * members, up)
     second, first = call(
         second_kernel,
         "second",

time: 35.8 us -> 35.4 us (0.989)
  transfers between devices with their start and end apart: 18 -> 18, of which waited for: 14 -> 13; matrix products, arithmetic and copies ran while one was open for 0% -> 0% of each run, Pallas kernels for 11% -> 11%
where the time goes in v8:
time: 35.4 us; the launch traced here: 35.1 us
  waiting for transfers between devices  16.1 us (45%)
  starting transfers between devices  11.3 us (32%)
  Pallas kernels  5.05 us (14%)
  between operations  2.71 us (8%)
    ppermute x6, waiting for transfers between devices, pair_swap(): return lax.ppermute(block, AXES, route)  10.1 us
    ppermute x12, starting transfers between devices, row_swap(): return lax.ppermute(block, AXES, route)  7.79 us
    ppermute x12, waiting for transfers between devices, row_swap(): return lax.ppermute(block, AXES, route)  5.95 us
    pallas_call x14, Pallas kernels, call(): pl.pallas_call(kernel, out_shape=list(outs), in_specs=list(places), out_s...  5.05 us
    ppermute x6, starting transfers between devices, pair_swap(): return lax.ppermute(block, AXES, route)  3.48 us
  transfers between devices with their start and end apart: 18, of which 13 were waited for; matrix products, arithmetic and copies ran while one was open for 0% of the time, Pallas kernels for 11%

profile of v8, /device:TPU:9, one launch (start us, length us, event | category | flops | bytes accessed | tf_op | source)
XLA Modules:
  0.0 35.1 jit_solution(13393034413594177929)
XLA Ops:
  0.6 0.7 %collective-permute-start = (bf16[32,256]{1,0:T(8,128)(2,1)}, bf16[32,256]{1,0:T(8,128)(2,1)S(1)}, u32[]{:S(2)}, u32[]{:S(2)}) collective-permute-start(bf16[32,256]{1,0:T(8,128)(2,1)} %vectors_hbm.1), channel_id=1, source_target_pairs={{0,8},{1,9},{2,10},{3,11},{4,12},{5,13},{6,14},{7,15},{8,0},{9,1},... | collective-permute-start | bytes 49160 | tf_op jit(solution)/shard_map/ppermute | solution.py:39
  1.4 1.3 %collective-permute-start.1 = (bf16[32,256]{1,0:T(8,128)(2,1)}, bf16[32,256]{1,0:T(8,128)(2,1)S(1)}, u32[]{:S(2)}, u32[]{:S(2)}) collective-permute-start(bf16[32,256]{1,0:T(8,128)(2,1)} %vectors_hbm.1), channel_id=1, source_target_pairs={{0,16},{1,17},{2,18},{3,19},{4,20},{5,21},{6,22},{7,23},{8,24},{9,... | collective-permute-start | bytes 49160 | tf_op jit(solution)/shard_map/ppermute | solution.py:39
  3.1 2.2 %load.1 = (bf16[32,256]{1,0:T(8,128)(2,1)S(1)}, bf16[32,128,256]{2,1,0:T(8,128)(2,1)S(1)}, bf16[32,128,256]{2,1,0:T(8,128)(2,1)S(1)}, s32[2,64]{1,0:T(2,128)S(4)}) custom-call(s32[1,64]{1,0:T(1,128)} %bitcast.4, s32[1,64]{1,0:T(1,128)} %bitcast.5, bf16[32,256]{1,0:T(8,128)(2,1)} %vectors_hbm.1, bf16[32,2,128,128]{3,2,1,0:T(8,128)(2,1)} %bitcast.3), custom_call_target="tpu_custom_call" | custom-call | bytes 6291456 | tf_op jit(solution)/shard_map/load/pallas_call | solution.py:23
  5.3 0.7 %collective-permute-done.2.refs_3_ = bf16[32,256]{1,0:T(8,128)(2,1)S(1)} collective-permute-done((bf16[32,256]{1,0:T(8,128)(2,1)}, bf16[32,256]{1,0:T(8,128)(2,1)S(1)}, u32[]{:S(2)}, u32[]{:S(2)}) %collective-permute-start.2) | collective-permute-done | bytes 16416 | tf_op jit(solution)/shard_map/ppermute | solution.py:39
  6.0 1.5 %collective-permute-start.3 = (bf16[4,2,32,128]{3,2,1,0:T(8,128)(2,1)S(1)}, bf16[4,2,32,128]{3,2,1,0:T(8,128)(2,1)S(1)}, u32[]{:S(2)}, u32[]{:S(2)}) collective-permute-start(bf16[4,2,32,128]{3,2,1,0:T(8,128)(2,1)S(1)} %stack.1.refs_0_.own_ref), channel_id=1, source_target_pairs={{0,9},{1,8},{2,11},{3,10},{4,13},{5,12},{6,15},{7,14},{8,1},{9,0},... | collective-permute-start | bytes 196616 | tf_op jit(solution)/shard_map/ppermute | solution.py:50
  9.3 0.9 %collective-permute-done.3.refs_1_.own_even_ref = bf16[4,2,32,128]{3,2,1,0:T(8,128)(2,1)S(1)} collective-permute-done((bf16[4,2,32,128]{3,2,1,0:T(8,128)(2,1)S(1)}, bf16[4,2,32,128]{3,2,1,0:T(8,128)(2,1)S(1)}, u32[]{:S(2)}, u32[]{:S(2)}) %collective-permute-start.3) | collective-permute-done | bytes 65568 | tf_op jit(solution)/shard_map/ppermute | solution.py:50
  10.2 2.1 %collective-permute-done.4.refs_2_.own_odd_ref = bf16[4,2,32,128]{3,2,1,0:T(8,128)(2,1)S(1)} collective-permute-done((bf16[4,2,32,128]{3,2,1,0:T(8,128)(2,1)S(1)}, bf16[4,2,32,128]{3,2,1,0:T(8,128)(2,1)S(1)}, u32[]{:S(2)}, u32[]{:S(2)}) %collective-permute-start.4) | collective-permute-done | bytes 65568 | tf_op jit(solution)/shard_map/ppermute | solution.py:50
  12.3 0.5 %direct.2 = (f32[2,2,32,128]{3,2,1,0:T(8,128)S(1)}, f32[2,2,32,128]{3,2,1,0:T(8,128)S(1)}) custom-call(s32[1]{0:T(128)S(6)} %copy.9.live_ref, s32[2,64]{1,0:T(2,128)S(4)} %get-tuple-element.30.index_ref, bf16[32,128,256]{2,1,0:T(8,128)(2,1)S(1)} %get-tuple-element.31.flipped_ref, f32[8,32,128]{2,1,0:T(8,128)S(1)} %get-tuple-element.33.low_ref, ...), custom_call_target="tpu_custom_call" | custom-call | flops 67108864 | bytes 2097152 | tf_op jit(solution)/shard_map/direct/pallas_call | solution.py:23
  13.1 0.7 %collective-permute-start.8 = (s16[144,128]{1,0:T(8,128)(2,1)S(1)}, s16[144,128]{1,0:T(8,128)(2,1)S(1)}, u32[]{:S(2)}, u32[]{:S(2)}) collective-permute-start(s16[144,128]{1,0:T(8,128)(2,1)S(1)} %get-tuple-element.41), channel_id=1, source_target_pairs={{0,24},{1,25},{2,26},{3,27},{4,28},{5,29},{6,30},{7,31},{8,16},{9,... | collective-permute-start | bytes 110600 | tf_op jit(solution)/shard_map/ppermute | solution.py:39
  14.2 0.9 %collective-permute-start.6 = (s16[144,128]{1,0:T(8,128)(2,1)S(1)}, s16[144,128]{1,0:T(8,128)(2,1)S(1)}, u32[]{:S(2)}, u32[]{:S(2)}) collective-permute-start(s16[144,128]{1,0:T(8,128)(2,1)S(1)} %get-tuple-element.37), channel_id=1, source_target_pairs={{0,24},{1,25},{2,26},{3,27},{4,28},{5,29},{6,30},{7,31},{8,16},{9,... | collective-permute-start | bytes 110600 | tf_op jit(solution)/shard_map/ppermute | solution.py:39
  15.1 1.5 %collective-permute-done.8.refs_3_ = s16[144,128]{1,0:T(8,128)(2,1)S(1)} collective-permute-done((s16[144,128]{1,0:T(8,128)(2,1)S(1)}, s16[144,128]{1,0:T(8,128)(2,1)S(1)}, u32[]{:S(2)}, u32[]{:S(2)}) %collective-permute-start.8) | collective-permute-done | bytes 36896 | tf_op jit(solution)/shard_map/ppermute | solution.py:39
  16.6 1.0 %collective-permute-done.6.refs_1_ = s16[144,128]{1,0:T(8,128)(2,1)S(1)} collective-permute-done((s16[144,128]{1,0:T(8,128)(2,1)S(1)}, s16[144,128]{1,0:T(8,128)(2,1)S(1)}, u32[]{:S(2)}, u32[]{:S(2)}) %collective-permute-start.6) | collective-permute-done | bytes 36896 | tf_op jit(solution)/shard_map/ppermute | solution.py:39
  17.7 0.6 %collective-permute-start.10 = (s16[144,128]{1,0:T(8,128)(2,1)S(1)}, s16[144,128]{1,0:T(8,128)(2,1)S(1)}, u32[]{:S(2)}, u32[]{:S(2)}) collective-permute-start(s16[144,128]{1,0:T(8,128)(2,1)S(1)} %get-tuple-element.44), channel_id=1, source_target_pairs={{0,9},{1,8},{2,11},{3,10},{4,13},{5,12},{6,15},{7,14},{8,1},{9,0},... | collective-permute-start | bytes 110600 | tf_op jit(solution)/shard_map/ppermute | solution.py:50
  19.5 1.6 %collective-permute-done.10.even_ref = s16[144,128]{1,0:T(8,128)(2,1)S(1)} collective-permute-done((s16[144,128]{1,0:T(8,128)(2,1)S(1)}, s16[144,128]{1,0:T(8,128)(2,1)S(1)}, u32[]{:S(2)}, u32[]{:S(2)}) %collective-permute-start.10) | collective-permute-done | bytes 36896 | tf_op jit(solution)/shard_map/ppermute | solution.py:50
  21.1 1.4 %collective-permute-done.9.odd_ref = s16[144,128]{1,0:T(8,128)(2,1)S(1)} collective-permute-done((s16[144,128]{1,0:T(8,128)(2,1)S(1)}, s16[144,128]{1,0:T(8,128)(2,1)S(1)}, u32[]{:S(2)}, u32[]{:S(2)}) %collective-permute-start.9) | collective-permute-done | bytes 36896 | tf_op jit(solution)/shard_map/ppermute | solution.py:50
  23.1 0.9 %collective-permute-done.11.refs_1_ = bf16[2,2,2,32,128]{4,3,2,1,0:T(8,128)(2,1)S(1)} collective-permute-done((bf16[2,2,2,32,128]{4,3,2,1,0:T(8,128)(2,1)S(1)}, bf16[2,2,2,32,128]{4,3,2,1,0:T(8,128)(2,1)S(1)}, u32[]{:S(2)}, u32[]{:S(2)}) %collective-permute-start.11) | collective-permute-done | bytes 65568 | tf_op jit(solution)/shard_map/ppermute | solution.py:39
  24.0 0.5 %mirror.3 = (f32[2,2,32,128]{3,2,1,0:T(8,128)S(1)}, f32[2,2,32,128]{3,2,1,0:T(8,128)S(1)}, f32[8,32,128]{2,1,0:T(8,128)S(1)}) custom-call(s32[1]{0:T(128)S(6)} %copy.9.live_ref, s32[2,64]{1,0:T(2,128)S(4)} %get-tuple-element.30.index_ref, bf16[32,128,256]{2,1,0:T(8,128)(2,1)S(1)} %get-tuple-element.32.tile_ref, ...), custom_call_target="tpu_custom_call" | custom-call | flops 67108864 | bytes 2097152 | tf_op jit(solution)/shard_map/mirror/pallas_call | solution.py:23
  25.8 1.1 %collective-permute-start.13 = (s16[80,128]{1,0:T(8,128)(2,1)S(1)}, s16[80,128]{1,0:T(8,128)(2,1)S(1)}, u32[]{:S(2)}, u32[]{:S(2)}) collective-permute-start(s16[80,128]{1,0:T(8,128)(2,1)S(1)} %get-tuple-element.48), channel_id=1, source_target_pairs={{0,24},{1,25},{2,26},{3,27},{4,28},{5,29},{6,30},{7,31},{8,16},{9,... | collective-permute-start | bytes 61448 | tf_op jit(solution)/shard_map/ppermute | solution.py:39
  27.0 0.7 %collective-permute-start.17 = (s16[80,128]{1,0:T(8,128)(2,1)S(1)}, s16[80,128]{1,0:T(8,128)(2,1)S(1)}, u32[]{:S(2)}, u32[]{:S(2)}) collective-permute-start(s16[80,128]{1,0:T(8,128)(2,1)S(1)} %get-tuple-element.53), channel_id=1, source_target_pairs={{0,24},{1,25},{2,26},{3,27},{4,28},{5,29},{6,30},{7,31},{8,16},{9,... | collective-permute-start | bytes 61448 | tf_op jit(solution)/shard_map/ppermute | solution.py:39
  27.7 1.4 %collective-permute-done.13.refs_0_ = s16[80,128]{1,0:T(8,128)(2,1)S(1)} collective-permute-done((s16[80,128]{1,0:T(8,128)(2,1)S(1)}, s16[80,128]{1,0:T(8,128)(2,1)S(1)}, u32[]{:S(2)}, u32[]{:S(2)}) %collective-permute-start.13) | collective-permute-done | bytes 20512 | tf_op jit(solution)/shard_map/ppermute | solution.py:39
  29.1 1.2 %collective-permute-start.14 = (s16[80,128]{1,0:T(8,128)(2,1)S(1)}, s16[80,128]{1,0:T(8,128)(2,1)S(1)}, u32[]{:S(2)}, u32[]{:S(2)}) collective-permute-start(s16[80,128]{1,0:T(8,128)(2,1)S(1)} %owner.1), channel_id=1, source_target_pairs={{0,9},{1,8},{2,11},{3,10},{4,13},{5,12},{6,15},{7,14},{8,1},{9,0},... | collective-permute-start | bytes 61448 | tf_op jit(solution)/shard_map/ppermute | solution.py:50
  30.4 2.0 %collective-permute-done.14.even_ref = s16[80,128]{1,0:T(8,128)(2,1)S(1)} collective-permute-done((s16[80,128]{1,0:T(8,128)(2,1)S(1)}, s16[80,128]{1,0:T(8,128)(2,1)S(1)}, u32[]{:S(2)}, u32[]{:S(2)}) %collective-permute-start.14) | collective-permute-done | bytes 20512 | tf_op jit(solution)/shard_map/ppermute | solution.py:50
  32.4 2.1 %collective-permute-done.15.odd_ref = s16[80,128]{1,0:T(8,128)(2,1)S(1)} collective-permute-done((s16[80,128]{1,0:T(8,128)(2,1)S(1)}, s16[80,128]{1,0:T(8,128)(2,1)S(1)}, u32[]{:S(2)}, u32[]{:S(2)}) %collective-permute-start.15) | collective-permute-done | bytes 20512 | tf_op jit(solution)/shard_map/ppermute | solution.py:50
  34.5 0.6 %second.1 = (f32[32,256]{1,0:T(8,128)}, bf16[32,256]{1,0:T(8,128)(2,1)}) custom-call(f32[1]{0:T(128)S(6)} %copy.10.center_ref, f32[1]{0:T(128)S(6)} %copy.11.radius_ref, bf16[4,2,32,128]{3,2,1,0:T(8,128)(2,1)S(1)} %stack.1.refs_0_.own_ref, bf16[2,2,2,32,128]{4,3,2,1,0:T(8,128)(2,1)S(1)} %first.1.refs_0_.first_ref, ...), custom_call_target="tpu_custom_call" | custom-call | tf_op jit(solution)/shard_map/second/pallas_call | solution.py:23
  (26 shorter events, 4.1 us)
Async XLA Ops:
  0.6 4.6 %collective-permute-start = (bf16[32,256]{1,0:T(8,128)(2,1)}, bf16[32,256]{1,0:T(8,128)(2,1)S(1)}, u32[]{:S(2)}, u32[]{:S(2)}) collective-permute-start(bf16[32,256]{1,0:T(8,128)(2,1)} %vectors_hbm.1), channel_id=1, source_target_pairs={{0,8},{1,9},{2,10},{3,11},{4,12},{5,13},{6,14},{7,15},{8,0},{9,1},... | collective-permute-start | bytes 49160 | tf_op jit(solution)/shard_map/ppermute | solution.py:39
  1.4 3.9 %collective-permute-start.1 = (bf16[32,256]{1,0:T(8,128)(2,1)}, bf16[32,256]{1,0:T(8,128)(2,1)S(1)}, u32[]{:S(2)}, u32[]{:S(2)}) collective-permute-start(bf16[32,256]{1,0:T(8,128)(2,1)} %vectors_hbm.1), channel_id=1, source_target_pairs={{0,16},{1,17},{2,18},{3,19},{4,20},{5,21},{6,22},{7,23},{8,24},{9,... | collective-permute-start | bytes 49160 | tf_op jit(solution)/shard_map/ppermute | solution.py:39
  2.6 3.4 %collective-permute-start.2 = (bf16[32,256]{1,0:T(8,128)(2,1)}, bf16[32,256]{1,0:T(8,128)(2,1)S(1)}, u32[]{:S(2)}, u32[]{:S(2)}) collective-permute-start(bf16[32,256]{1,0:T(8,128)(2,1)} %vectors_hbm.1), channel_id=1, source_target_pairs={{0,24},{1,25},{2,26},{3,27},{4,28},{5,29},{6,30},{7,31},{8,16},{9,... | collective-permute-start | bytes 49160 | tf_op jit(solution)/shard_map/ppermute | solution.py:39
  6.0 4.1 %collective-permute-start.3 = (bf16[4,2,32,128]{3,2,1,0:T(8,128)(2,1)S(1)}, bf16[4,2,32,128]{3,2,1,0:T(8,128)(2,1)S(1)}, u32[]{:S(2)}, u32[]{:S(2)}) collective-permute-start(bf16[4,2,32,128]{3,2,1,0:T(8,128)(2,1)S(1)} %stack.1.refs_0_.own_ref), channel_id=1, source_target_pairs={{0,9},{1,8},{2,11},{3,10},{4,13},{5,12},{6,15},{7,14},{8,1},{9,0},... | collective-permute-start | bytes 196616 | tf_op jit(solution)/shard_map/ppermute | solution.py:50
  7.5 4.8 %collective-permute-start.4 = (bf16[4,2,32,128]{3,2,1,0:T(8,128)(2,1)S(1)}, bf16[4,2,32,128]{3,2,1,0:T(8,128)(2,1)S(1)}, u32[]{:S(2)}, u32[]{:S(2)}) collective-permute-start(bf16[4,2,32,128]{3,2,1,0:T(8,128)(2,1)S(1)} %stack.1.refs_0_.own_ref), channel_id=1, source_target_pairs={{0,8},{1,10},{2,9},{3,12},{4,11},{5,14},{6,13},{7,15},{8,0},{9,2},... | collective-permute-start | bytes 196616 | tf_op jit(solution)/shard_map/ppermute | solution.py:50
  8.9 4.2 %collective-permute-start.7 = (f32[2,2,32,128]{3,2,1,0:T(8,128)S(1)}, f32[2,2,32,128]{3,2,1,0:T(8,128)S(1)}, u32[]{:S(2)}, u32[]{:S(2)}) collective-permute-start(f32[2,2,32,128]{3,2,1,0:T(8,128)S(1)} %get-tuple-element.39), channel_id=1, source_target_pairs={{0,8},{1,9},{2,10},{3,11},{4,12},{5,13},{6,14},{7,15},{8,0},{9,1},... | collective-permute-start | bytes 196616 | tf_op jit(solution)/shard_map/ppermute | solution.py:39
  12.8 1.3 %collective-permute-start.5 = (f32[2,2,32,128]{3,2,1,0:T(8,128)S(1)}, f32[2,2,32,128]{3,2,1,0:T(8,128)S(1)}, u32[]{:S(2)}, u32[]{:S(2)}) collective-permute-start(f32[2,2,32,128]{3,2,1,0:T(8,128)S(1)} %get-tuple-element.35), channel_id=1, source_target_pairs={{0,8},{1,9},{2,10},{3,11},{4,12},{5,13},{6,14},{7,15},{8,0},{9,1},... | collective-permute-start | bytes 196616 | tf_op jit(solution)/shard_map/ppermute | solution.py:39
  13.1 3.4 %collective-permute-start.8 = (s16[144,128]{1,0:T(8,128)(2,1)S(1)}, s16[144,128]{1,0:T(8,128)(2,1)S(1)}, u32[]{:S(2)}, u32[]{:S(2)}) collective-permute-start(s16[144,128]{1,0:T(8,128)(2,1)S(1)} %get-tuple-element.41), channel_id=1, source_target_pairs={{0,24},{1,25},{2,26},{3,27},{4,28},{5,29},{6,30},{7,31},{8,16},{9,... | collective-permute-start | bytes 110600 | tf_op jit(solution)/shard_map/ppermute | solution.py:39
  14.2 3.4 %collective-permute-start.6 = (s16[144,128]{1,0:T(8,128)(2,1)S(1)}, s16[144,128]{1,0:T(8,128)(2,1)S(1)}, u32[]{:S(2)}, u32[]{:S(2)}) collective-permute-start(s16[144,128]{1,0:T(8,128)(2,1)S(1)} %get-tuple-element.37), channel_id=1, source_target_pairs={{0,24},{1,25},{2,26},{3,27},{4,28},{5,29},{6,30},{7,31},{8,16},{9,... | collective-permute-start | bytes 110600 | tf_op jit(solution)/shard_map/ppermute | solution.py:39
  17.7 3.4 %collective-permute-start.10 = (s16[144,128]{1,0:T(8,128)(2,1)S(1)}, s16[144,128]{1,0:T(8,128)(2,1)S(1)}, u32[]{:S(2)}, u32[]{:S(2)}) collective-permute-start(s16[144,128]{1,0:T(8,128)(2,1)S(1)} %get-tuple-element.44), channel_id=1, source_target_pairs={{0,9},{1,8},{2,11},{3,10},{4,13},{5,12},{6,15},{7,14},{8,1},{9,0},... | collective-permute-start | bytes 110600 | tf_op jit(solution)/shard_map/ppermute | solution.py:50
  18.2 4.3 %collective-permute-start.9 = (s16[144,128]{1,0:T(8,128)(2,1)S(1)}, s16[144,128]{1,0:T(8,128)(2,1)S(1)}, u32[]{:S(2)}, u32[]{:S(2)}) collective-permute-start(s16[144,128]{1,0:T(8,128)(2,1)S(1)} %get-tuple-element.43), channel_id=1, source_target_pairs={{0,8},{1,10},{2,9},{3,12},{4,11},{5,14},{6,13},{7,15},{8,0},{9,2},... | collective-permute-start | bytes 110600 | tf_op jit(solution)/shard_map/ppermute | solution.py:50
  22.6 1.3 %collective-permute-start.11 = (bf16[2,2,2,32,128]{4,3,2,1,0:T(8,128)(2,1)S(1)}, bf16[2,2,2,32,128]{4,3,2,1,0:T(8,128)(2,1)S(1)}, u32[]{:S(2)}, u32[]{:S(2)}) collective-permute-start(bf16[2,2,2,32,128]{4,3,2,1,0:T(8,128)(2,1)S(1)} %first.1.refs_0_.first_ref), channel_id=1, source_target_pairs={{0,8},{1,9},{2,10},{3,11},{4,12},{5,13},{6,14},{7,15},{8,0},{9,1},... | collective-permute-start | bytes 196616 | tf_op jit(solution)/shard_map/ppermute | solution.py:39
  24.5 1.3 %collective-permute-start.12 = (f32[2,2,32,128]{3,2,1,0:T(8,128)S(1)}, f32[2,2,32,128]{3,2,1,0:T(8,128)S(1)}, u32[]{:S(2)}, u32[]{:S(2)}) collective-permute-start(f32[2,2,32,128]{3,2,1,0:T(8,128)S(1)} %get-tuple-element.46), channel_id=1, source_target_pairs={{0,8},{1,9},{2,10},{3,11},{4,12},{5,13},{6,14},{7,15},{8,0},{9,1},... | collective-permute-start | bytes 196616 | tf_op jit(solution)/shard_map/ppermute | solution.py:39
  25.4 1.6 %collective-permute-start.16 = (f32[2,2,32,128]{3,2,1,0:T(8,128)S(1)}, f32[2,2,32,128]{3,2,1,0:T(8,128)S(1)}, u32[]{:S(2)}, u32[]{:S(2)}) collective-permute-start(f32[2,2,32,128]{3,2,1,0:T(8,128)S(1)} %get-tuple-element.51), channel_id=1, source_target_pairs={{0,8},{1,9},{2,10},{3,11},{4,12},{5,13},{6,14},{7,15},{8,0},{9,1},... | collective-permute-start | bytes 196616 | tf_op jit(solution)/shard_map/ppermute | solution.py:39
  25.8 3.3 %collective-permute-start.13 = (s16[80,128]{1,0:T(8,128)(2,1)S(1)}, s16[80,128]{1,0:T(8,128)(2,1)S(1)}, u32[]{:S(2)}, u32[]{:S(2)}) collective-permute-start(s16[80,128]{1,0:T(8,128)(2,1)S(1)} %get-tuple-element.48), channel_id=1, source_target_pairs={{0,24},{1,25},{2,26},{3,27},{4,28},{5,29},{6,30},{7,31},{8,16},{9,... | collective-permute-start | bytes 61448 | tf_op jit(solution)/shard_map/ppermute | solution.py:39
  27.0 3.4 %collective-permute-start.17 = (s16[80,128]{1,0:T(8,128)(2,1)S(1)}, s16[80,128]{1,0:T(8,128)(2,1)S(1)}, u32[]{:S(2)}, u32[]{:S(2)}) collective-permute-start(s16[80,128]{1,0:T(8,128)(2,1)S(1)} %get-tuple-element.53), channel_id=1, source_target_pairs={{0,24},{1,25},{2,26},{3,27},{4,28},{5,29},{6,30},{7,31},{8,16},{9,... | collective-permute-start | bytes 61448 | tf_op jit(solution)/shard_map/ppermute | solution.py:39
  29.1 3.3 %collective-permute-start.14 = (s16[80,128]{1,0:T(8,128)(2,1)S(1)}, s16[80,128]{1,0:T(8,128)(2,1)S(1)}, u32[]{:S(2)}, u32[]{:S(2)}) collective-permute-start(s16[80,128]{1,0:T(8,128)(2,1)S(1)} %owner.1), channel_id=1, source_target_pairs={{0,9},{1,8},{2,11},{3,10},{4,13},{5,12},{6,15},{7,14},{8,1},{9,0},... | collective-permute-start | bytes 61448 | tf_op jit(solution)/shard_map/ppermute | solution.py:50
  30.4 4.1 %collective-permute-start.15 = (s16[80,128]{1,0:T(8,128)(2,1)S(1)}, s16[80,128]{1,0:T(8,128)(2,1)S(1)}, u32[]{:S(2)}, u32[]{:S(2)}) collective-permute-start(s16[80,128]{1,0:T(8,128)(2,1)S(1)} %owner.1), channel_id=1, source_target_pairs={{0,8},{1,10},{2,9},{3,12},{4,11},{5,14},{6,13},{7,15},{8,0},{9,2},... | collective-permute-start | bytes 61448 | tf_op jit(solution)/shard_map/ppermute | solution.py:50

commit v9 on v8

--- a/solution.py
+++ b/solution.py
@@ -47,6 +47,12 @@
             other = c + 1 if c % 2 == odd else c - 1
             other = other if 0 <= other < cols else c
             route.append((r * cols + c, (r ^ 1) * cols + other))
+    return lax.ppermute(block, AXES, route)
+
+
+def shift_up(block):
+    rows, cols = lax.axis_size("row"), lax.axis_size("col")
+    route = [(r * cols + c, (r ^ 1) * cols + (c + 1) % cols) for r in range(rows) for c in range(cols)]
     return lax.ppermute(block, AXES, route)
 
 
@@ -285,24 +291,19 @@
     encode([total_of(own_ref, refs[:-1], b) for b in range(own_ref.shape[0])], refs[-1])
 
 
-def second_kernel(center_ref, radius_ref, own_ref, first_ref, even_ref, odd_ref, *refs):
-    (low_ref, *others), (out_ref, first_out_ref) = refs[:-2], refs[-2:]
+def second_kernel(center_ref, radius_ref, own_ref, first_ref, arrived_ref, low_ref, *refs):
+    others, (out_ref, first_out_ref) = refs[:-2], refs[-2:]
     col = lax.axis_index("col")
     center, radius = center_ref[0], radius_ref[0]
     blk, height, size = low_ref.shape
-
-    def finish(from_previous):
-        step = step_of(from_previous, height)
-        for b in range(blk):
-            arrived = jnp.where(col > 0, decode(from_previous, b, step), 0.0)
-            image = total_of(low_ref, others, b) + arrived
-            first = first_ref[0, 0, b].astype(F32)
-            second = 2.0 * (image - center * first) / radius - own_ref[0, b].astype(F32)
-            out_ref[:, b * size : (b + 1) * size] = second
-
+    step = step_of(arrived_ref, height)
     for b in range(blk):
-        first_out_ref[:, b * size : (b + 1) * size] = first_ref[0, 0, b]
-    by_parity(lambda: finish(odd_ref), lambda: finish(even_ref))
+        arrived = jnp.where(col > 0, decode(arrived_ref, b, step), 0.0)
+        image = total_of(low_ref, others, b) + arrived
+        first = first_ref[0, 0, b]
+        second = 2.0 * (image - center * first.astype(F32)) / radius - own_ref[0, b].astype(F32)
+        out_ref[:, b * size : (b + 1) * size] = second
+        first_out_ref[:, b * size : (b + 1) * size] = first
 
 
 def local(vectors, tile_data, tile_row, tile_offset, tile_live, damp_center, damp_radius):
@@ -417,8 +418,8 @@
         second_kernel,
         "second",
         [jax.ShapeDtypeStruct((count, width), F32), jax.ShapeDtypeStruct((count, width), BF16)],
-        [SMEM] * 2 + [VMEM] * (4 + members),
-        [damp_center, damp_radius, own, first, pair_swap(up, 0), pair_swap(up, 1), *low],
+        [SMEM] * 2 + [VMEM] * (3 + members),
+        [damp_center, damp_radius, own, first, shift_up(up), *low],
     )
     return first, second
 

time: 35.4 us -> 34.4 us (0.972)
  waiting for transfers between devices: 16.1 us -> 14.9 us
    ppermute x6 -> x4, waiting for transfers between devices: 10.1 us -> 6.04 us  [pair_swap(): return lax.ppermute(block, AXES, route)]
    ppermute x0 -> x1, waiting for transfers between devices: none -> 2.92 us  [shift_up(): return lax.ppermute(block, AXES, route)]
    ppermute x0 -> x1, starting transfers between devices: none -> 1.24 us  [shift_up(): return lax.ppermute(block, AXES, route)]
    ppermute x6 -> x4, starting transfers between devices: 3.48 us -> 2.26 us  [pair_swap(): return lax.ppermute(block, AXES, route)]
  transfers between devices with their start and end apart: 18 -> 17, of which waited for: 13 -> 12; matrix products, arithmetic and copies ran while one was open for 0% -> 0% of each run, Pallas kernels for 11% -> 11%
where the time goes in v9:
time: 34.4 us; the launch traced here: 34 us
  waiting for transfers between devices  14.9 us (43%)
  starting transfers between devices  11.2 us (33%)
  Pallas kernels  5.12 us (15%)
  between operations  2.71 us (8%)
    ppermute x12, starting transfers between devices, row_swap(): return lax.ppermute(block, AXES, route)  7.7 us
    ppermute x4, waiting for transfers between devices, pair_swap(): return lax.ppermute(block, AXES, route)  6.04 us
    ppermute x12, waiting for transfers between devices, row_swap(): return lax.ppermute(block, AXES, route)  6 us
    pallas_call x14, Pallas kernels, call(): pl.pallas_call(kernel, out_shape=list(outs), in_specs=list(places), out_s...  5.12 us
    ppermute x1, waiting for transfers between devices, shift_up(): return lax.ppermute(block, AXES, route)  2.92 us
    ppermute x4, starting transfers between devices, pair_swap(): return lax.ppermute(block, AXES, route)  2.26 us
    ppermute x1, starting transfers between devices, shift_up(): return lax.ppermute(block, AXES, route)  1.24 us
  transfers between devices with their start and end apart: 17, of which 12 were waited for; matrix products, arithmetic and copies ran while one was open for 0% of the time, Pallas kernels for 11%

profile of v9, /device:TPU:9, one launch (start us, length us, event | category | flops | bytes accessed | tf_op | source)
XLA Modules:
  0.0 34.0 jit_solution(16979563292876137389)
XLA Ops:
  0.6 0.7 %collective-permute-start = (bf16[32,256]{1,0:T(8,128)(2,1)}, bf16[32,256]{1,0:T(8,128)(2,1)S(1)}, u32[]{:S(2)}, u32[]{:S(2)}) collective-permute-start(bf16[32,256]{1,0:T(8,128)(2,1)} %vectors_hbm.1), channel_id=1, source_target_pairs={{0,8},{1,9},{2,10},{3,11},{4,12},{5,13},{6,14},{7,15},{8,0},{9,1},... | collective-permute-start | bytes 49160 | tf_op jit(solution)/shard_map/ppermute | solution.py:39
  1.4 1.3 %collective-permute-start.1 = (bf16[32,256]{1,0:T(8,128)(2,1)}, bf16[32,256]{1,0:T(8,128)(2,1)S(1)}, u32[]{:S(2)}, u32[]{:S(2)}) collective-permute-start(bf16[32,256]{1,0:T(8,128)(2,1)} %vectors_hbm.1), channel_id=1, source_target_pairs={{0,16},{1,17},{2,18},{3,19},{4,20},{5,21},{6,22},{7,23},{8,24},{9,... | collective-permute-start | bytes 49160 | tf_op jit(solution)/shard_map/ppermute | solution.py:39
  3.1 2.2 %load.1 = (bf16[32,256]{1,0:T(8,128)(2,1)S(1)}, bf16[32,128,256]{2,1,0:T(8,128)(2,1)S(1)}, bf16[32,128,256]{2,1,0:T(8,128)(2,1)S(1)}, s32[2,64]{1,0:T(2,128)S(4)}) custom-call(s32[1,64]{1,0:T(1,128)} %bitcast.4, s32[1,64]{1,0:T(1,128)} %bitcast.5, bf16[32,256]{1,0:T(8,128)(2,1)} %vectors_hbm.1, bf16[32,2,128,128]{3,2,1,0:T(8,128)(2,1)} %bitcast.3), custom_call_target="tpu_custom_call" | custom-call | bytes 6291456 | tf_op jit(solution)/shard_map/load/pallas_call | solution.py:23
  5.3 0.7 %collective-permute-done.2.refs_3_ = bf16[32,256]{1,0:T(8,128)(2,1)S(1)} collective-permute-done((bf16[32,256]{1,0:T(8,128)(2,1)}, bf16[32,256]{1,0:T(8,128)(2,1)S(1)}, u32[]{:S(2)}, u32[]{:S(2)}) %collective-permute-start.2) | collective-permute-done | bytes 16416 | tf_op jit(solution)/shard_map/ppermute | solution.py:39
  6.0 1.5 %collective-permute-start.3 = (bf16[4,2,32,128]{3,2,1,0:T(8,128)(2,1)S(1)}, bf16[4,2,32,128]{3,2,1,0:T(8,128)(2,1)S(1)}, u32[]{:S(2)}, u32[]{:S(2)}) collective-permute-start(bf16[4,2,32,128]{3,2,1,0:T(8,128)(2,1)S(1)} %stack.1.refs_0_.own_ref), channel_id=1, source_target_pairs={{0,9},{1,8},{2,11},{3,10},{4,13},{5,12},{6,15},{7,14},{8,1},{9,0},... | collective-permute-start | bytes 196616 | tf_op jit(solution)/shard_map/ppermute | solution.py:50
  8.4 0.5 %mirror.2 = (f32[2,2,32,128]{3,2,1,0:T(8,128)S(1)}, f32[2,2,32,128]{3,2,1,0:T(8,128)S(1)}, f32[8,32,128]{2,1,0:T(8,128)S(1)}) custom-call(s32[1]{0:T(128)S(6)} %copy.9.live_ref, s32[2,64]{1,0:T(2,128)S(4)} %get-tuple-element.30.index_ref, bf16[32,128,256]{2,1,0:T(8,128)(2,1)S(1)} %get-tuple-element.32.tile_ref, bf16[4,2,32,128]{3,2,1,0:T(8,128)(2,1)S(1)} %stack.1.refs_0_.own_ref), custom_call_target="tpu_custom_call" | custom-call | flops 67108864 | bytes 2097152 | tf_op jit(solution)/shard_map/mirror/pallas_call | solution.py:23
  9.3 0.9 %collective-permute-done.3.refs_1_.own_even_ref = bf16[4,2,32,128]{3,2,1,0:T(8,128)(2,1)S(1)} collective-permute-done((bf16[4,2,32,128]{3,2,1,0:T(8,128)(2,1)S(1)}, bf16[4,2,32,128]{3,2,1,0:T(8,128)(2,1)S(1)}, u32[]{:S(2)}, u32[]{:S(2)}) %collective-permute-start.3) | collective-permute-done | bytes 65568 | tf_op jit(solution)/shard_map/ppermute | solution.py:50
  10.2 2.1 %collective-permute-done.4.refs_2_.own_odd_ref = bf16[4,2,32,128]{3,2,1,0:T(8,128)(2,1)S(1)} collective-permute-done((bf16[4,2,32,128]{3,2,1,0:T(8,128)(2,1)S(1)}, bf16[4,2,32,128]{3,2,1,0:T(8,128)(2,1)S(1)}, u32[]{:S(2)}, u32[]{:S(2)}) %collective-permute-start.4) | collective-permute-done | bytes 65568 | tf_op jit(solution)/shard_map/ppermute | solution.py:50
  12.3 0.5 %direct.2 = (f32[2,2,32,128]{3,2,1,0:T(8,128)S(1)}, f32[2,2,32,128]{3,2,1,0:T(8,128)S(1)}) custom-call(s32[1]{0:T(128)S(6)} %copy.9.live_ref, s32[2,64]{1,0:T(2,128)S(4)} %get-tuple-element.30.index_ref, bf16[32,128,256]{2,1,0:T(8,128)(2,1)S(1)} %get-tuple-element.31.flipped_ref, f32[8,32,128]{2,1,0:T(8,128)S(1)} %get-tuple-element.33.low_ref, ...), custom_call_target="tpu_custom_call" | custom-call | flops 67108864 | bytes 2097152 | tf_op jit(solution)/shard_map/direct/pallas_call | solution.py:23
  13.1 0.8 %collective-permute-start.8 = (s16[144,128]{1,0:T(8,128)(2,1)S(1)}, s16[144,128]{1,0:T(8,128)(2,1)S(1)}, u32[]{:S(2)}, u32[]{:S(2)}) collective-permute-start(s16[144,128]{1,0:T(8,128)(2,1)S(1)} %get-tuple-element.41), channel_id=1, source_target_pairs={{0,24},{1,25},{2,26},{3,27},{4,28},{5,29},{6,30},{7,31},{8,16},{9,... | collective-permute-start | bytes 110600 | tf_op jit(solution)/shard_map/ppermute | solution.py:39
  14.2 0.9 %collective-permute-start.6 = (s16[144,128]{1,0:T(8,128)(2,1)S(1)}, s16[144,128]{1,0:T(8,128)(2,1)S(1)}, u32[]{:S(2)}, u32[]{:S(2)}) collective-permute-start(s16[144,128]{1,0:T(8,128)(2,1)S(1)} %get-tuple-element.37), channel_id=1, source_target_pairs={{0,24},{1,25},{2,26},{3,27},{4,28},{5,29},{6,30},{7,31},{8,16},{9,... | collective-permute-start | bytes 110600 | tf_op jit(solution)/shard_map/ppermute | solution.py:39
  15.1 1.5 %collective-permute-done.8.refs_3_ = s16[144,128]{1,0:T(8,128)(2,1)S(1)} collective-permute-done((s16[144,128]{1,0:T(8,128)(2,1)S(1)}, s16[144,128]{1,0:T(8,128)(2,1)S(1)}, u32[]{:S(2)}, u32[]{:S(2)}) %collective-permute-start.8) | collective-permute-done | bytes 36896 | tf_op jit(solution)/shard_map/ppermute | solution.py:39
  16.6 1.0 %collective-permute-done.6.refs_1_ = s16[144,128]{1,0:T(8,128)(2,1)S(1)} collective-permute-done((s16[144,128]{1,0:T(8,128)(2,1)S(1)}, s16[144,128]{1,0:T(8,128)(2,1)S(1)}, u32[]{:S(2)}, u32[]{:S(2)}) %collective-permute-start.6) | collective-permute-done | bytes 36896 | tf_op jit(solution)/shard_map/ppermute | solution.py:39
  17.7 0.6 %collective-permute-start.10 = (s16[144,128]{1,0:T(8,128)(2,1)S(1)}, s16[144,128]{1,0:T(8,128)(2,1)S(1)}, u32[]{:S(2)}, u32[]{:S(2)}) collective-permute-start(s16[144,128]{1,0:T(8,128)(2,1)S(1)} %get-tuple-element.44), channel_id=1, source_target_pairs={{0,9},{1,8},{2,11},{3,10},{4,13},{5,12},{6,15},{7,14},{8,1},{9,0},... | collective-permute-start | bytes 110600 | tf_op jit(solution)/shard_map/ppermute | solution.py:50
  19.6 1.6 %collective-permute-done.10.even_ref = s16[144,128]{1,0:T(8,128)(2,1)S(1)} collective-permute-done((s16[144,128]{1,0:T(8,128)(2,1)S(1)}, s16[144,128]{1,0:T(8,128)(2,1)S(1)}, u32[]{:S(2)}, u32[]{:S(2)}) %collective-permute-start.10) | collective-permute-done | bytes 36896 | tf_op jit(solution)/shard_map/ppermute | solution.py:50
  21.2 1.4 %collective-permute-done.9.odd_ref = s16[144,128]{1,0:T(8,128)(2,1)S(1)} collective-permute-done((s16[144,128]{1,0:T(8,128)(2,1)S(1)}, s16[144,128]{1,0:T(8,128)(2,1)S(1)}, u32[]{:S(2)}, u32[]{:S(2)}) %collective-permute-start.9) | collective-permute-done | bytes 36896 | tf_op jit(solution)/shard_map/ppermute | solution.py:50
  23.1 0.9 %collective-permute-done.11.refs_1_ = bf16[2,2,2,32,128]{4,3,2,1,0:T(8,128)(2,1)S(1)} collective-permute-done((bf16[2,2,2,32,128]{4,3,2,1,0:T(8,128)(2,1)S(1)}, bf16[2,2,2,32,128]{4,3,2,1,0:T(8,128)(2,1)S(1)}, u32[]{:S(2)}, u32[]{:S(2)}) %collective-permute-start.11) | collective-permute-done | bytes 65568 | tf_op jit(solution)/shard_map/ppermute | solution.py:39
  24.0 0.5 %mirror.3 = (f32[2,2,32,128]{3,2,1,0:T(8,128)S(1)}, f32[2,2,32,128]{3,2,1,0:T(8,128)S(1)}, f32[8,32,128]{2,1,0:T(8,128)S(1)}) custom-call(s32[1]{0:T(128)S(6)} %copy.9.live_ref, s32[2,64]{1,0:T(2,128)S(4)} %get-tuple-element.30.index_ref, bf16[32,128,256]{2,1,0:T(8,128)(2,1)S(1)} %get-tuple-element.32.tile_ref, ...), custom_call_target="tpu_custom_call" | custom-call | flops 67108864 | bytes 2097152 | tf_op jit(solution)/shard_map/mirror/pallas_call | solution.py:23
  25.9 1.0 %collective-permute-start.13 = (s16[80,128]{1,0:T(8,128)(2,1)S(1)}, s16[80,128]{1,0:T(8,128)(2,1)S(1)}, u32[]{:S(2)}, u32[]{:S(2)}) collective-permute-start(s16[80,128]{1,0:T(8,128)(2,1)S(1)} %get-tuple-element.48), channel_id=1, source_target_pairs={{0,24},{1,25},{2,26},{3,27},{4,28},{5,29},{6,30},{7,31},{8,16},{9,... | collective-permute-start | bytes 61448 | tf_op jit(solution)/shard_map/ppermute | solution.py:39
  26.9 0.9 %collective-permute-start.16 = (s16[80,128]{1,0:T(8,128)(2,1)S(1)}, s16[80,128]{1,0:T(8,128)(2,1)S(1)}, u32[]{:S(2)}, u32[]{:S(2)}) collective-permute-start(s16[80,128]{1,0:T(8,128)(2,1)S(1)} %get-tuple-element.53), channel_id=1, source_target_pairs={{0,24},{1,25},{2,26},{3,27},{4,28},{5,29},{6,30},{7,31},{8,16},{9,... | collective-permute-start | bytes 61448 | tf_op jit(solution)/shard_map/ppermute | solution.py:39
  27.8 1.4 %collective-permute-done.13.refs_0_ = s16[80,128]{1,0:T(8,128)(2,1)S(1)} collective-permute-done((s16[80,128]{1,0:T(8,128)(2,1)S(1)}, s16[80,128]{1,0:T(8,128)(2,1)S(1)}, u32[]{:S(2)}, u32[]{:S(2)}) %collective-permute-start.13) | collective-permute-done | bytes 20512 | tf_op jit(solution)/shard_map/ppermute | solution.py:39
  29.2 1.2 %collective-permute-start.14 = (s16[80,128]{1,0:T(8,128)(2,1)S(1)}, s16[80,128]{1,0:T(8,128)(2,1)S(1)}, u32[]{:S(2)}, u32[]{:S(2)}) collective-permute-start(s16[80,128]{1,0:T(8,128)(2,1)S(1)} %owner.1), channel_id=1, source_target_pairs={{0,9},{1,10},{2,11},{3,12},{4,13},{5,14},{6,15},{7,8},{8,1},{9,2},... | collective-permute-start | bytes 61448 | tf_op jit(solution)/shard_map/ppermute | solution.py:56
  30.4 2.9 %collective-permute-done.14.arrived_ref = s16[80,128]{1,0:T(8,128)(2,1)S(1)} collective-permute-done((s16[80,128]{1,0:T(8,128)(2,1)S(1)}, s16[80,128]{1,0:T(8,128)(2,1)S(1)}, u32[]{:S(2)}, u32[]{:S(2)}) %collective-permute-start.14) | collective-permute-done | bytes 20512 | tf_op jit(solution)/shard_map/ppermute | solution.py:56
  33.3 0.6 %second.1 = (f32[32,256]{1,0:T(8,128)}, bf16[32,256]{1,0:T(8,128)(2,1)}) custom-call(f32[1]{0:T(128)S(6)} %copy.10.center_ref, f32[1]{0:T(128)S(6)} %copy.11.radius_ref, bf16[4,2,32,128]{3,2,1,0:T(8,128)(2,1)S(1)} %stack.1.refs_0_.own_ref, bf16[2,2,2,32,128]{4,3,2,1,0:T(8,128)(2,1)S(1)} %first.1.refs_0_.first_ref, ...), custom_call_target="tpu_custom_call" | custom-call | tf_op jit(solution)/shard_map/second/pallas_call | solution.py:23
  (24 shorter events, 3.6 us)
Async XLA Ops:
  0.6 4.6 %collective-permute-start = (bf16[32,256]{1,0:T(8,128)(2,1)}, bf16[32,256]{1,0:T(8,128)(2,1)S(1)}, u32[]{:S(2)}, u32[]{:S(2)}) collective-permute-start(bf16[32,256]{1,0:T(8,128)(2,1)} %vectors_hbm.1), channel_id=1, source_target_pairs={{0,8},{1,9},{2,10},{3,11},{4,12},{5,13},{6,14},{7,15},{8,0},{9,1},... | collective-permute-start | bytes 49160 | tf_op jit(solution)/shard_map/ppermute | solution.py:39
  1.4 3.9 %collective-permute-start.1 = (bf16[32,256]{1,0:T(8,128)(2,1)}, bf16[32,256]{1,0:T(8,128)(2,1)S(1)}, u32[]{:S(2)}, u32[]{:S(2)}) collective-permute-start(bf16[32,256]{1,0:T(8,128)(2,1)} %vectors_hbm.1), channel_id=1, source_target_pairs={{0,16},{1,17},{2,18},{3,19},{4,20},{5,21},{6,22},{7,23},{8,24},{9,... | collective-permute-start | bytes 49160 | tf_op jit(solution)/shard_map/ppermute | solution.py:39
  2.6 3.4 %collective-permute-start.2 = (bf16[32,256]{1,0:T(8,128)(2,1)}, bf16[32,256]{1,0:T(8,128)(2,1)S(1)}, u32[]{:S(2)}, u32[]{:S(2)}) collective-permute-start(bf16[32,256]{1,0:T(8,128)(2,1)} %vectors_hbm.1), channel_id=1, source_target_pairs={{0,24},{1,25},{2,26},{3,27},{4,28},{5,29},{6,30},{7,31},{8,16},{9,... | collective-permute-start | bytes 49160 | tf_op jit(solution)/shard_map/ppermute | solution.py:39
  6.0 4.1 %collective-permute-start.3 = (bf16[4,2,32,128]{3,2,1,0:T(8,128)(2,1)S(1)}, bf16[4,2,32,128]{3,2,1,0:T(8,128)(2,1)S(1)}, u32[]{:S(2)}, u32[]{:S(2)}) collective-permute-start(bf16[4,2,32,128]{3,2,1,0:T(8,128)(2,1)S(1)} %stack.1.refs_0_.own_ref), channel_id=1, source_target_pairs={{0,9},{1,8},{2,11},{3,10},{4,13},{5,12},{6,15},{7,14},{8,1},{9,0},... | collective-permute-start | bytes 196616 | tf_op jit(solution)/shard_map/ppermute | solution.py:50
  7.5 4.8 %collective-permute-start.4 = (bf16[4,2,32,128]{3,2,1,0:T(8,128)(2,1)S(1)}, bf16[4,2,32,128]{3,2,1,0:T(8,128)(2,1)S(1)}, u32[]{:S(2)}, u32[]{:S(2)}) collective-permute-start(bf16[4,2,32,128]{3,2,1,0:T(8,128)(2,1)S(1)} %stack.1.refs_0_.own_ref), channel_id=1, source_target_pairs={{0,8},{1,10},{2,9},{3,12},{4,11},{5,14},{6,13},{7,15},{8,0},{9,2},... | collective-permute-start | bytes 196616 | tf_op jit(solution)/shard_map/ppermute | solution.py:50
  8.9 4.2 %collective-permute-start.7 = (f32[2,2,32,128]{3,2,1,0:T(8,128)S(1)}, f32[2,2,32,128]{3,2,1,0:T(8,128)S(1)}, u32[]{:S(2)}, u32[]{:S(2)}) collective-permute-start(f32[2,2,32,128]{3,2,1,0:T(8,128)S(1)} %get-tuple-element.39), channel_id=1, source_target_pairs={{0,8},{1,9},{2,10},{3,11},{4,12},{5,13},{6,14},{7,15},{8,0},{9,1},... | collective-permute-start | bytes 196616 | tf_op jit(solution)/shard_map/ppermute | solution.py:39
  12.8 1.3 %collective-permute-start.5 = (f32[2,2,32,128]{3,2,1,0:T(8,128)S(1)}, f32[2,2,32,128]{3,2,1,0:T(8,128)S(1)}, u32[]{:S(2)}, u32[]{:S(2)}) collective-permute-start(f32[2,2,32,128]{3,2,1,0:T(8,128)S(1)} %get-tuple-element.35), channel_id=1, source_target_pairs={{0,8},{1,9},{2,10},{3,11},{4,12},{5,13},{6,14},{7,15},{8,0},{9,1},... | collective-permute-start | bytes 196616 | tf_op jit(solution)/shard_map/ppermute | solution.py:39
  13.1 3.4 %collective-permute-start.8 = (s16[144,128]{1,0:T(8,128)(2,1)S(1)}, s16[144,128]{1,0:T(8,128)(2,1)S(1)}, u32[]{:S(2)}, u32[]{:S(2)}) collective-permute-start(s16[144,128]{1,0:T(8,128)(2,1)S(1)} %get-tuple-element.41), channel_id=1, source_target_pairs={{0,24},{1,25},{2,26},{3,27},{4,28},{5,29},{6,30},{7,31},{8,16},{9,... | collective-permute-start | bytes 110600 | tf_op jit(solution)/shard_map/ppermute | solution.py:39
  14.2 3.4 %collective-permute-start.6 = (s16[144,128]{1,0:T(8,128)(2,1)S(1)}, s16[144,128]{1,0:T(8,128)(2,1)S(1)}, u32[]{:S(2)}, u32[]{:S(2)}) collective-permute-start(s16[144,128]{1,0:T(8,128)(2,1)S(1)} %get-tuple-element.37), channel_id=1, source_target_pairs={{0,24},{1,25},{2,26},{3,27},{4,28},{5,29},{6,30},{7,31},{8,16},{9,... | collective-permute-start | bytes 110600 | tf_op jit(solution)/shard_map/ppermute | solution.py:39
  17.7 3.4 %collective-permute-start.10 = (s16[144,128]{1,0:T(8,128)(2,1)S(1)}, s16[144,128]{1,0:T(8,128)(2,1)S(1)}, u32[]{:S(2)}, u32[]{:S(2)}) collective-permute-start(s16[144,128]{1,0:T(8,128)(2,1)S(1)} %get-tuple-element.44), channel_id=1, source_target_pairs={{0,9},{1,8},{2,11},{3,10},{4,13},{5,12},{6,15},{7,14},{8,1},{9,0},... | collective-permute-start | bytes 110600 | tf_op jit(solution)/shard_map/ppermute | solution.py:50
  18.3 4.3 %collective-permute-start.9 = (s16[144,128]{1,0:T(8,128)(2,1)S(1)}, s16[144,128]{1,0:T(8,128)(2,1)S(1)}, u32[]{:S(2)}, u32[]{:S(2)}) collective-permute-start(s16[144,128]{1,0:T(8,128)(2,1)S(1)} %get-tuple-element.43), channel_id=1, source_target_pairs={{0,8},{1,10},{2,9},{3,12},{4,11},{5,14},{6,13},{7,15},{8,0},{9,2},... | collective-permute-start | bytes 110600 | tf_op jit(solution)/shard_map/ppermute | solution.py:50
  22.7 1.3 %collective-permute-start.11 = (bf16[2,2,2,32,128]{4,3,2,1,0:T(8,128)(2,1)S(1)}, bf16[2,2,2,32,128]{4,3,2,1,0:T(8,128)(2,1)S(1)}, u32[]{:S(2)}, u32[]{:S(2)}) collective-permute-start(bf16[2,2,2,32,128]{4,3,2,1,0:T(8,128)(2,1)S(1)} %first.1.refs_0_.first_ref), channel_id=1, source_target_pairs={{0,8},{1,9},{2,10},{3,11},{4,12},{5,13},{6,14},{7,15},{8,0},{9,1},... | collective-permute-start | bytes 196616 | tf_op jit(solution)/shard_map/ppermute | solution.py:39
  24.5 1.3 %collective-permute-start.12 = (f32[2,2,32,128]{3,2,1,0:T(8,128)S(1)}, f32[2,2,32,128]{3,2,1,0:T(8,128)S(1)}, u32[]{:S(2)}, u32[]{:S(2)}) collective-permute-start(f32[2,2,32,128]{3,2,1,0:T(8,128)S(1)} %get-tuple-element.46), channel_id=1, source_target_pairs={{0,8},{1,9},{2,10},{3,11},{4,12},{5,13},{6,14},{7,15},{8,0},{9,1},... | collective-permute-start | bytes 196616 | tf_op jit(solution)/shard_map/ppermute | solution.py:39
  25.4 1.5 %collective-permute-start.15 = (f32[2,2,32,128]{3,2,1,0:T(8,128)S(1)}, f32[2,2,32,128]{3,2,1,0:T(8,128)S(1)}, u32[]{:S(2)}, u32[]{:S(2)}) collective-permute-start(f32[2,2,32,128]{3,2,1,0:T(8,128)S(1)} %get-tuple-element.51), channel_id=1, source_target_pairs={{0,8},{1,9},{2,10},{3,11},{4,12},{5,13},{6,14},{7,15},{8,0},{9,1},... | collective-permute-start | bytes 196616 | tf_op jit(solution)/shard_map/ppermute | solution.py:39
  25.9 3.3 %collective-permute-start.13 = (s16[80,128]{1,0:T(8,128)(2,1)S(1)}, s16[80,128]{1,0:T(8,128)(2,1)S(1)}, u32[]{:S(2)}, u32[]{:S(2)}) collective-permute-start(s16[80,128]{1,0:T(8,128)(2,1)S(1)} %get-tuple-element.48), channel_id=1, source_target_pairs={{0,24},{1,25},{2,26},{3,27},{4,28},{5,29},{6,30},{7,31},{8,16},{9,... | collective-permute-start | bytes 61448 | tf_op jit(solution)/shard_map/ppermute | solution.py:39
  26.9 3.5 %collective-permute-start.16 = (s16[80,128]{1,0:T(8,128)(2,1)S(1)}, s16[80,128]{1,0:T(8,128)(2,1)S(1)}, u32[]{:S(2)}, u32[]{:S(2)}) collective-permute-start(s16[80,128]{1,0:T(8,128)(2,1)S(1)} %get-tuple-element.53), channel_id=1, source_target_pairs={{0,24},{1,25},{2,26},{3,27},{4,28},{5,29},{6,30},{7,31},{8,16},{9,... | collective-permute-start | bytes 61448 | tf_op jit(solution)/shard_map/ppermute | solution.py:39
  29.2 4.2 %collective-permute-start.14 = (s16[80,128]{1,0:T(8,128)(2,1)S(1)}, s16[80,128]{1,0:T(8,128)(2,1)S(1)}, u32[]{:S(2)}, u32[]{:S(2)}) collective-permute-start(s16[80,128]{1,0:T(8,128)(2,1)S(1)} %owner.1), channel_id=1, source_target_pairs={{0,9},{1,10},{2,11},{3,12},{4,13},{5,14},{6,15},{7,8},{8,1},{9,2},... | collective-permute-start | bytes 61448 | tf_op jit(solution)/shard_map/ppermute | solution.py:56

commit v10 on v9

--- a/solution.py
+++ b/solution.py
@@ -139,7 +139,7 @@
 def stack_kernel(*refs):
     parts, out_ref = refs[:-1], refs[-1]
     size = out_ref.shape[-1]
-    for s, part in enumerate(parts):
+    for s, part in zip((0, *range(len(parts) - 1, 0, -1)), parts):
         for b in range(out_ref.shape[1]):
             out_ref[s, b] = part[:, b * size : (b + 1) * size]
 
@@ -371,7 +371,7 @@
         return (keep_up, got_up), (keep_low, row_swap(send_low, 1))
 
     (own,) = call(
-        stack_kernel, "stack", [shape(BF16, rows, blk)], [VMEM] * rows, [vectors, *sent]
+        stack_kernel, "stack", [shape(BF16, rows, blk)], [VMEM] * rows, [vectors, *sent[::-1]]
     )
     arrived = [pair_swap(own, 0), pair_swap(own, 1)]
     up, low = apply([own], [list(range(rows))], arrived)

time: 34.4 us -> 34 us (0.988)
  waiting for transfers between devices: 14.9 us -> 14.2 us
    ppermute x12, waiting for transfers between devices: 6 us -> 5.62 us  [row_swap(): return lax.ppermute(block, AXES, route)]
where the time goes in v10:
time: 34 us; the launch traced here: 33.6 us
  waiting for transfers between devices  14.2 us (42%)
  starting transfers between devices  11.5 us (34%)
  Pallas kernels  5.1 us (15%)
  between operations  2.72 us (8%)
    ppermute x12, starting transfers between devices, row_swap(): return lax.ppermute(block, AXES, route)  7.54 us
    ppermute x4, waiting for transfers between devices, pair_swap(): return lax.ppermute(block, AXES, route)  5.87 us
    ppermute x12, waiting for transfers between devices, row_swap(): return lax.ppermute(block, AXES, route)  5.62 us
    pallas_call x14, Pallas kernels, call(): pl.pallas_call(kernel, out_shape=list(outs), in_specs=list(places), out_s...  5.1 us
    ppermute x1, waiting for transfers between devices, shift_up(): return lax.ppermute(block, AXES, route)  2.74 us
    ppermute x4, starting transfers between devices, pair_swap(): return lax.ppermute(block, AXES, route)  2.59 us
    ppermute x1, starting transfers between devices, shift_up(): return lax.ppermute(block, AXES, route)  1.42 us
  transfers between devices with their start and end apart: 17, of which 12 were waited for; matrix products, arithmetic and copies ran while one was open for 0% of the time, Pallas kernels for 11%

profile of v10, /device:TPU:9, one launch (start us, length us, event | category | flops | bytes accessed | tf_op | source)
XLA Modules:
  0.0 33.6 jit_solution(13687860979384491362)
XLA Ops:
  0.6 1.9 %collective-permute-start = (bf16[32,256]{1,0:T(8,128)(2,1)}, bf16[32,256]{1,0:T(8,128)(2,1)S(1)}, u32[]{:S(2)}, u32[]{:S(2)}) collective-permute-start(bf16[32,256]{1,0:T(8,128)(2,1)} %vectors_hbm.1), channel_id=1, source_target_pairs={{0,24},{1,25},{2,26},{3,27},{4,28},{5,29},{6,30},{7,31},{8,16},{9,... | collective-permute-start | bytes 49160 | tf_op jit(solution)/shard_map/ppermute | solution.py:39
  3.0 2.2 %load.1 = (bf16[32,256]{1,0:T(8,128)(2,1)S(1)}, bf16[32,128,256]{2,1,0:T(8,128)(2,1)S(1)}, bf16[32,128,256]{2,1,0:T(8,128)(2,1)S(1)}, s32[2,64]{1,0:T(2,128)S(4)}) custom-call(s32[1,64]{1,0:T(1,128)} %bitcast.4, s32[1,64]{1,0:T(1,128)} %bitcast.5, bf16[32,256]{1,0:T(8,128)(2,1)} %vectors_hbm.1, bf16[32,2,128,128]{3,2,1,0:T(8,128)(2,1)} %bitcast.3), custom_call_target="tpu_custom_call" | custom-call | bytes 6291456 | tf_op jit(solution)/shard_map/load/pallas_call | solution.py:23
  5.3 2.1 %collective-permute-start.3 = (bf16[4,2,32,128]{3,2,1,0:T(8,128)(2,1)S(1)}, bf16[4,2,32,128]{3,2,1,0:T(8,128)(2,1)S(1)}, u32[]{:S(2)}, u32[]{:S(2)}) collective-permute-start(bf16[4,2,32,128]{3,2,1,0:T(8,128)(2,1)S(1)} %stack.1.refs_0_.own_ref), channel_id=1, source_target_pairs={{0,9},{1,8},{2,11},{3,10},{4,13},{5,12},{6,15},{7,14},{8,1},{9,0},... | collective-permute-start | bytes 196616 | tf_op jit(solution)/shard_map/ppermute | solution.py:50
  8.1 0.5 %mirror.2 = (f32[2,2,32,128]{3,2,1,0:T(8,128)S(1)}, f32[2,2,32,128]{3,2,1,0:T(8,128)S(1)}, f32[8,32,128]{2,1,0:T(8,128)S(1)}) custom-call(s32[1]{0:T(128)S(6)} %copy.9.live_ref, s32[2,64]{1,0:T(2,128)S(4)} %get-tuple-element.30.index_ref, bf16[32,128,256]{2,1,0:T(8,128)(2,1)S(1)} %get-tuple-element.32.tile_ref, bf16[4,2,32,128]{3,2,1,0:T(8,128)(2,1)S(1)} %stack.1.refs_0_.own_ref), custom_call_target="tpu_custom_call" | custom-call | flops 67108864 | bytes 2097152 | tf_op jit(solution)/shard_map/mirror/pallas_call | solution.py:23
  8.6 0.6 %collective-permute-start.7 = (f32[2,2,32,128]{3,2,1,0:T(8,128)S(1)}, f32[2,2,32,128]{3,2,1,0:T(8,128)S(1)}, u32[]{:S(2)}, u32[]{:S(2)}) collective-permute-start(f32[2,2,32,128]{3,2,1,0:T(8,128)S(1)} %get-tuple-element.39), channel_id=1, source_target_pairs={{0,8},{1,9},{2,10},{3,11},{4,12},{5,13},{6,14},{7,15},{8,0},{9,1},... | collective-permute-start | bytes 196616 | tf_op jit(solution)/shard_map/ppermute | solution.py:39
  9.2 1.1 %collective-permute-done.3.refs_1_.own_even_ref = bf16[4,2,32,128]{3,2,1,0:T(8,128)(2,1)S(1)} collective-permute-done((bf16[4,2,32,128]{3,2,1,0:T(8,128)(2,1)S(1)}, bf16[4,2,32,128]{3,2,1,0:T(8,128)(2,1)S(1)}, u32[]{:S(2)}, u32[]{:S(2)}) %collective-permute-start.3) | collective-permute-done | bytes 65568 | tf_op jit(solution)/shard_map/ppermute | solution.py:50
  10.3 1.7 %collective-permute-done.4.refs_2_.own_odd_ref = bf16[4,2,32,128]{3,2,1,0:T(8,128)(2,1)S(1)} collective-permute-done((bf16[4,2,32,128]{3,2,1,0:T(8,128)(2,1)S(1)}, bf16[4,2,32,128]{3,2,1,0:T(8,128)(2,1)S(1)}, u32[]{:S(2)}, u32[]{:S(2)}) %collective-permute-start.4) | collective-permute-done | bytes 65568 | tf_op jit(solution)/shard_map/ppermute | solution.py:50
  12.1 0.5 %direct.2 = (f32[2,2,32,128]{3,2,1,0:T(8,128)S(1)}, f32[2,2,32,128]{3,2,1,0:T(8,128)S(1)}) custom-call(s32[1]{0:T(128)S(6)} %copy.9.live_ref, s32[2,64]{1,0:T(2,128)S(4)} %get-tuple-element.30.index_ref, bf16[32,128,256]{2,1,0:T(8,128)(2,1)S(1)} %get-tuple-element.31.flipped_ref, f32[8,32,128]{2,1,0:T(8,128)S(1)} %get-tuple-element.33.low_ref, ...), custom_call_target="tpu_custom_call" | custom-call | flops 67108864 | bytes 2097152 | tf_op jit(solution)/shard_map/direct/pallas_call | solution.py:23
  12.7 0.9 %collective-permute-start.8 = (s16[144,128]{1,0:T(8,128)(2,1)S(1)}, s16[144,128]{1,0:T(8,128)(2,1)S(1)}, u32[]{:S(2)}, u32[]{:S(2)}) collective-permute-start(s16[144,128]{1,0:T(8,128)(2,1)S(1)} %get-tuple-element.41), channel_id=1, source_target_pairs={{0,24},{1,25},{2,26},{3,27},{4,28},{5,29},{6,30},{7,31},{8,16},{9,... | collective-permute-start | bytes 110600 | tf_op jit(solution)/shard_map/ppermute | solution.py:39
  13.9 0.7 %collective-permute-start.6 = (s16[144,128]{1,0:T(8,128)(2,1)S(1)}, s16[144,128]{1,0:T(8,128)(2,1)S(1)}, u32[]{:S(2)}, u32[]{:S(2)}) collective-permute-start(s16[144,128]{1,0:T(8,128)(2,1)S(1)} %get-tuple-element.37), channel_id=1, source_target_pairs={{0,24},{1,25},{2,26},{3,27},{4,28},{5,29},{6,30},{7,31},{8,16},{9,... | collective-permute-start | bytes 110600 | tf_op jit(solution)/shard_map/ppermute | solution.py:39
  14.6 1.8 %collective-permute-done.8.refs_3_ = s16[144,128]{1,0:T(8,128)(2,1)S(1)} collective-permute-done((s16[144,128]{1,0:T(8,128)(2,1)S(1)}, s16[144,128]{1,0:T(8,128)(2,1)S(1)}, u32[]{:S(2)}, u32[]{:S(2)}) %collective-permute-start.8) | collective-permute-done | bytes 36896 | tf_op jit(solution)/shard_map/ppermute | solution.py:39
  16.4 0.9 %collective-permute-done.6.refs_1_ = s16[144,128]{1,0:T(8,128)(2,1)S(1)} collective-permute-done((s16[144,128]{1,0:T(8,128)(2,1)S(1)}, s16[144,128]{1,0:T(8,128)(2,1)S(1)}, u32[]{:S(2)}, u32[]{:S(2)}) %collective-permute-start.6) | collective-permute-done | bytes 36896 | tf_op jit(solution)/shard_map/ppermute | solution.py:39
  17.5 0.4 %collective-permute-start.10 = (s16[144,128]{1,0:T(8,128)(2,1)S(1)}, s16[144,128]{1,0:T(8,128)(2,1)S(1)}, u32[]{:S(2)}, u32[]{:S(2)}) collective-permute-start(s16[144,128]{1,0:T(8,128)(2,1)S(1)} %get-tuple-element.44), channel_id=1, source_target_pairs={{0,9},{1,8},{2,11},{3,10},{4,13},{5,12},{6,15},{7,14},{8,1},{9,0},... | collective-permute-start | bytes 110600 | tf_op jit(solution)/shard_map/ppermute | solution.py:50
  19.2 1.7 %collective-permute-done.10.even_ref = s16[144,128]{1,0:T(8,128)(2,1)S(1)} collective-permute-done((s16[144,128]{1,0:T(8,128)(2,1)S(1)}, s16[144,128]{1,0:T(8,128)(2,1)S(1)}, u32[]{:S(2)}, u32[]{:S(2)}) %collective-permute-start.10) | collective-permute-done | bytes 36896 | tf_op jit(solution)/shard_map/ppermute | solution.py:50
  20.9 1.3 %collective-permute-done.9.odd_ref = s16[144,128]{1,0:T(8,128)(2,1)S(1)} collective-permute-done((s16[144,128]{1,0:T(8,128)(2,1)S(1)}, s16[144,128]{1,0:T(8,128)(2,1)S(1)}, u32[]{:S(2)}, u32[]{:S(2)}) %collective-permute-start.9) | collective-permute-done | bytes 36896 | tf_op jit(solution)/shard_map/ppermute | solution.py:50
  22.7 0.9 %collective-permute-done.11.refs_1_ = bf16[2,2,2,32,128]{4,3,2,1,0:T(8,128)(2,1)S(1)} collective-permute-done((bf16[2,2,2,32,128]{4,3,2,1,0:T(8,128)(2,1)S(1)}, bf16[2,2,2,32,128]{4,3,2,1,0:T(8,128)(2,1)S(1)}, u32[]{:S(2)}, u32[]{:S(2)}) %collective-permute-start.11) | collective-permute-done | bytes 65568 | tf_op jit(solution)/shard_map/ppermute | solution.py:39
  23.6 0.5 %mirror.3 = (f32[2,2,32,128]{3,2,1,0:T(8,128)S(1)}, f32[2,2,32,128]{3,2,1,0:T(8,128)S(1)}, f32[8,32,128]{2,1,0:T(8,128)S(1)}) custom-call(s32[1]{0:T(128)S(6)} %copy.9.live_ref, s32[2,64]{1,0:T(2,128)S(4)} %get-tuple-element.30.index_ref, bf16[32,128,256]{2,1,0:T(8,128)(2,1)S(1)} %get-tuple-element.32.tile_ref, ...), custom_call_target="tpu_custom_call" | custom-call | flops 67108864 | bytes 2097152 | tf_op jit(solution)/shard_map/mirror/pallas_call | solution.py:23
  24.5 0.5 %direct.3 = (f32[2,2,32,128]{3,2,1,0:T(8,128)S(1)}, f32[2,2,32,128]{3,2,1,0:T(8,128)S(1)}) custom-call(s32[1]{0:T(128)S(6)} %copy.9.live_ref, s32[2,64]{1,0:T(2,128)S(4)} %get-tuple-element.30.index_ref, bf16[32,128,256]{2,1,0:T(8,128)(2,1)S(1)} %get-tuple-element.31.flipped_ref, f32[8,32,128]{2,1,0:T(8,128)S(1)} %get-tuple-element.49.low_ref, ...), custom_call_target="tpu_custom_call" | custom-call | flops 67108864 | bytes 2097152 | tf_op jit(solution)/shard_map/direct/pallas_call | solution.py:23
  25.5 1.1 %collective-permute-start.13 = (s16[80,128]{1,0:T(8,128)(2,1)S(1)}, s16[80,128]{1,0:T(8,128)(2,1)S(1)}, u32[]{:S(2)}, u32[]{:S(2)}) collective-permute-start(s16[80,128]{1,0:T(8,128)(2,1)S(1)} %get-tuple-element.48), channel_id=1, source_target_pairs={{0,24},{1,25},{2,26},{3,27},{4,28},{5,29},{6,30},{7,31},{8,16},{9,... | collective-permute-start | bytes 61448 | tf_op jit(solution)/shard_map/ppermute | solution.py:39
  26.7 0.7 %collective-permute-start.16 = (s16[80,128]{1,0:T(8,128)(2,1)S(1)}, s16[80,128]{1,0:T(8,128)(2,1)S(1)}, u32[]{:S(2)}, u32[]{:S(2)}) collective-permute-start(s16[80,128]{1,0:T(8,128)(2,1)S(1)} %get-tuple-element.53), channel_id=1, source_target_pairs={{0,24},{1,25},{2,26},{3,27},{4,28},{5,29},{6,30},{7,31},{8,16},{9,... | collective-permute-start | bytes 61448 | tf_op jit(solution)/shard_map/ppermute | solution.py:39
  27.4 1.4 %collective-permute-done.13.refs_0_ = s16[80,128]{1,0:T(8,128)(2,1)S(1)} collective-permute-done((s16[80,128]{1,0:T(8,128)(2,1)S(1)}, s16[80,128]{1,0:T(8,128)(2,1)S(1)}, u32[]{:S(2)}, u32[]{:S(2)}) %collective-permute-start.13) | collective-permute-done | bytes 20512 | tf_op jit(solution)/shard_map/ppermute | solution.py:39
  28.8 1.4 %collective-permute-start.14 = (s16[80,128]{1,0:T(8,128)(2,1)S(1)}, s16[80,128]{1,0:T(8,128)(2,1)S(1)}, u32[]{:S(2)}, u32[]{:S(2)}) collective-permute-start(s16[80,128]{1,0:T(8,128)(2,1)S(1)} %owner.1), channel_id=1, source_target_pairs={{0,9},{1,10},{2,11},{3,12},{4,13},{5,14},{6,15},{7,8},{8,1},{9,2},... | collective-permute-start | bytes 61448 | tf_op jit(solution)/shard_map/ppermute | solution.py:56
  30.2 2.7 %collective-permute-done.14.arrived_ref = s16[80,128]{1,0:T(8,128)(2,1)S(1)} collective-permute-done((s16[80,128]{1,0:T(8,128)(2,1)S(1)}, s16[80,128]{1,0:T(8,128)(2,1)S(1)}, u32[]{:S(2)}, u32[]{:S(2)}) %collective-permute-start.14) | collective-permute-done | bytes 20512 | tf_op jit(solution)/shard_map/ppermute | solution.py:56
  33.0 0.6 %second.1 = (f32[32,256]{1,0:T(8,128)}, bf16[32,256]{1,0:T(8,128)(2,1)}) custom-call(f32[1]{0:T(128)S(6)} %copy.10.center_ref, f32[1]{0:T(128)S(6)} %copy.11.radius_ref, bf16[4,2,32,128]{3,2,1,0:T(8,128)(2,1)S(1)} %stack.1.refs_0_.own_ref, bf16[2,2,2,32,128]{4,3,2,1,0:T(8,128)(2,1)S(1)} %first.1.refs_0_.first_ref, ...), custom_call_target="tpu_custom_call" | custom-call | tf_op jit(solution)/shard_map/second/pallas_call | solution.py:23
  (24 shorter events, 2.5 us)
Async XLA Ops:
  0.6 4.5 %collective-permute-start = (bf16[32,256]{1,0:T(8,128)(2,1)}, bf16[32,256]{1,0:T(8,128)(2,1)S(1)}, u32[]{:S(2)}, u32[]{:S(2)}) collective-permute-start(bf16[32,256]{1,0:T(8,128)(2,1)} %vectors_hbm.1), channel_id=1, source_target_pairs={{0,24},{1,25},{2,26},{3,27},{4,28},{5,29},{6,30},{7,31},{8,16},{9,... | collective-permute-start | bytes 49160 | tf_op jit(solution)/shard_map/ppermute | solution.py:39
  2.5 2.8 %collective-permute-start.1 = (bf16[32,256]{1,0:T(8,128)(2,1)}, bf16[32,256]{1,0:T(8,128)(2,1)S(1)}, u32[]{:S(2)}, u32[]{:S(2)}) collective-permute-start(bf16[32,256]{1,0:T(8,128)(2,1)} %vectors_hbm.1), channel_id=1, source_target_pairs={{0,16},{1,17},{2,18},{3,19},{4,20},{5,21},{6,22},{7,23},{8,24},{9,... | collective-permute-start | bytes 49160 | tf_op jit(solution)/shard_map/ppermute | solution.py:39
  2.7 2.6 %collective-permute-start.2 = (bf16[32,256]{1,0:T(8,128)(2,1)}, bf16[32,256]{1,0:T(8,128)(2,1)S(1)}, u32[]{:S(2)}, u32[]{:S(2)}) collective-permute-start(bf16[32,256]{1,0:T(8,128)(2,1)} %vectors_hbm.1), channel_id=1, source_target_pairs={{0,8},{1,9},{2,10},{3,11},{4,12},{5,13},{6,14},{7,15},{8,0},{9,1},... | collective-permute-start | bytes 49160 | tf_op jit(solution)/shard_map/ppermute | solution.py:39
  5.3 5.0 %collective-permute-start.3 = (bf16[4,2,32,128]{3,2,1,0:T(8,128)(2,1)S(1)}, bf16[4,2,32,128]{3,2,1,0:T(8,128)(2,1)S(1)}, u32[]{:S(2)}, u32[]{:S(2)}) collective-permute-start(bf16[4,2,32,128]{3,2,1,0:T(8,128)(2,1)S(1)} %stack.1.refs_0_.own_ref), channel_id=1, source_target_pairs={{0,9},{1,8},{2,11},{3,10},{4,13},{5,12},{6,15},{7,14},{8,1},{9,0},... | collective-permute-start | bytes 196616 | tf_op jit(solution)/shard_map/ppermute | solution.py:50
  7.5 4.6 %collective-permute-start.4 = (bf16[4,2,32,128]{3,2,1,0:T(8,128)(2,1)S(1)}, bf16[4,2,32,128]{3,2,1,0:T(8,128)(2,1)S(1)}, u32[]{:S(2)}, u32[]{:S(2)}) collective-permute-start(bf16[4,2,32,128]{3,2,1,0:T(8,128)(2,1)S(1)} %stack.1.refs_0_.own_ref), channel_id=1, source_target_pairs={{0,8},{1,10},{2,9},{3,12},{4,11},{5,14},{6,13},{7,15},{8,0},{9,2},... | collective-permute-start | bytes 196616 | tf_op jit(solution)/shard_map/ppermute | solution.py:50
  8.6 4.0 %collective-permute-start.7 = (f32[2,2,32,128]{3,2,1,0:T(8,128)S(1)}, f32[2,2,32,128]{3,2,1,0:T(8,128)S(1)}, u32[]{:S(2)}, u32[]{:S(2)}) collective-permute-start(f32[2,2,32,128]{3,2,1,0:T(8,128)S(1)} %get-tuple-element.39), channel_id=1, source_target_pairs={{0,8},{1,9},{2,10},{3,11},{4,12},{5,13},{6,14},{7,15},{8,0},{9,1},... | collective-permute-start | bytes 196616 | tf_op jit(solution)/shard_map/ppermute | solution.py:39
  12.6 1.3 %collective-permute-start.5 = (f32[2,2,32,128]{3,2,1,0:T(8,128)S(1)}, f32[2,2,32,128]{3,2,1,0:T(8,128)S(1)}, u32[]{:S(2)}, u32[]{:S(2)}) collective-permute-start(f32[2,2,32,128]{3,2,1,0:T(8,128)S(1)} %get-tuple-element.35), channel_id=1, source_target_pairs={{0,8},{1,9},{2,10},{3,11},{4,12},{5,13},{6,14},{7,15},{8,0},{9,1},... | collective-permute-start | bytes 196616 | tf_op jit(solution)/shard_map/ppermute | solution.py:39
  12.7 3.7 %collective-permute-start.8 = (s16[144,128]{1,0:T(8,128)(2,1)S(1)}, s16[144,128]{1,0:T(8,128)(2,1)S(1)}, u32[]{:S(2)}, u32[]{:S(2)}) collective-permute-start(s16[144,128]{1,0:T(8,128)(2,1)S(1)} %get-tuple-element.41), channel_id=1, source_target_pairs={{0,24},{1,25},{2,26},{3,27},{4,28},{5,29},{6,30},{7,31},{8,16},{9,... | collective-permute-start | bytes 110600 | tf_op jit(solution)/shard_map/ppermute | solution.py:39
  13.9 3.4 %collective-permute-start.6 = (s16[144,128]{1,0:T(8,128)(2,1)S(1)}, s16[144,128]{1,0:T(8,128)(2,1)S(1)}, u32[]{:S(2)}, u32[]{:S(2)}) collective-permute-start(s16[144,128]{1,0:T(8,128)(2,1)S(1)} %get-tuple-element.37), channel_id=1, source_target_pairs={{0,24},{1,25},{2,26},{3,27},{4,28},{5,29},{6,30},{7,31},{8,16},{9,... | collective-permute-start | bytes 110600 | tf_op jit(solution)/shard_map/ppermute | solution.py:39
  17.5 3.4 %collective-permute-start.10 = (s16[144,128]{1,0:T(8,128)(2,1)S(1)}, s16[144,128]{1,0:T(8,128)(2,1)S(1)}, u32[]{:S(2)}, u32[]{:S(2)}) collective-permute-start(s16[144,128]{1,0:T(8,128)(2,1)S(1)} %get-tuple-element.44), channel_id=1, source_target_pairs={{0,9},{1,8},{2,11},{3,10},{4,13},{5,12},{6,15},{7,14},{8,1},{9,0},... | collective-permute-start | bytes 110600 | tf_op jit(solution)/shard_map/ppermute | solution.py:50
  17.9 4.3 %collective-permute-start.9 = (s16[144,128]{1,0:T(8,128)(2,1)S(1)}, s16[144,128]{1,0:T(8,128)(2,1)S(1)}, u32[]{:S(2)}, u32[]{:S(2)}) collective-permute-start(s16[144,128]{1,0:T(8,128)(2,1)S(1)} %get-tuple-element.43), channel_id=1, source_target_pairs={{0,8},{1,10},{2,9},{3,12},{4,11},{5,14},{6,13},{7,15},{8,0},{9,2},... | collective-permute-start | bytes 110600 | tf_op jit(solution)/shard_map/ppermute | solution.py:50
  22.3 1.3 %collective-permute-start.11 = (bf16[2,2,2,32,128]{4,3,2,1,0:T(8,128)(2,1)S(1)}, bf16[2,2,2,32,128]{4,3,2,1,0:T(8,128)(2,1)S(1)}, u32[]{:S(2)}, u32[]{:S(2)}) collective-permute-start(bf16[2,2,2,32,128]{4,3,2,1,0:T(8,128)(2,1)S(1)} %first.1.refs_0_.first_ref), channel_id=1, source_target_pairs={{0,8},{1,9},{2,10},{3,11},{4,12},{5,13},{6,14},{7,15},{8,0},{9,1},... | collective-permute-start | bytes 196616 | tf_op jit(solution)/shard_map/ppermute | solution.py:39
  24.1 1.3 %collective-permute-start.12 = (f32[2,2,32,128]{3,2,1,0:T(8,128)S(1)}, f32[2,2,32,128]{3,2,1,0:T(8,128)S(1)}, u32[]{:S(2)}, u32[]{:S(2)}) collective-permute-start(f32[2,2,32,128]{3,2,1,0:T(8,128)S(1)} %get-tuple-element.46), channel_id=1, source_target_pairs={{0,8},{1,9},{2,10},{3,11},{4,12},{5,13},{6,14},{7,15},{8,0},{9,1},... | collective-permute-start | bytes 196616 | tf_op jit(solution)/shard_map/ppermute | solution.py:39
  25.1 1.6 %collective-permute-start.15 = (f32[2,2,32,128]{3,2,1,0:T(8,128)S(1)}, f32[2,2,32,128]{3,2,1,0:T(8,128)S(1)}, u32[]{:S(2)}, u32[]{:S(2)}) collective-permute-start(f32[2,2,32,128]{3,2,1,0:T(8,128)S(1)} %get-tuple-element.51), channel_id=1, source_target_pairs={{0,8},{1,9},{2,10},{3,11},{4,12},{5,13},{6,14},{7,15},{8,0},{9,1},... | collective-permute-start | bytes 196616 | tf_op jit(solution)/shard_map/ppermute | solution.py:39
  25.5 3.3 %collective-permute-start.13 = (s16[80,128]{1,0:T(8,128)(2,1)S(1)}, s16[80,128]{1,0:T(8,128)(2,1)S(1)}, u32[]{:S(2)}, u32[]{:S(2)}) collective-permute-start(s16[80,128]{1,0:T(8,128)(2,1)S(1)} %get-tuple-element.48), channel_id=1, source_target_pairs={{0,24},{1,25},{2,26},{3,27},{4,28},{5,29},{6,30},{7,31},{8,16},{9,... | collective-permute-start | bytes 61448 | tf_op jit(solution)/shard_map/ppermute | solution.py:39
  26.7 3.6 %collective-permute-start.16 = (s16[80,128]{1,0:T(8,128)(2,1)S(1)}, s16[80,128]{1,0:T(8,128)(2,1)S(1)}, u32[]{:S(2)}, u32[]{:S(2)}) collective-permute-start(s16[80,128]{1,0:T(8,128)(2,1)S(1)} %get-tuple-element.53), channel_id=1, source_target_pairs={{0,24},{1,25},{2,26},{3,27},{4,28},{5,29},{6,30},{7,31},{8,16},{9,... | collective-permute-start | bytes 61448 | tf_op jit(solution)/shard_map/ppermute | solution.py:39
  28.8 4.2 %collective-permute-start.14 = (s16[80,128]{1,0:T(8,128)(2,1)S(1)}, s16[80,128]{1,0:T(8,128)(2,1)S(1)}, u32[]{:S(2)}, u32[]{:S(2)}) collective-permute-start(s16[80,128]{1,0:T(8,128)(2,1)S(1)} %owner.1), channel_id=1, source_target_pairs={{0,9},{1,10},{2,11},{3,12},{4,13},{5,14},{6,15},{7,8},{8,1},{9,2},... | collective-permute-start | bytes 61448 | tf_op jit(solution)/shard_map/ppermute | solution.py:56
